TPU v7x, 32 devices: a whole 2x2x4 slice. The times are simulated.
32 devices in a mesh: req: 4 (over z), exp: 8 (over y, x, core).
Axes of the slice: x: 2, y: 2, z: 4, core: 2. Of those that a mesh axis runs over, the one named last changes fastest.
Arguments:
- queries: bfloat16 [32, 64, 2048], P(('req', 'exp'))
- new_kv: bfloat16 [32, 64, 2, 2048], P(('req', 'exp')), may hold values from -6 to 6
- cache: bfloat16 [32, 512, 2, 2048], P(('req', 'exp'))
- lengths: int32 [32], P(('req', 'exp')), may hold values from 8 to 448
- residual: bfloat16 [32, 64, 2048], P(('req', 'exp')), may hold values from -6 to 6
- out_weight: bfloat16 [2048, 2048], replicated, may hold values from -0.125 to 0.125
- norm_gain: float32 [2048], replicated, may hold values from 0.1 to 1.9
- expert_ids: int32 [32, 64, 8], P(('req', 'exp')), may hold values from 0 to 15, all different within a row; in each aligned block of 64 rows (0 to 63, 64 to 127, ..., all dimensions but the last counted through in order) at most 40 rows name the same one
- gates: float32 [32, 64, 8], P(('req', 'exp')), may hold values from 0.1 to 1
- w_gate: bfloat16 [32, 2048, 512], P(('req', 'exp')), may hold values from -0.125 to 0.125
- w_up: bfloat16 [32, 2048, 512], P(('req', 'exp')), may hold values from -0.125 to 0.125
- w_down: bfloat16 [32, 512, 2048], P(('req', 'exp')), may hold values from -0.1875 to 0.1875
Outputs:
- layer_out: bfloat16 [32, 64, 2048], P(('req', 'exp'))
- appended: bfloat16 [32, 512, 2, 2048], P(('req', 'exp'))
Inputs may be any that keep to these rules, and one draw needn't show every extreme that they name: `expert_ids`: among the tokens of one request, no expert is named by more than 40 rows.
All inputs are finite; a program needn't handle non-finite values.
Results may differ from a plain program's by a relative error of at most 0.0095.
Values may be sent and summed in bfloat16 or wider, within the bound.
No kernel may reach another device: no remote copies, remote signals or barrier semaphores. Data moves between devices by JAX's collectives and lax.ppermute only.
A program may use at most 128 MiB of HBM per device.

v0:
```python
import jax
import jax.numpy as jnp
from jax import lax
from jax.sharding import PartitionSpec as P

HEADS = 16
HEAD_DIM = 128


masked_value = -1e30


def expert_rows(piece, gate_half, up_half, down_half):
    leading, counted, features = piece.shape
    flat_rows = piece.reshape(leading * counted, features)
    gate_act = jnp.dot(flat_rows, gate_half, preferred_element_type=jnp.float32)
    upward = jnp.dot(flat_rows, up_half, preferred_element_type=jnp.float32)
    hidden = (jax.nn.silu(gate_act) * upward).astype(jnp.bfloat16)
    partial_sum = jnp.dot(hidden, down_half, preferred_element_type=jnp.float32)
    return partial_sum.reshape(leading, counted, partial_sum.shape[-1])


def shards(
    queries,
    new_kv,
    cache,
    lengths,
    residual,
    out_weight,
    norm_gain,
    expert_ids,
    gates,
    w_gate,
    w_up,
    w_down,
):
    gate_half = w_gate[0]
    up_half = w_up[0]
    down_half = w_down[0]
    query_rows = queries[0]
    new_rows = new_kv[0]
    cache_rows = cache[0]
    length_now = lengths[0]
    group_len = query_rows.shape[0]
    features = query_rows.shape[1]
    key_rows = jnp.concatenate([cache_rows[:, 0], new_rows[:, 0]], axis=0)
    value_rows = jnp.concatenate([cache_rows[:, 1], new_rows[:, 1]], axis=0)
    positions = key_rows.shape[0]
    queried = query_rows.reshape(group_len, HEADS, HEAD_DIM)
    keyed = key_rows.reshape(positions, HEADS, HEAD_DIM)
    valued = value_rows.reshape(positions, HEADS, HEAD_DIM)
    scores = jnp.einsum(
        "qhd,khd->hqk", queried, keyed, preferred_element_type=jnp.float32
    ) * HEAD_DIM ** (-0.5)
    slot_place = jnp.arange(positions, dtype=jnp.int32)
    counted = (slot_place < length_now) | (slot_place >= cache_rows.shape[0])
    scores = jnp.where(counted[None, None, :], scores, masked_value)
    peak_score = jnp.max(scores, axis=-1, keepdims=True)
    raised = jnp.exp(scores - peak_score)
    softmax_bf = (raised / jnp.sum(raised, axis=-1, keepdims=True)).astype(jnp.bfloat16)
    mixed_heads = jnp.einsum("hqk,khd->qhd", softmax_bf, valued, preferred_element_type=jnp.float32)
    attention = mixed_heads.reshape(group_len, features).astype(jnp.bfloat16)
    stream = residual[0].astype(jnp.float32) + jnp.dot(
        attention, out_weight, preferred_element_type=jnp.float32
    )
    appended = lax.dynamic_update_slice(
        cache_rows, new_rows, (length_now, jnp.int32(0), jnp.int32(0))
    )[None]
    mean_square = jnp.mean(stream * stream, axis=-1, keepdims=True)
    normed = (stream * lax.rsqrt(mean_square + 1e-06) * norm_gain).astype(jnp.bfloat16)
    devices_all = lax.axis_size(("req", "exp"))
    experts_all = devices_all // 2
    top_k = expert_ids.shape[2]
    capacity = 5 * group_len * top_k // (4 * experts_all)
    routed = expert_ids[0].reshape(-1)
    one_hot = (routed[:, None] == jnp.arange(experts_all, dtype=jnp.int32)[None, :]).astype(
        jnp.int32
    )
    ranking = jnp.sum((jnp.cumsum(one_hot, axis=0) - one_hot) * one_hot, axis=1)
    position = routed * capacity + ranking
    row_token = jnp.arange(group_len * top_k, dtype=jnp.int32) // top_k
    token_of = jnp.full((experts_all * capacity,), group_len, jnp.int32).at[position].set(row_token)
    padded = jnp.concatenate([normed, jnp.zeros((1, features), jnp.bfloat16)], axis=0)
    outgoing = padded[token_of].reshape(experts_all, capacity, features)
    doubled = jnp.broadcast_to(outgoing[:, None], (experts_all, 2, capacity, features)).reshape(
        devices_all, capacity, features
    )
    partials = expert_rows(
        lax.all_to_all(doubled, ("req", "exp"), split_axis=0, concat_axis=0, tiled=True),
        gate_half,
        up_half,
        down_half,
    )
    returned = lax.all_to_all(
        partials.astype(jnp.bfloat16), ("req", "exp"), split_axis=0, concat_axis=0, tiled=True
    ).astype(partials.dtype)
    expert_out = jnp.sum(returned.reshape(experts_all, 2, capacity, features), axis=1).astype(
        jnp.bfloat16
    )
    picked = expert_out.reshape(experts_all * capacity, features)[position].reshape(
        group_len, top_k, features
    )
    blended = jnp.sum(gates[0][:, :, None] * picked.astype(jnp.float32), axis=1)
    layer_out = (stream + blended).astype(jnp.bfloat16)[None]
    return (layer_out, appended)


def solution(mesh):
    placed = (
        P(("req", "exp"), None, None),
        P(("req", "exp"), None, None, None),
        P(("req", "exp"), None, None, None),
        P(("req", "exp")),
        P(("req", "exp"), None, None),
        P(),
        P(),
        P(("req", "exp"), None, None),
        P(("req", "exp"), None, None),
        P(("req", "exp"), None, None),
        P(("req", "exp"), None, None),
        P(("req", "exp"), None, None),
    )
    return jax.shard_map(
        shards,
        mesh=mesh,
        in_specs=placed,
        out_specs=(P(("req", "exp"), None, None), P(("req", "exp"), None, None, None)),
        check_vma=False,
    )
```

profile of v0, /device:TPU:0, one launch (start us, length us, event | category | flops | bytes accessed | tf_op | source)
XLA Modules:
  0.0 327.5 jit_solution(11903131148949002137)
XLA Ops:
  0.7 7.2 %copy.47 = bf16[1,512,2,2048]{3,2,1,0:T(2,128)(2,1)} copy(bf16[1,512,2,2048]{3,2,1,0:T(2,128)(2,1)} %param.14) | data formatting | bytes 8388608
  8.2 11.1 %copy.16 = bf16[1,512,2,2048]{1,3,2,0:T(8,128)(2,1)} copy(bf16[1,512,2,2048]{3,2,1,0:T(2,128)(2,1)} %copy.47) | data formatting | bytes 8388608 | tf_op args[2]
  19.3 4.5 %fusion.46 = (bf16[512,1,2048]{0,2,1:T(8,128)(2,1)}, bf16[512,1,2048]{0,2,1:T(8,128)(2,1)}) fusion(bf16[512,2,2048]{0,2,1:T(8,128)(2,1)} %bitcast.96), kind=kLoop, calls=%fused_computation.77 | loop fusion | bytes 8388608 | tf_op jit(solution)/shard_map/slice | solution.py:46
  23.8 4.0 %copy.19 = bf16[512,16,128]{2,0,1:T(8,128)(2,1)} copy(bf16[512,16,128]{0,2,1:T(8,128)(2,1)} %bitcast.99) | data formatting | bytes 4194304 | tf_op jit(solution)/shard_map/concatenate | solution.py:46
  27.8 2.3 slice_reduce_fusion.1
  30.1 1.0 copy.32
  31.8 3.9 %copy.17 = bf16[512,16,128]{2,0,1:T(8,128)(2,1)} copy(bf16[512,16,128]{0,2,1:T(8,128)(2,1)} %bitcast.98) | data formatting | bytes 4194304 | tf_op jit(solution)/shard_map/concatenate | solution.py:47
  35.8 2.7 fusion.5
  38.5 0.9 fusion.47
  39.5 0.6 fusion.25
  40.1 0.6 slice-done
  40.6 1.6 slice-done.1
  42.2 1.7 multiply_reduce_fusion
  43.9 1.2 reduce-window.6
  45.1 0.2 slice_reduce_fusion.2
  45.4 0.1 mul.73
  45.5 0.1 fusion.34
  45.6 2.6 scatter_custom_fusion
  48.3 0.1 multiply_convert_fusion
  48.5 4.1 %gather_fusion = bf16[640,2048]{1,0:T(8,128)(2,1)} fusion(bf16[65,2048]{1,0:T(8,128)(2,1)S(1)} %concatenate.25, s32[1024]{0:T(1024)S(1)} %pad_clamp_fusion.1), kind=kCustom, calls=%fused_computation | custom fusion | bytes 5245440 | tf_op jit(solution)/shard_map/gather | solution.py:84
  52.5 2.4 broadcast_in_dim.43
  55.0 123.2 %all_to_all.10 = bf16[32,40,2048]{2,1,0:T(8,128)(2,1)S(1)} all-to-all(bf16[32,40,2048]{2,1,0:T(8,128)(2,1)S(1)} %bitcast.95), channel_id=1, replica_groups=mesh['req'=4,'exp'=8] {'req','exp'}, dimensions={0} | all-to-all | bytes 10485760 | tf_op jit(solution)/shard_map/all_to_all | solution.py:89
  178.2 2.9 fusion.15
  181.1 3.3 %fusion.2 = bf16[1280,512]{1,0:T(8,128)(2,1)S(1)} fusion(bf16[1280,2048]{1,0:T(8,128)(2,1)S(1)} %bitcast.101, f32[1280,512]{1,0:T(8,128)S(1)} %fusion.15, bf16[1,2048,512]{2,1,0:T(8,128)(2,1)S(1)} %copy-done.8), kind=kOutput, calls=%fused_computation.9 | convolution fusion | flops 2688286720 | bytes 11272192 | tf_op jit(solution)/shard_map/dot_general | solution.py:17
  184.5 4.7 %convolution_convert_fusion = bf16[32,40,2048]{2,1,0:T(8,128)(2,1)} fusion(bf16[32,40,512]{2,1,0:T(8,128)(2,1)S(1)} %bitcast.109, bf16[1,512,2048]{2,1,0:T(8,128)(2,1)S(1)} %copy-done), kind=kOutput, calls=%fused_computation.7 | convolution fusion | flops 2686976000 | bytes 8650752 | tf_op jit(solution)/shard_map/dot_general | solution.py:19
  189.2 4.1 %all-to-all-start.1 = ((bf16[32,40,2048]{2,1,0:T(8,128)(2,1)}), bf16[32,40,2048]{2,1,0:T(8,128)(2,1)}, u32[]{:S(2)}, u32[]{:S(2)}) async-start(bf16[32,40,2048]{2,1,0:T(8,128)(2,1)} %convolution_convert_fusion), calls=%async_computation.1 | async-start | bytes 10485760 | tf_op jit(solution)/shard_map/all_to_all | solution.py:94
  193.4 1.2 constant_dynamic-update-slice_fusion
  194.5 115.3 %all-to-all-done.1 = bf16[32,40,2048]{2,1,0:T(8,128)(2,1)} async-done(((bf16[32,40,2048]{2,1,0:T(8,128)(2,1)}), bf16[32,40,2048]{2,1,0:T(8,128)(2,1)}, u32[]{:S(2)}, u32[]{:S(2)}) %all-to-all-start.1) | async-done | bytes 5242912 | tf_op jit(solution)/shard_map/all_to_all | solution.py:94
  309.9 6.0 %bitcast_reduce_fusion = bf16[16,40,2048]{2,1,0:T(8,128)(2,1)} fusion(bf16[32,40,2048]{2,1,0:T(8,128)(2,1)} %all-to-all-done.1), kind=kLoop, calls=%fused_computation.4 | loop fusion | flops 1310720 | bytes 7864320 | tf_op jit(solution)/shard_map/reduce_sum | solution.py:97
  315.9 7.4 %gather_fusion.1 = bf16[512,2048]{1,0:T(8,128)(2,1)} fusion(bf16[640,2048]{1,0:T(8,128)(2,1)} %bitcast.92, s32[1024]{0:T(1024)S(1)} %pad_clamp_fusion), kind=kCustom, calls=%fused_computation.1 | custom fusion | bytes 4196352 | tf_op jit(solution)/shard_map/gather | solution.py:100
  323.2 3.4 %fusion.1 = f32[64,2048]{1,0:T(8,128)S(1)} fusion(bf16[512,2048]{1,0:T(8,128)(2,1)} %gather_fusion.1, f32[64,8]{1,0:T(8,128)S(1)} %copy.23), kind=kLoop, calls=%fused_computation.6 | loop fusion | flops 3014656 | bytes 2623488 | tf_op jit(solution)/shard_map/reduce_sum | solution.py:103
  326.7 0.8 fusion.28
  (40 shorter events, 0.7 us)
Async XLA Ops:
  0.6 183.8 %copy-start = (bf16[1,512,2048]{2,1,0:T(8,128)(2,1)S(1)}, bf16[1,512,2048]{2,1,0:T(8,128)(2,1)}, u32[]{:S(2)}) copy-start(bf16[1,512,2048]{2,1,0:T(8,128)(2,1)} %param.23) | copy-start | bytes 6291460
  0.6 7.2 %copy-start.4 = (s32[1,64,8]{1,2,0:T(8,128)S(1)}, s32[1,64,8]{1,2,0:T(8,128)}, u32[]{:S(2)}) copy-start(s32[1,64,8]{1,2,0:T(8,128)} %param.19) | copy-start | bytes 6148
  23.8 4.0 %copy-start.1 = (bf16[1,64,2,2048]{3,2,1,0:T(2,128)(2,1)S(1)}, bf16[1,64,2,2048]{3,2,1,0:T(2,128)(2,1)}, u32[]{:S(2)}) copy-start(bf16[1,64,2,2048]{3,2,1,0:T(2,128)(2,1)} %param.13) | copy-start | bytes 1572868
  35.8 3.7 %copy-start.2 = (bf16[512,16,128]{2,0,1:T(8,128)(2,1)S(1)}, bf16[512,16,128]{2,0,1:T(8,128)(2,1)}, u32[]{:S(2)}) copy-start(bf16[512,16,128]{2,0,1:T(8,128)(2,1)} %copy.17) | copy-start | bytes 6291460
  38.4 2.2 slice-start
  39.4 2.8 slice-start.1
  39.4 2.8 copy-start.3
  42.2 6.1 %copy-start.5 = (f32[2048]{0:T(1024)S(1)}, f32[2048]{0:T(1024)}, u32[]{:S(2)}) copy-start(f32[2048]{0:T(1024)} %param.18) | copy-start | bytes 24580
  54.9 123.2 %copy-start.7 = (bf16[1,2048,512]{2,1,0:T(8,128)(2,1)S(1)}, bf16[1,2048,512]{2,1,0:T(8,128)(2,1)}, u32[]{:S(2)}) copy-start(bf16[1,2048,512]{2,1,0:T(8,128)(2,1)} %param.21) | copy-start | bytes 6291460
  178.2 2.9 copy-start.8
  189.2 4.1 %copy-start.6 = (f32[1,64,8]{1,2,0:T(8,128)S(1)}, f32[1,64,8]{1,2,0:T(8,128)}, u32[]{:S(2)}) copy-start(f32[1,64,8]{1,2,0:T(8,128)} %param.20) | copy-start | bytes 6148
  189.2 120.7 %all-to-all-start.1 = ((bf16[32,40,2048]{2,1,0:T(8,128)(2,1)}), bf16[32,40,2048]{2,1,0:T(8,128)(2,1)}, u32[]{:S(2)}, u32[]{:S(2)}) async-start(bf16[32,40,2048]{2,1,0:T(8,128)(2,1)} %convolution_convert_fusion), calls=%async_computation.1 | async-start | bytes 10485760 | tf_op jit(solution)/shard_map/all_to_all | solution.py:94
where the time goes:
time: 328 us; the launch traced here: 327 us
  blocking collectives  123 us (38%)
  waiting for transfers between devices  115 us (35%)
  local copies, waits for them, and re-layouts  54.7 us (17%)
  matrix products  15.9 us (5%)
  other arithmetic  12.6 us (4%)
  starting transfers between devices  4.09 us (1%)
    all_to_all x1, blocking collectives, shards(): lax.all_to_all(doubled, ('req', 'exp'), split_axis=0, concat_axis=0, tile...  123 us
    all_to_all x1, waiting for transfers between devices, shards(): lax.all_to_all(partials.astype(jnp.bfloat16), ('req', 'exp'), split_axis=...  115 us
    unnamed x26, local copies, waits for them, and re-layouts  21.6 us
    gather x1, local copies, waits for them, and re-layouts, shards(): expert_out.reshape(experts_all * capacity, features)[position]  7.36 us
    slice x2, local copies, waits for them, and re-layouts, shards(): key_rows = jnp.concatenate([cache_rows[:, 0], new_rows[:, 0]], axis=0)  6.73 us
  transfers between devices with their start and end apart: 1, of which 1 were waited for; matrix products, arithmetic and copies ran while one was open for 0% of the time, Pallas kernels for 0%

commit v1 on v0

v1 whole, which is shorter than its diff:
```python
import functools

import jax
import jax.numpy as jnp
from jax import lax
from jax.experimental import pallas as pl
from jax.experimental.pallas import tpu as pltpu
from jax.sharding import Mesh, PartitionSpec as P

HEADS = 16
HEAD_DIM = 128
masked_value = -1e30
ALL = ("req", "chip", "core")
VMEM = pltpu.VMEM


def dot(a, b):
    return jnp.dot(a, b, preferred_element_type=jnp.float32)


def slot_weights(weights, base, mine, chips, capacity):
    tokens, experts = weights.shape
    routed = weights > 0.0
    earlier = lax.broadcasted_iota(jnp.int32, (tokens, tokens), 0) > lax.broadcasted_iota(
        jnp.int32, (tokens, tokens), 1
    )
    ranks = dot(earlier.astype(jnp.bfloat16), routed.astype(jnp.bfloat16))
    ranks = jnp.where(routed, ranks, -1.0)
    expert_at = lax.broadcasted_iota(jnp.int32, (tokens, experts), 1)
    column = lax.broadcasted_iota(jnp.int32, (tokens, chips * capacity), 1)
    gate_at = jnp.zeros((tokens, chips * capacity), jnp.float32)
    hit = jnp.zeros((tokens, chips * capacity), jnp.float32)
    for j in range(chips):
        chosen = expert_at == base + jnp.bitwise_xor(mine, j)
        gate_j = jnp.sum(jnp.where(chosen, weights, 0.0), axis=1, keepdims=True)
        rank_j = jnp.sum(jnp.where(chosen, ranks, 0.0), axis=1, keepdims=True).astype(jnp.int32)
        here = (column == rank_j + j * capacity) & (rank_j >= 0)
        gate_at = jnp.where(here, gate_j, gate_at)
        hit = jnp.where(here, 1.0, hit)
    return gate_at, hit


def gather_rows(rows, weights, base, mine, chips, capacity, outs):
    _, hit = slot_weights(weights, base, mine, chips, capacity)
    picked = lax.dot_general(
        hit.astype(jnp.bfloat16), rows, (((0,), (0,)), ((), ())), preferred_element_type=jnp.float32
    )
    scatter_out(picked, capacity, outs)


def scatter_out(rows, capacity, outs):
    if len(outs) == 1:
        outs[0][...] = rows.astype(outs[0].dtype)
    else:
        for j, out in enumerate(outs):
            out[...] = rows[j * capacity : (j + 1) * capacity].astype(out.dtype)


def stacked(refs):
    if len(refs) == 1:
        return refs[0][...]
    return jnp.concatenate([ref[...].astype(jnp.float32) for ref in refs], axis=0).astype(jnp.bfloat16)


def combined(refs, weights, base, mine, chips, capacity):
    gate_at, _ = slot_weights(weights, base, mine, chips, capacity)
    high = gate_at.astype(jnp.bfloat16)
    low = (gate_at - high.astype(jnp.float32)).astype(jnp.bfloat16)
    tokens = gate_at.shape[0]
    both = dot(jnp.concatenate([high, low], axis=0), stacked(refs))
    return both[:tokens] + both[tokens:]


def attention_kernel(
    chips, capacity, place, length, queries, new_kv, cache, residual, out_weight, gain, weights,
    stream, normed, appended, *rest,
):
    outs, scratch = rest[:-9], rest[-9:]
    cached, newest, queried, resid, projection, keys, values, mixed, sems = scratch
    slots = cache.shape[0]
    group = new_kv.shape[0]
    pieces = 4
    part = slots // pieces
    loads = [
        pltpu.make_async_copy(
            cache.at[pl.ds(i * part, part)], cached.at[pl.ds(i * part, part)], sems.at[i]
        )
        for i in range(pieces)
    ]
    load_new = pltpu.make_async_copy(new_kv, newest, sems.at[pieces])
    load_queries = pltpu.make_async_copy(queries, queried, sems.at[pieces + 1])
    load_resid = pltpu.make_async_copy(residual, resid, sems.at[pieces + 2])
    load_projection = pltpu.make_async_copy(out_weight, projection, sems.at[pieces + 3])
    load_new.start()
    for load in loads:
        load.start()
    load_queries.start()
    load_resid.start()
    load_projection.start()

    def split(source, first, target):
        planes = jnp.swapaxes(source[pl.ds(first, 16)], 0, 1)
        keys[pl.ds(target, 16), :] = planes[0]
        values[pl.ds(target, 16), :] = planes[1]

    load_new.wait()
    for i in range(group // 16):
        split(newest, i * 16, slots + i * 16)
    for i in range(pieces):
        loads[i].wait()

        def step(k, carry):
            first = pl.multiple_of(i * part + k * 16, 16)
            split(cached, first, first)
            return carry

        lax.fori_loop(0, part // 16, step, 0)
    store_cache = pltpu.make_async_copy(cached, appended, sems.at[pieces + 4])
    store_cache.start()
    load_queries.wait()
    positions = slots + group
    slot_place = lax.broadcasted_iota(jnp.int32, (1, positions), 1)
    counted = (slot_place < length[0]) | (slot_place >= slots)
    for h in range(HEADS):
        head = slice(h * HEAD_DIM, (h + 1) * HEAD_DIM)
        scores = lax.dot_general(
            queried[:, head], keys[:, head], (((1,), (1,)), ((), ())), preferred_element_type=jnp.float32
        ) * HEAD_DIM ** (-0.5)
        scores = jnp.where(counted, scores, masked_value)
        raised = jnp.exp(scores - jnp.max(scores, axis=-1, keepdims=True))
        softmax_bf = (raised / jnp.sum(raised, axis=-1, keepdims=True)).astype(jnp.bfloat16)
        mixed[:, head] = dot(softmax_bf, values[:, head]).astype(jnp.bfloat16)
    store_cache.wait()
    store_new = pltpu.make_async_copy(newest, appended.at[pl.ds(length[0], group)], sems.at[pieces + 4])
    store_new.start()
    load_resid.wait()
    load_projection.wait()
    total = resid[...].astype(jnp.float32) + dot(mixed[...], projection[...])
    stream[...] = total
    mean_square = jnp.mean(total * total, axis=-1, keepdims=True)
    rows = (total * lax.rsqrt(mean_square + 1e-06) * gain[...]).astype(jnp.bfloat16)
    normed[...] = rows
    gather_rows(rows, weights[...], place[0], place[1], chips, capacity, outs)
    store_new.wait()


def gather_kernel(chips, capacity, place, rows, weights, *outs):
    gather_rows(rows[...], weights[...], place[0], place[1], chips, capacity, outs)


def expert_kernel(capacity, counts, *refs):
    ins, halves, outs = refs[:counts], refs[counts : counts + 6], refs[counts + 6 :]
    rows = stacked(ins)
    total = None
    for i in range(2):
        gate_half, up_half, down_half = halves[3 * i : 3 * i + 3]
        gate_act = dot(rows, gate_half[...])
        hidden = (gate_act / (1.0 + jnp.exp(-gate_act)) * dot(rows, up_half[...])).astype(jnp.bfloat16)
        partial = dot(hidden, down_half[...])
        total = partial if total is None else total + partial
    scatter_out(total, capacity, outs)


def combine_kernel(chips, capacity, place, weights, *refs):
    refs[-1][...] = combined(refs[:-1], weights[...], place[0], place[1], chips, capacity).astype(jnp.bfloat16)


def final_kernel(chips, capacity, counts, place, weights, stream, *refs):
    total = combined(refs[:counts], weights[...], place[0], place[1], chips, capacity)
    for ref in refs[counts:-1]:
        total = total + ref[...].astype(jnp.float32)
    refs[-1][...] = (stream[...] + total).astype(jnp.bfloat16)


def in_vmem(count):
    return [pl.BlockSpec(memory_space=VMEM)] * count


SMEM_SPEC = pl.BlockSpec(memory_space=pltpu.SMEM)
ANY_SPEC = pl.BlockSpec(memory_space=pl.ANY)


def shards(
    queries, new_kv, cache, lengths, residual, out_weight, norm_gain, expert_ids, gates, w_gate, w_up, w_down,
):
    planes, chips, cores = (lax.axis_size(axis) for axis in ALL)
    mine = lax.axis_index("chip")
    base = lax.axis_index("req") * chips
    experts = planes * chips
    group, features = queries.shape[1:]
    slots = cache.shape[1]
    top_k = expert_ids.shape[2]
    capacity = 5 * group * top_k // (4 * experts)
    tiled = capacity % 8 == 0
    bf16 = jnp.bfloat16
    place = jnp.stack([base, mine]).astype(jnp.int32)

    def params(mib):
        return pltpu.CompilerParams(vmem_limit_bytes=mib << 20)

    def across(x, axis, j):
        size = lax.axis_size(axis)
        return lax.ppermute(x, axis, [(i, i ^ j) for i in range(size)])

    def to_chips(blocks):
        return [blocks[0]] + [across(blocks[j], "chip", j) for j in range(1, chips)]

    if tiled:
        block_shapes = [jax.ShapeDtypeStruct((capacity, features), bf16)] * chips
    else:
        block_shapes = [jax.ShapeDtypeStruct((chips * capacity, features), bf16)]
    blocks_n = len(block_shapes)

    def cut(blocks):
        return blocks if tiled else [blocks[0][j * capacity : (j + 1) * capacity] for j in range(chips)]

    def joined(blocks):
        return blocks if tiled else [jnp.concatenate(blocks, axis=0)]

    own_halves = [w_gate[0], w_up[0], w_down[0]]
    other_halves = [across(half, "core", 1) for half in own_halves]

    weights = jnp.sum(
        jnp.where(
            expert_ids[0][:, :, None] == jnp.arange(experts, dtype=jnp.int32), gates[0][:, :, None], 0.0
        ),
        axis=1,
    )
    weights_of = [weights] + [across(weights, "req", s) for s in range(1, planes)]

    stream, normed, appended, *outgoing = pl.pallas_call(
        functools.partial(attention_kernel, chips, capacity),
        out_shape=[
            jax.ShapeDtypeStruct((group, features), jnp.float32),
            jax.ShapeDtypeStruct((group, features), bf16),
            jax.ShapeDtypeStruct(cache.shape[1:], cache.dtype),
        ]
        + block_shapes,
        in_specs=[SMEM_SPEC, SMEM_SPEC] + [ANY_SPEC] * 5 + in_vmem(2),
        out_specs=in_vmem(2) + [ANY_SPEC] + in_vmem(blocks_n),
        scratch_shapes=[
            VMEM(cache.shape[1:], bf16),
            VMEM(new_kv.shape[1:], bf16),
            VMEM((group, features), bf16),
            VMEM((group, features), bf16),
            VMEM(out_weight.shape, bf16),
            VMEM((slots + group, features), bf16),
            VMEM((slots + group, features), bf16),
            VMEM((group, features), bf16),
            pltpu.SemaphoreType.DMA((9,)),
        ],
        compiler_params=params(40),
        name="attention",
    )(place, lengths, queries[0], new_kv[0], cache[0], residual[0], out_weight, norm_gain[None], weights)

    rows_of = [normed] + [across(normed, "req", s) for s in range(1, planes)]
    partials = []
    for s in range(planes):
        if s > 0:
            outgoing = pl.pallas_call(
                functools.partial(gather_kernel, chips, capacity),
                out_shape=block_shapes,
                in_specs=[SMEM_SPEC] + in_vmem(2),
                out_specs=in_vmem(blocks_n),
                compiler_params=params(16),
                name="gather",
            )(place, rows_of[s], weights_of[s])
        arrived = joined(to_chips(cut(outgoing)))
        results = pl.pallas_call(
            functools.partial(expert_kernel, capacity, blocks_n),
            out_shape=block_shapes,
            in_specs=in_vmem(blocks_n + 6),
            out_specs=in_vmem(blocks_n),
            compiler_params=params(24),
            cost_estimate=pl.CostEstimate(
                flops=12 * chips * capacity * features * w_gate.shape[2],
                bytes_accessed=12 * features * w_gate.shape[2],
                transcendentals=0,
            ),
            name="experts",
        )(*arrived, *own_halves, *other_halves)
        returned = joined(to_chips(cut(results)))
        if s == 0:
            own_returned = returned
        else:
            partial = pl.pallas_call(
                functools.partial(combine_kernel, chips, capacity),
                out_shape=jax.ShapeDtypeStruct((group, features), bf16),
                in_specs=[SMEM_SPEC] + in_vmem(1 + blocks_n),
                out_specs=pl.BlockSpec(memory_space=VMEM),
                compiler_params=params(16),
                name="combine",
            )(place, weights_of[s], *returned)
            partials.append(across(partial, "req", s))
    layer_out = pl.pallas_call(
        functools.partial(final_kernel, chips, capacity, blocks_n),
        out_shape=jax.ShapeDtypeStruct((group, features), bf16),
        in_specs=[SMEM_SPEC] + in_vmem(2 + blocks_n + len(partials)),
        out_specs=pl.BlockSpec(memory_space=VMEM),
        compiler_params=params(16),
        name="final",
    )(place, weights, stream, *own_returned, *partials)
    return (layer_out[None], appended[None])


def solution(mesh):
    planes, width = (mesh.shape[axis] for axis in ("req", "exp"))
    split = Mesh(mesh.devices.reshape(planes, width // 2, 2), ALL)
    by_device = P(ALL)
    placed = (by_device,) * 5 + (P(), P()) + (by_device,) * 5
    return jax.shard_map(
        shards,
        mesh=split,
        in_specs=placed,
        out_specs=(by_device, by_device),
        check_vma=False,
    )
```

time: 328 us -> 133 us (0.41)
  blocking collectives: 123 us -> 0 us
  waiting for transfers between devices: 115 us -> 34.2 us
  starting transfers between devices: 4.09 us -> 53.3 us
  local copies, waits for them, and re-layouts: 54.7 us -> 5.92 us
  Pallas kernels: 0 us -> 36.7 us
  matrix products: 15.9 us -> 0 us
  other arithmetic: 12.6 us -> 0.8 us
    all_to_all x1 -> x0, blocking collectives: 123 us -> none  [shards(): lax.all_to_all(doubled, ('req', 'exp'), split_axis=0, concat_axis=0, tile...]
    all_to_all x1 -> x0, waiting for transfers between devices: 115 us -> none  [shards(): lax.all_to_all(partials.astype(jnp.bfloat16), ('req', 'exp'), split_axis=...]
    ppermute x0 -> x36, starting transfers between devices: none -> 53.3 us  [across(): return lax.ppermute(x, axis, [(i, i ^ j) for i in range(size)])]
    pallas_call x0 -> x12, Pallas kernels: none -> 36.7 us  [the longest x4 18.4 us: shards(): pl.pallas_call(functools.partial(expert_kernel, capacity, blocks_n), out_...]
    ppermute x0 -> x36, waiting for transfers between devices: none -> 34.2 us  [across(): return lax.ppermute(x, axis, [(i, i ^ j) for i in range(size)])]
    dot_general x6 -> x0, matrix products: 15.9 us -> none  [the longest x1 4.69 us: expert_rows(): partial_sum = jnp.dot(hidden, down_half, preferred_element_type=jnp.float32)]
    unnamed x26 -> x16, local copies, waits for them, and re-layouts: 21.6 us -> 5.84 us
    gather x2 -> x0, local copies, waits for them, and re-layouts: 11.4 us -> none  [the longest x1 7.36 us: shards(): expert_out.reshape(experts_all * capacity, features)[position]]
  transfers between devices with their start and end apart: 1 -> 36, of which waited for: 1 -> 10; matrix products, arithmetic and copies ran while one was open for 0% -> 1% of each run, Pallas kernels for 0% -> 26%
where the time goes in v1:
time: 133 us; the launch traced here: 132 us
  starting transfers between devices  53.3 us (40%)
  Pallas kernels  36.7 us (28%)
  waiting for transfers between devices  34.2 us (26%)
  local copies, waits for them, and re-layouts  5.92 us (4%)
  between operations  1.49 us (1%)
    ppermute x36, starting transfers between devices, across(): return lax.ppermute(x, axis, [(i, i ^ j) for i in range(size)])  53.3 us
    ppermute x36, waiting for transfers between devices, across(): return lax.ppermute(x, axis, [(i, i ^ j) for i in range(size)])  34.2 us
    pallas_call x4, Pallas kernels, shards(): pl.pallas_call(functools.partial(expert_kernel, capacity, blocks_n), out_...  18.4 us
    pallas_call x1, Pallas kernels, shards(): pl.pallas_call(functools.partial(attention_kernel, chips, capacity), out_...  9.96 us
    unnamed x16, local copies, waits for them, and re-layouts  5.84 us
    pallas_call x3, Pallas kernels, shards(): pl.pallas_call(functools.partial(gather_kernel, chips, capacity), out_sha...  3.39 us
    pallas_call x3, Pallas kernels, shards(): pl.pallas_call(functools.partial(combine_kernel, chips, capacity), out_sh...  3.18 us
  transfers between devices with their start and end apart: 36, of which 10 were waited for; matrix products, arithmetic and copies ran while one was open for 1% of the time, Pallas kernels for 26%

profile of v1, /device:TPU:0, one launch (start us, length us, event | category | flops | bytes accessed | tf_op | source)
XLA Modules:
  0.0 132.5 jit_solution(2422824057981368897)
XLA Ops:
  3.2 2.2 %copy-done.3 = bf16[1,512,2,2048]{3,2,1,0:T(2,128)(2,1)S(1)} copy-done((bf16[1,512,2,2048]{3,2,1,0:T(2,128)(2,1)S(1)}, bf16[1,512,2,2048]{3,2,1,0:T(2,128)(2,1)}, u32[]{:S(2)}) %copy-start.3) | copy-done | bytes 4194328
  9.0 10.0 %attention.1 = (f32[64,2048]{1,0:T(8,128)S(1)}, bf16[64,2048]{1,0:T(8,128)(2,1)S(1)}, bf16[512,2,2048]{2,1,0:T(2,128)(2,1)}, bf16[40,2048]{1,0:T(8,128)(2,1)S(1)...) custom-call(s32[2]{0:T(128)S(1)} %pad_add_fusion.place, ...), custom_call_target="tpu_custom_call" | custom-call | tf_op jit(solution)/shard_map/attention/pallas_call | solution.py:231
  19.0 4.7 %collective-permute-start.28 = (bf16[64,2048]{1,0:T(8,128)(2,1)S(1)}, bf16[64,2048]{1,0:T(8,128)(2,1)S(1)}, u32[]{:S(2)}, u32[]{:S(2)}) collective-permute-start(bf16[64,2048]{1,0:T(8,128)(2,1)S(1)} %get-tuple-element.46), channel_id=1, source_target_pairs={{0,24},{8,16},{16,8},{24,0},{1,25},{9,17},{17,9},{25,1},{2,26},{10... | collective-permute-start | bytes 786440 | tf_op jit(solution)/shard_map/ppermute | solution.py:203
  23.8 7.6 %collective-permute-done.27.weights = f32[64,16]{1,0:T(8,128)S(1)} collective-permute-done((f32[64,16]{1,0:T(8,128)S(1)}, f32[64,16]{1,0:T(8,128)S(1)}, u32[]{:S(2)}, u32[]{:S(2)}) %collective-permute-start.27) | collective-permute-done | bytes 4128 | tf_op jit(solution)/shard_map/ppermute | solution.py:203
  31.5 7.0 %collective-permute-start.18 = (f32[64,16]{1,0:T(8,128)S(1)}, f32[64,16]{1,0:T(8,128)S(1)}, u32[]{:S(2)}, u32[]{:S(2)}) collective-permute-start(f32[64,16]{1,0:T(8,128)S(1)} %copy.20.weights), channel_id=1, source_target_pairs={{0,16},{8,24},{16,0},{24,8},{1,17},{9,25},{17,1},{25,9},{2,18},{10... | collective-permute-start | bytes 12296 | tf_op jit(solution)/shard_map/ppermute | solution.py:203
  38.4 2.2 %collective-permute-done.18.weights = f32[64,16]{1,0:T(8,128)S(1)} collective-permute-done((f32[64,16]{1,0:T(8,128)S(1)}, f32[64,16]{1,0:T(8,128)S(1)}, u32[]{:S(2)}, u32[]{:S(2)}) %collective-permute-start.18) | collective-permute-done | bytes 4128 | tf_op jit(solution)/shard_map/ppermute | solution.py:203
  40.7 1.6 %collective-permute-start.9 = (f32[64,16]{1,0:T(8,128)S(1)}, f32[64,16]{1,0:T(8,128)S(1)}, u32[]{:S(2)}, u32[]{:S(2)}) collective-permute-start(f32[64,16]{1,0:T(8,128)S(1)} %copy.20.weights), channel_id=1, source_target_pairs={{0,8},{8,0},{16,24},{24,16},{1,9},{9,1},{17,25},{25,17},{2,10},{10... | collective-permute-start | bytes 12296 | tf_op jit(solution)/shard_map/ppermute | solution.py:203
  42.2 2.4 %collective-permute-done.9.weights = f32[64,16]{1,0:T(8,128)S(1)} collective-permute-done((f32[64,16]{1,0:T(8,128)S(1)}, f32[64,16]{1,0:T(8,128)S(1)}, u32[]{:S(2)}, u32[]{:S(2)}) %collective-permute-start.9) | collective-permute-done | bytes 4128 | tf_op jit(solution)/shard_map/ppermute | solution.py:203
  44.6 2.6 %collective-permute-start.19 = (bf16[64,2048]{1,0:T(8,128)(2,1)S(1)}, bf16[64,2048]{1,0:T(8,128)(2,1)S(1)}, u32[]{:S(2)}, u32[]{:S(2)}) collective-permute-start(bf16[64,2048]{1,0:T(8,128)(2,1)S(1)} %get-tuple-element.46), channel_id=1, source_target_pairs={{0,16},{8,24},{16,0},{24,8},{1,17},{9,25},{17,1},{25,9},{2,18},{10... | collective-permute-start | bytes 786440 | tf_op jit(solution)/shard_map/ppermute | solution.py:203
  48.4 8.3 %collective-permute-done.19.rows = bf16[64,2048]{1,0:T(8,128)(2,1)S(1)} collective-permute-done((bf16[64,2048]{1,0:T(8,128)(2,1)S(1)}, bf16[64,2048]{1,0:T(8,128)(2,1)S(1)}, u32[]{:S(2)}, u32[]{:S(2)}) %collective-permute-start.19) | collective-permute-done | bytes 262176 | tf_op jit(solution)/shard_map/ppermute | solution.py:203
  56.7 1.5 %collective-permute-start.29 = (bf16[40,2048]{1,0:T(8,128)(2,1)S(1)}, bf16[40,2048]{1,0:T(8,128)(2,1)S(1)}, u32[]{:S(2)}, u32[]{:S(2)}) collective-permute-start(bf16[40,2048]{1,0:T(8,128)(2,1)S(1)} %get-tuple-element.64), channel_id=1, source_target_pairs={{0,2},{2,0},{4,6},{6,4},{1,3},{3,1},{5,7},{7,5},{8,10},{10,8},{12,... | collective-permute-start | bytes 491528 | tf_op jit(solution)/shard_map/ppermute | solution.py:203
  58.2 1.5 %collective-permute-start.30 = (bf16[40,2048]{1,0:T(8,128)(2,1)S(1)}, bf16[40,2048]{1,0:T(8,128)(2,1)S(1)}, u32[]{:S(2)}, u32[]{:S(2)}) collective-permute-start(bf16[40,2048]{1,0:T(8,128)(2,1)S(1)} %get-tuple-element.65), channel_id=1, source_target_pairs={{0,4},{2,6},{4,0},{6,2},{1,5},{3,7},{5,1},{7,3},{8,12},{10,14},{12... | collective-permute-start | bytes 491528 | tf_op jit(solution)/shard_map/ppermute | solution.py:203
  59.7 2.3 %collective-permute-done.29.refs_1_ = bf16[40,2048]{1,0:T(8,128)(2,1)S(1)} collective-permute-done((bf16[40,2048]{1,0:T(8,128)(2,1)S(1)}, bf16[40,2048]{1,0:T(8,128)(2,1)S(1)}, u32[]{:S(2)}, u32[]{:S(2)}) %collective-permute-start.29) | collective-permute-done | bytes 163872 | tf_op jit(solution)/shard_map/ppermute | solution.py:203
  62.0 2.4 %collective-permute-start.31 = (bf16[40,2048]{1,0:T(8,128)(2,1)S(1)}, bf16[40,2048]{1,0:T(8,128)(2,1)S(1)}, u32[]{:S(2)}, u32[]{:S(2)}) collective-permute-start(bf16[40,2048]{1,0:T(8,128)(2,1)S(1)} %get-tuple-element.66), channel_id=1, source_target_pairs={{0,6},{2,4},{4,2},{6,0},{1,7},{3,5},{5,3},{7,1},{8,14},{10,12},{12... | collective-permute-start | bytes 491528 | tf_op jit(solution)/shard_map/ppermute | solution.py:203
  67.3 2.6 %collective-permute-done.31.refs_3_ = bf16[40,2048]{1,0:T(8,128)(2,1)S(1)} collective-permute-done((bf16[40,2048]{1,0:T(8,128)(2,1)S(1)}, bf16[40,2048]{1,0:T(8,128)(2,1)S(1)}, u32[]{:S(2)}, u32[]{:S(2)}) %collective-permute-start.31) | collective-permute-done | bytes 163872 | tf_op jit(solution)/shard_map/ppermute | solution.py:203
  70.0 1.5 %collective-permute-start.1 = (bf16[40,2048]{1,0:T(8,128)(2,1)S(1)}, bf16[40,2048]{1,0:T(8,128)(2,1)S(1)}, u32[]{:S(2)}, u32[]{:S(2)}) collective-permute-start(bf16[40,2048]{1,0:T(8,128)(2,1)S(1)} %get-tuple-element.40), channel_id=1, source_target_pairs={{0,4},{2,6},{4,0},{6,2},{1,5},{3,7},{5,1},{7,3},{8,12},{10,14},{12... | collective-permute-start | bytes 491528 | tf_op jit(solution)/shard_map/ppermute | solution.py:203
  73.3 1.6 %collective-permute-start.22 = (bf16[40,2048]{1,0:T(8,128)(2,1)S(1)}, bf16[40,2048]{1,0:T(8,128)(2,1)S(1)}, u32[]{:S(2)}, u32[]{:S(2)}) collective-permute-start(bf16[40,2048]{1,0:T(8,128)(2,1)S(1)} %get-tuple-element.58), channel_id=1, source_target_pairs={{0,6},{2,4},{4,2},{6,0},{1,7},{3,5},{5,3},{7,1},{8,14},{10,12},{12... | collective-permute-start | bytes 491528 | tf_op jit(solution)/shard_map/ppermute | solution.py:203
  75.0 4.6 %experts.7 = (bf16[40,2048]{1,0:T(8,128)(2,1)S(1)}, bf16[40,2048]{1,0:T(8,128)(2,1)S(1)}, bf16[40,2048]{1,0:T(8,128)(2,1)S(1)}, bf16[40,2048]{1,0:T(8,128)(2,1)S(1)}) custom-call(bf16[40,2048]{1,0:T(8,128)(2,1)S(1)} %get-tuple-element.63.refs_0_, bf16[40,2048]{1,0:T(8,128)(2,1)S(1)} %collective-permute-done.29.refs_1_, ...), custom_call_target="tpu_custom_call" | custom-call | flops 2013265920 | bytes 12582912 | tf_op jit(solution)/shard_map/experts/pallas_call | solution.py:269
  80.9 2.8 %collective-permute-done.21.refs_2_ = bf16[40,2048]{1,0:T(8,128)(2,1)S(1)} collective-permute-done((bf16[40,2048]{1,0:T(8,128)(2,1)S(1)}, bf16[40,2048]{1,0:T(8,128)(2,1)S(1)}, u32[]{:S(2)}, u32[]{:S(2)}) %collective-permute-start.21) | collective-permute-done | bytes 163872 | tf_op jit(solution)/shard_map/ppermute | solution.py:203
  83.7 2.0 %collective-permute-start.12 = (bf16[40,2048]{1,0:T(8,128)(2,1)S(1)}, bf16[40,2048]{1,0:T(8,128)(2,1)S(1)}, u32[]{:S(2)}, u32[]{:S(2)}) collective-permute-start(bf16[40,2048]{1,0:T(8,128)(2,1)S(1)} %get-tuple-element.49), channel_id=1, source_target_pairs={{0,4},{2,6},{4,0},{6,2},{1,5},{3,7},{5,1},{7,3},{8,12},{10,14},{12... | collective-permute-start | bytes 491528 | tf_op jit(solution)/shard_map/ppermute | solution.py:203
  86.0 4.6 %experts.6 = (bf16[40,2048]{1,0:T(8,128)(2,1)S(1)}, bf16[40,2048]{1,0:T(8,128)(2,1)S(1)}, bf16[40,2048]{1,0:T(8,128)(2,1)S(1)}, bf16[40,2048]{1,0:T(8,128)(2,1)S(1)}) custom-call(bf16[40,2048]{1,0:T(8,128)(2,1)S(1)} %get-tuple-element.55.refs_0_, bf16[40,2048]{1,0:T(8,128)(2,1)S(1)} %collective-permute-done.20.refs_1_, ...), custom_call_target="tpu_custom_call" | custom-call | flops 2013265920 | bytes 12582912 | tf_op jit(solution)/shard_map/experts/pallas_call | solution.py:269
  90.6 2.7 %collective-permute-start.2 = (bf16[40,2048]{1,0:T(8,128)(2,1)S(1)}, bf16[40,2048]{1,0:T(8,128)(2,1)S(1)}, u32[]{:S(2)}, u32[]{:S(2)}) collective-permute-start(bf16[40,2048]{1,0:T(8,128)(2,1)S(1)} %get-tuple-element.41), channel_id=1, source_target_pairs={{0,6},{2,4},{4,2},{6,0},{1,7},{3,5},{5,3},{7,1},{8,14},{10,12},{12... | collective-permute-start | bytes 491528 | tf_op jit(solution)/shard_map/ppermute | solution.py:203
  94.2 2.6 %collective-permute-start.34 = (bf16[40,2048]{1,0:T(8,128)(2,1)S(1)}, bf16[40,2048]{1,0:T(8,128)(2,1)S(1)}, u32[]{:S(2)}, u32[]{:S(2)}) collective-permute-start(bf16[40,2048]{1,0:T(8,128)(2,1)S(1)} %get-tuple-element.70), channel_id=1, source_target_pairs={{0,6},{2,4},{4,2},{6,0},{1,7},{3,5},{5,3},{7,1},{8,14},{10,12},{12... | collective-permute-start | bytes 491528 | tf_op jit(solution)/shard_map/ppermute | solution.py:203
  97.2 4.8 %experts.5 = (bf16[40,2048]{1,0:T(8,128)(2,1)S(1)}, bf16[40,2048]{1,0:T(8,128)(2,1)S(1)}, bf16[40,2048]{1,0:T(8,128)(2,1)S(1)}, bf16[40,2048]{1,0:T(8,128)(2,1)S(1)}) custom-call(bf16[40,2048]{1,0:T(8,128)(2,1)S(1)} %get-tuple-element.47.refs_0_, bf16[40,2048]{1,0:T(8,128)(2,1)S(1)} %collective-permute-done.11.refs_1_, ...), custom_call_target="tpu_custom_call" | custom-call | flops 2013265920 | bytes 12582912 | tf_op jit(solution)/shard_map/experts/pallas_call | solution.py:269
  102.5 2.6 %collective-permute-start.25 = (bf16[40,2048]{1,0:T(8,128)(2,1)S(1)}, bf16[40,2048]{1,0:T(8,128)(2,1)S(1)}, u32[]{:S(2)}, u32[]{:S(2)}) collective-permute-start(bf16[40,2048]{1,0:T(8,128)(2,1)S(1)} %get-tuple-element.62), channel_id=1, source_target_pairs={{0,6},{2,4},{4,2},{6,0},{1,7},{3,5},{5,3},{7,1},{8,14},{10,12},{12... | collective-permute-start | bytes 491528 | tf_op jit(solution)/shard_map/ppermute | solution.py:203
  108.3 2.1 %collective-permute-start.16 = (bf16[40,2048]{1,0:T(8,128)(2,1)S(1)}, bf16[40,2048]{1,0:T(8,128)(2,1)S(1)}, u32[]{:S(2)}, u32[]{:S(2)}) collective-permute-start(bf16[40,2048]{1,0:T(8,128)(2,1)S(1)} %get-tuple-element.54), channel_id=1, source_target_pairs={{0,6},{2,4},{4,2},{6,0},{1,7},{3,5},{5,3},{7,1},{8,14},{10,12},{12... | collective-permute-start | bytes 491528 | tf_op jit(solution)/shard_map/ppermute | solution.py:203
  110.4 4.6 %experts.4 = (bf16[40,2048]{1,0:T(8,128)(2,1)S(1)}, bf16[40,2048]{1,0:T(8,128)(2,1)S(1)}, bf16[40,2048]{1,0:T(8,128)(2,1)S(1)}, bf16[40,2048]{1,0:T(8,128)(2,1)S(1)}) custom-call(bf16[40,2048]{1,0:T(8,128)(2,1)S(1)} %get-tuple-element.38.refs_0_, bf16[40,2048]{1,0:T(8,128)(2,1)S(1)} %collective-permute-done.refs_1_, ...), custom_call_target="tpu_custom_call" | custom-call | flops 2013265920 | bytes 12582912 | tf_op jit(solution)/shard_map/experts/pallas_call | solution.py:269
  116.8 2.2 %collective-permute-start.35 = (bf16[64,2048]{1,0:T(8,128)(2,1)S(1)}, bf16[64,2048]{1,0:T(8,128)(2,1)S(1)}, u32[]{:S(2)}, u32[]{:S(2)}) collective-permute-start(bf16[64,2048]{1,0:T(8,128)(2,1)S(1)} %combine.5), channel_id=1, source_target_pairs={{0,24},{8,16},{16,8},{24,0},{1,25},{9,17},{17,9},{25,1},{2,26},{10... | collective-permute-start | bytes 786440 | tf_op jit(solution)/shard_map/ppermute | solution.py:203
  121.3 2.2 %collective-permute-start.17 = (bf16[64,2048]{1,0:T(8,128)(2,1)S(1)}, bf16[64,2048]{1,0:T(8,128)(2,1)S(1)}, u32[]{:S(2)}, u32[]{:S(2)}) collective-permute-start(bf16[64,2048]{1,0:T(8,128)(2,1)S(1)} %combine.3), channel_id=1, source_target_pairs={{0,8},{8,0},{16,24},{24,16},{1,9},{9,1},{17,25},{25,17},{2,10},{10... | collective-permute-start | bytes 786440 | tf_op jit(solution)/shard_map/ppermute | solution.py:203
  124.2 2.1 %collective-permute-start.8 = (bf16[40,2048]{1,0:T(8,128)(2,1)S(1)}, bf16[40,2048]{1,0:T(8,128)(2,1)S(1)}, u32[]{:S(2)}, u32[]{:S(2)}) collective-permute-start(bf16[40,2048]{1,0:T(8,128)(2,1)S(1)} %get-tuple-element.45), channel_id=1, source_target_pairs={{0,6},{2,4},{4,2},{6,0},{1,7},{3,5},{5,3},{7,1},{8,14},{10,12},{12... | collective-permute-start | bytes 491528 | tf_op jit(solution)/shard_map/ppermute | solution.py:203
  126.3 4.3 %collective-permute-done.7.refs_2_ = bf16[40,2048]{1,0:T(8,128)(2,1)S(1)} collective-permute-done((bf16[40,2048]{1,0:T(8,128)(2,1)S(1)}, bf16[40,2048]{1,0:T(8,128)(2,1)S(1)}, u32[]{:S(2)}, u32[]{:S(2)}) %collective-permute-start.7) | collective-permute-done | bytes 163872 | tf_op jit(solution)/shard_map/ppermute | solution.py:203
  130.7 1.8 %final.1 = bf16[64,2048]{1,0:T(8,128)(2,1)} custom-call(s32[2]{0:T(128)S(1)} %pad_add_fusion.place, f32[64,16]{1,0:T(8,128)S(1)} %copy.20.weights, f32[64,2048]{1,0:T(8,128)S(1)} %get-tuple-element.37.stream, bf16[40,2048]{1,0:T(8,128)(2,1)S(1)} %get-tuple-element.42.refs_0_, bf16[40,2048]{1,0:T(8,128)(2,1)S(1)} %collective-permute-done.6.refs_1_, ...), custom_call_target="tpu_custom_call" | custom-call | tf_op jit(solution)/shard_map/final/pallas_call | solution.py:295
  (71 shorter events, 23.1 us)
Async XLA Ops:
  0.6 70.8 %collective-permute-start.3 = (bf16[2048,512]{1,0:T(8,128)(2,1)}, bf16[2048,512]{1,0:T(8,128)(2,1)S(1)}, u32[]{:S(2)}, u32[]{:S(2)}) collective-permute-start(bf16[2048,512]{1,0:T(8,128)(2,1)} %bitcast.14), channel_id=1, source_target_pairs={{0,1},{1,0},{2,3},{3,2},{4,5},{5,4},{6,7},{7,6},{8,9},{9,8},{10,11... | collective-permute-start | bytes 6291464 | tf_op jit(solution)/shard_map/ppermute | solution.py:203
  1.1 71.6 %collective-permute-start.4 = (bf16[2048,512]{1,0:T(8,128)(2,1)}, bf16[2048,512]{1,0:T(8,128)(2,1)}, u32[]{:S(2)}, u32[]{:S(2)}) collective-permute-start(bf16[2048,512]{1,0:T(8,128)(2,1)} %bitcast.19), channel_id=1, source_target_pairs={{0,1},{1,0},{2,3},{3,2},{4,5},{5,4},{6,7},{7,6},{8,9},{9,8},{10,11... | collective-permute-start | bytes 6291464 | tf_op jit(solution)/shard_map/ppermute | solution.py:203
  1.2 72.1 %collective-permute-start.5 = (bf16[512,2048]{1,0:T(8,128)(2,1)}, bf16[512,2048]{1,0:T(8,128)(2,1)}, u32[]{:S(2)}, u32[]{:S(2)}) collective-permute-start(bf16[512,2048]{1,0:T(8,128)(2,1)} %bitcast.24), channel_id=1, source_target_pairs={{0,1},{1,0},{2,3},{3,2},{4,5},{5,4},{6,7},{7,6},{8,9},{9,8},{10,11... | collective-permute-start | bytes 6291464 | tf_op jit(solution)/shard_map/ppermute | solution.py:203
  19.0 28.2 %collective-permute-start.28 = (bf16[64,2048]{1,0:T(8,128)(2,1)S(1)}, bf16[64,2048]{1,0:T(8,128)(2,1)S(1)}, u32[]{:S(2)}, u32[]{:S(2)}) collective-permute-start(bf16[64,2048]{1,0:T(8,128)(2,1)S(1)} %get-tuple-element.46), channel_id=1, source_target_pairs={{0,24},{8,16},{16,8},{24,0},{1,25},{9,17},{17,9},{25,1},{2,26},{10... | collective-permute-start | bytes 786440 | tf_op jit(solution)/shard_map/ppermute | solution.py:203
  23.7 7.7 %collective-permute-start.27 = (f32[64,16]{1,0:T(8,128)S(1)}, f32[64,16]{1,0:T(8,128)S(1)}, u32[]{:S(2)}, u32[]{:S(2)}) collective-permute-start(f32[64,16]{1,0:T(8,128)S(1)} %copy.20.weights), channel_id=1, source_target_pairs={{0,24},{8,16},{16,8},{24,0},{1,25},{9,17},{17,9},{25,1},{2,26},{10... | collective-permute-start | bytes 12296 | tf_op jit(solution)/shard_map/ppermute | solution.py:203
  31.5 9.2 %collective-permute-start.18 = (f32[64,16]{1,0:T(8,128)S(1)}, f32[64,16]{1,0:T(8,128)S(1)}, u32[]{:S(2)}, u32[]{:S(2)}) collective-permute-start(f32[64,16]{1,0:T(8,128)S(1)} %copy.20.weights), channel_id=1, source_target_pairs={{0,16},{8,24},{16,0},{24,8},{1,17},{9,25},{17,1},{25,9},{2,18},{10... | collective-permute-start | bytes 12296 | tf_op jit(solution)/shard_map/ppermute | solution.py:203
  44.6 12.1 %collective-permute-start.19 = (bf16[64,2048]{1,0:T(8,128)(2,1)S(1)}, bf16[64,2048]{1,0:T(8,128)(2,1)S(1)}, u32[]{:S(2)}, u32[]{:S(2)}) collective-permute-start(bf16[64,2048]{1,0:T(8,128)(2,1)S(1)} %get-tuple-element.46), channel_id=1, source_target_pairs={{0,16},{8,24},{16,0},{24,8},{1,17},{9,25},{17,1},{25,9},{2,18},{10... | collective-permute-start | bytes 786440 | tf_op jit(solution)/shard_map/ppermute | solution.py:203
  47.2 11.0 %collective-permute-start.10 = (bf16[64,2048]{1,0:T(8,128)(2,1)S(1)}, bf16[64,2048]{1,0:T(8,128)(2,1)S(1)}, u32[]{:S(2)}, u32[]{:S(2)}) collective-permute-start(bf16[64,2048]{1,0:T(8,128)(2,1)S(1)} %get-tuple-element.46), channel_id=1, source_target_pairs={{0,8},{8,0},{16,24},{24,16},{1,9},{9,1},{17,25},{25,17},{2,10},{10... | collective-permute-start | bytes 786440 | tf_op jit(solution)/shard_map/ppermute | solution.py:203
  58.2 8.5 %collective-permute-start.30 = (bf16[40,2048]{1,0:T(8,128)(2,1)S(1)}, bf16[40,2048]{1,0:T(8,128)(2,1)S(1)}, u32[]{:S(2)}, u32[]{:S(2)}) collective-permute-start(bf16[40,2048]{1,0:T(8,128)(2,1)S(1)} %get-tuple-element.65), channel_id=1, source_target_pairs={{0,4},{2,6},{4,0},{6,2},{1,5},{3,7},{5,1},{7,3},{8,12},{10,14},{12... | collective-permute-start | bytes 491528 | tf_op jit(solution)/shard_map/ppermute | solution.py:203
  62.0 7.9 %collective-permute-start.31 = (bf16[40,2048]{1,0:T(8,128)(2,1)S(1)}, bf16[40,2048]{1,0:T(8,128)(2,1)S(1)}, u32[]{:S(2)}, u32[]{:S(2)}) collective-permute-start(bf16[40,2048]{1,0:T(8,128)(2,1)S(1)} %get-tuple-element.66), channel_id=1, source_target_pairs={{0,6},{2,4},{4,2},{6,0},{1,7},{3,5},{5,3},{7,1},{8,14},{10,12},{12... | collective-permute-start | bytes 491528 | tf_op jit(solution)/shard_map/ppermute | solution.py:203
  66.7 23.9 %collective-permute-start = (bf16[40,2048]{1,0:T(8,128)(2,1)S(1)}, bf16[40,2048]{1,0:T(8,128)(2,1)S(1)}, u32[]{:S(2)}, u32[]{:S(2)}) collective-permute-start(bf16[40,2048]{1,0:T(8,128)(2,1)S(1)} %get-tuple-element.39), channel_id=1, source_target_pairs={{0,2},{2,0},{4,6},{6,4},{1,3},{3,1},{5,7},{7,5},{8,10},{10,8},{12,... | collective-permute-start | bytes 491528 | tf_op jit(solution)/shard_map/ppermute | solution.py:203
  70.0 23.3 %collective-permute-start.1 = (bf16[40,2048]{1,0:T(8,128)(2,1)S(1)}, bf16[40,2048]{1,0:T(8,128)(2,1)S(1)}, u32[]{:S(2)}, u32[]{:S(2)}) collective-permute-start(bf16[40,2048]{1,0:T(8,128)(2,1)S(1)} %get-tuple-element.40), channel_id=1, source_target_pairs={{0,4},{2,6},{4,0},{6,2},{1,5},{3,7},{5,1},{7,3},{8,12},{10,14},{12... | collective-permute-start | bytes 491528 | tf_op jit(solution)/shard_map/ppermute | solution.py:203
  71.5 8.1 %collective-permute-start.20 = (bf16[40,2048]{1,0:T(8,128)(2,1)S(1)}, bf16[40,2048]{1,0:T(8,128)(2,1)S(1)}, u32[]{:S(2)}, u32[]{:S(2)}) collective-permute-start(bf16[40,2048]{1,0:T(8,128)(2,1)S(1)} %get-tuple-element.56), channel_id=1, source_target_pairs={{0,2},{2,0},{4,6},{6,4},{1,3},{3,1},{5,7},{7,5},{8,10},{10,8},{12,... | collective-permute-start | bytes 491528 | tf_op jit(solution)/shard_map/ppermute | solution.py:203
  72.8 11.0 %collective-permute-start.21 = (bf16[40,2048]{1,0:T(8,128)(2,1)S(1)}, bf16[40,2048]{1,0:T(8,128)(2,1)S(1)}, u32[]{:S(2)}, u32[]{:S(2)}) collective-permute-start(bf16[40,2048]{1,0:T(8,128)(2,1)S(1)} %get-tuple-element.57), channel_id=1, source_target_pairs={{0,4},{2,6},{4,0},{6,2},{1,5},{3,7},{5,1},{7,3},{8,12},{10,14},{12... | collective-permute-start | bytes 491528 | tf_op jit(solution)/shard_map/ppermute | solution.py:203
  73.3 12.4 %collective-permute-start.22 = (bf16[40,2048]{1,0:T(8,128)(2,1)S(1)}, bf16[40,2048]{1,0:T(8,128)(2,1)S(1)}, u32[]{:S(2)}, u32[]{:S(2)}) collective-permute-start(bf16[40,2048]{1,0:T(8,128)(2,1)S(1)} %get-tuple-element.58), channel_id=1, source_target_pairs={{0,6},{2,4},{4,2},{6,0},{1,7},{3,5},{5,3},{7,1},{8,14},{10,12},{12... | collective-permute-start | bytes 491528 | tf_op jit(solution)/shard_map/ppermute | solution.py:203
  79.5 14.2 %collective-permute-start.11 = (bf16[40,2048]{1,0:T(8,128)(2,1)S(1)}, bf16[40,2048]{1,0:T(8,128)(2,1)S(1)}, u32[]{:S(2)}, u32[]{:S(2)}) collective-permute-start(bf16[40,2048]{1,0:T(8,128)(2,1)S(1)} %get-tuple-element.48), channel_id=1, source_target_pairs={{0,2},{2,0},{4,6},{6,4},{1,3},{3,1},{5,7},{7,5},{8,10},{10,8},{12,... | collective-permute-start | bytes 491528 | tf_op jit(solution)/shard_map/ppermute | solution.py:203
  83.7 10.4 %collective-permute-start.12 = (bf16[40,2048]{1,0:T(8,128)(2,1)S(1)}, bf16[40,2048]{1,0:T(8,128)(2,1)S(1)}, u32[]{:S(2)}, u32[]{:S(2)}) collective-permute-start(bf16[40,2048]{1,0:T(8,128)(2,1)S(1)} %get-tuple-element.49), channel_id=1, source_target_pairs={{0,4},{2,6},{4,0},{6,2},{1,5},{3,7},{5,1},{7,3},{8,12},{10,14},{12... | collective-permute-start | bytes 491528 | tf_op jit(solution)/shard_map/ppermute | solution.py:203
  85.7 11.1 %collective-permute-start.13 = (bf16[40,2048]{1,0:T(8,128)(2,1)S(1)}, bf16[40,2048]{1,0:T(8,128)(2,1)S(1)}, u32[]{:S(2)}, u32[]{:S(2)}) collective-permute-start(bf16[40,2048]{1,0:T(8,128)(2,1)S(1)} %get-tuple-element.50), channel_id=1, source_target_pairs={{0,6},{2,4},{4,2},{6,0},{1,7},{3,5},{5,3},{7,1},{8,14},{10,12},{12... | collective-permute-start | bytes 491528 | tf_op jit(solution)/shard_map/ppermute | solution.py:203
  90.6 11.4 %collective-permute-start.2 = (bf16[40,2048]{1,0:T(8,128)(2,1)S(1)}, bf16[40,2048]{1,0:T(8,128)(2,1)S(1)}, u32[]{:S(2)}, u32[]{:S(2)}) collective-permute-start(bf16[40,2048]{1,0:T(8,128)(2,1)S(1)} %get-tuple-element.41), channel_id=1, source_target_pairs={{0,6},{2,4},{4,2},{6,0},{1,7},{3,5},{5,3},{7,1},{8,14},{10,12},{12... | collective-permute-start | bytes 491528 | tf_op jit(solution)/shard_map/ppermute | solution.py:203
  93.2 9.3 %collective-permute-start.32 = (bf16[40,2048]{1,0:T(8,128)(2,1)S(1)}, bf16[40,2048]{1,0:T(8,128)(2,1)S(1)}, u32[]{:S(2)}, u32[]{:S(2)}) collective-permute-start(bf16[40,2048]{1,0:T(8,128)(2,1)S(1)} %get-tuple-element.68), channel_id=1, source_target_pairs={{0,2},{2,0},{4,6},{6,4},{1,3},{3,1},{5,7},{7,5},{8,10},{10,8},{12,... | collective-permute-start | bytes 491528 | tf_op jit(solution)/shard_map/ppermute | solution.py:203
  93.7 11.9 %collective-permute-start.33 = (bf16[40,2048]{1,0:T(8,128)(2,1)S(1)}, bf16[40,2048]{1,0:T(8,128)(2,1)S(1)}, u32[]{:S(2)}, u32[]{:S(2)}) collective-permute-start(bf16[40,2048]{1,0:T(8,128)(2,1)S(1)} %get-tuple-element.69), channel_id=1, source_target_pairs={{0,4},{2,6},{4,0},{6,2},{1,5},{3,7},{5,1},{7,3},{8,12},{10,14},{12... | collective-permute-start | bytes 491528 | tf_op jit(solution)/shard_map/ppermute | solution.py:203
  94.2 12.9 %collective-permute-start.34 = (bf16[40,2048]{1,0:T(8,128)(2,1)S(1)}, bf16[40,2048]{1,0:T(8,128)(2,1)S(1)}, u32[]{:S(2)}, u32[]{:S(2)}) collective-permute-start(bf16[40,2048]{1,0:T(8,128)(2,1)S(1)} %get-tuple-element.70), channel_id=1, source_target_pairs={{0,6},{2,4},{4,2},{6,0},{1,7},{3,5},{5,3},{7,1},{8,14},{10,12},{12... | collective-permute-start | bytes 491528 | tf_op jit(solution)/shard_map/ppermute | solution.py:203
  96.8 11.5 %collective-permute-start.23 = (bf16[40,2048]{1,0:T(8,128)(2,1)S(1)}, bf16[40,2048]{1,0:T(8,128)(2,1)S(1)}, u32[]{:S(2)}, u32[]{:S(2)}) collective-permute-start(bf16[40,2048]{1,0:T(8,128)(2,1)S(1)} %get-tuple-element.60), channel_id=1, source_target_pairs={{0,2},{2,0},{4,6},{6,4},{1,3},{3,1},{5,7},{7,5},{8,10},{10,8},{12,... | collective-permute-start | bytes 491528 | tf_op jit(solution)/shard_map/ppermute | solution.py:203
  102.0 13.0 %collective-permute-start.24 = (bf16[40,2048]{1,0:T(8,128)(2,1)S(1)}, bf16[40,2048]{1,0:T(8,128)(2,1)S(1)}, u32[]{:S(2)}, u32[]{:S(2)}) collective-permute-start(bf16[40,2048]{1,0:T(8,128)(2,1)S(1)} %get-tuple-element.61), channel_id=1, source_target_pairs={{0,4},{2,6},{4,0},{6,2},{1,5},{3,7},{5,1},{7,3},{8,12},{10,14},{12... | collective-permute-start | bytes 491528 | tf_op jit(solution)/shard_map/ppermute | solution.py:203
  102.5 14.3 %collective-permute-start.25 = (bf16[40,2048]{1,0:T(8,128)(2,1)S(1)}, bf16[40,2048]{1,0:T(8,128)(2,1)S(1)}, u32[]{:S(2)}, u32[]{:S(2)}) collective-permute-start(bf16[40,2048]{1,0:T(8,128)(2,1)S(1)} %get-tuple-element.62), channel_id=1, source_target_pairs={{0,6},{2,4},{4,2},{6,0},{1,7},{3,5},{5,3},{7,1},{8,14},{10,12},{12... | collective-permute-start | bytes 491528 | tf_op jit(solution)/shard_map/ppermute | solution.py:203
  105.6 14.6 %collective-permute-start.14 = (bf16[40,2048]{1,0:T(8,128)(2,1)S(1)}, bf16[40,2048]{1,0:T(8,128)(2,1)S(1)}, u32[]{:S(2)}, u32[]{:S(2)}) collective-permute-start(bf16[40,2048]{1,0:T(8,128)(2,1)S(1)} %get-tuple-element.52), channel_id=1, source_target_pairs={{0,2},{2,0},{4,6},{6,4},{1,3},{3,1},{5,7},{7,5},{8,10},{10,8},{12,... | collective-permute-start | bytes 491528 | tf_op jit(solution)/shard_map/ppermute | solution.py:203
  107.0 13.2 %collective-permute-start.15 = (bf16[40,2048]{1,0:T(8,128)(2,1)S(1)}, bf16[40,2048]{1,0:T(8,128)(2,1)S(1)}, u32[]{:S(2)}, u32[]{:S(2)}) collective-permute-start(bf16[40,2048]{1,0:T(8,128)(2,1)S(1)} %get-tuple-element.53), channel_id=1, source_target_pairs={{0,4},{2,6},{4,0},{6,2},{1,5},{3,7},{5,1},{7,3},{8,12},{10,14},{12... | collective-permute-start | bytes 491528 | tf_op jit(solution)/shard_map/ppermute | solution.py:203
  108.3 12.0 %collective-permute-start.16 = (bf16[40,2048]{1,0:T(8,128)(2,1)S(1)}, bf16[40,2048]{1,0:T(8,128)(2,1)S(1)}, u32[]{:S(2)}, u32[]{:S(2)}) collective-permute-start(bf16[40,2048]{1,0:T(8,128)(2,1)S(1)} %get-tuple-element.54), channel_id=1, source_target_pairs={{0,6},{2,4},{4,2},{6,0},{1,7},{3,5},{5,3},{7,1},{8,14},{10,12},{12... | collective-permute-start | bytes 491528 | tf_op jit(solution)/shard_map/ppermute | solution.py:203
  115.0 9.3 %collective-permute-start.6 = (bf16[40,2048]{1,0:T(8,128)(2,1)S(1)}, bf16[40,2048]{1,0:T(8,128)(2,1)S(1)}, u32[]{:S(2)}, u32[]{:S(2)}) collective-permute-start(bf16[40,2048]{1,0:T(8,128)(2,1)S(1)} %get-tuple-element.43), channel_id=1, source_target_pairs={{0,2},{2,0},{4,6},{6,4},{1,3},{3,1},{5,7},{7,5},{8,10},{10,8},{12,... | collective-permute-start | bytes 491528 | tf_op jit(solution)/shard_map/ppermute | solution.py:203
  116.8 13.8 %collective-permute-start.35 = (bf16[64,2048]{1,0:T(8,128)(2,1)S(1)}, bf16[64,2048]{1,0:T(8,128)(2,1)S(1)}, u32[]{:S(2)}, u32[]{:S(2)}) collective-permute-start(bf16[64,2048]{1,0:T(8,128)(2,1)S(1)} %combine.5), channel_id=1, source_target_pairs={{0,24},{8,16},{16,8},{24,0},{1,25},{9,17},{17,9},{25,1},{2,26},{10... | collective-permute-start | bytes 786440 | tf_op jit(solution)/shard_map/ppermute | solution.py:203
  120.2 10.5 %collective-permute-start.26 = (bf16[64,2048]{1,0:T(8,128)(2,1)S(1)}, bf16[64,2048]{1,0:T(8,128)(2,1)S(1)}, u32[]{:S(2)}, u32[]{:S(2)}) collective-permute-start(bf16[64,2048]{1,0:T(8,128)(2,1)S(1)} %combine.4), channel_id=1, source_target_pairs={{0,16},{8,24},{16,0},{24,8},{1,17},{9,25},{17,1},{25,9},{2,18},{10... | collective-permute-start | bytes 786440 | tf_op jit(solution)/shard_map/ppermute | solution.py:203
  121.3 9.4 %collective-permute-start.17 = (bf16[64,2048]{1,0:T(8,128)(2,1)S(1)}, bf16[64,2048]{1,0:T(8,128)(2,1)S(1)}, u32[]{:S(2)}, u32[]{:S(2)}) collective-permute-start(bf16[64,2048]{1,0:T(8,128)(2,1)S(1)} %combine.3), channel_id=1, source_target_pairs={{0,8},{8,0},{16,24},{24,16},{1,9},{9,1},{17,25},{25,17},{2,10},{10... | collective-permute-start | bytes 786440 | tf_op jit(solution)/shard_map/ppermute | solution.py:203
  (12 other events, 226.3 us)

commit v2 on v1

--- a/solution.py
+++ b/solution.py
@@ -40,7 +40,27 @@
     return gate_at, hit
 
 
-def gather_rows(rows, weights, base, mine, chips, capacity, outs):
+def routing(ids, gates, experts):
+    top_k, tokens = ids.shape
+    expert_at = lax.broadcasted_iota(jnp.int32, (experts, tokens), 0)
+    found = jnp.zeros((experts, tokens), jnp.float32)
+    for k in range(top_k):
+        found = jnp.where(ids[k : k + 1, :] == expert_at, gates[k : k + 1, :], found)
+    return found.T
+
+
+def position(chips):
+    return lax.axis_index("req") * chips, lax.axis_index("chip")
+
+
+def unpacked(payload, features, experts):
+    high = payload[:, features : features + experts].astype(jnp.float32)
+    low = payload[:, features + experts : features + 2 * experts].astype(jnp.float32)
+    return high + low
+
+
+def gather_rows(rows, weights, chips, capacity, outs):
+    base, mine = position(chips)
     _, hit = slot_weights(weights, base, mine, chips, capacity)
     picked = lax.dot_general(
         hit.astype(jnp.bfloat16), rows, (((0,), (0,)), ((), ())), preferred_element_type=jnp.float32
@@ -62,7 +82,8 @@
     return jnp.concatenate([ref[...].astype(jnp.float32) for ref in refs], axis=0).astype(jnp.bfloat16)
 
 
-def combined(refs, weights, base, mine, chips, capacity):
+def combined(refs, weights, chips, capacity):
+    base, mine = position(chips)
     gate_at, _ = slot_weights(weights, base, mine, chips, capacity)
     high = gate_at.astype(jnp.bfloat16)
     low = (gate_at - high.astype(jnp.float32)).astype(jnp.bfloat16)
@@ -72,8 +93,8 @@
 
 
 def attention_kernel(
-    chips, capacity, place, length, queries, new_kv, cache, residual, out_weight, gain, weights,
-    stream, normed, appended, *rest,
+    chips, capacity, experts, length, queries, new_kv, cache, residual, out_weight, gain, ids, gates,
+    stream, payload, appended, *rest,
 ):
     outs, scratch = rest[:-9], rest[-9:]
     cached, newest, queried, resid, projection, keys, values, mixed, sems = scratch
@@ -139,13 +160,21 @@
     stream[...] = total
     mean_square = jnp.mean(total * total, axis=-1, keepdims=True)
     rows = (total * lax.rsqrt(mean_square + 1e-06) * gain[...]).astype(jnp.bfloat16)
-    normed[...] = rows
-    gather_rows(rows, weights[...], place[0], place[1], chips, capacity, outs)
+    features = rows.shape[1]
+    weights = routing(ids[...], gates[...], experts)
+    high = weights.astype(jnp.bfloat16)
+    low = (weights - high.astype(jnp.float32)).astype(jnp.bfloat16)
+    spare = payload.shape[1] - features - 2 * experts
+    trail = [high, low] + ([jnp.zeros((rows.shape[0], spare), jnp.bfloat16)] if spare else [])
+    payload[:, :features] = rows
+    payload[:, features:] = jnp.concatenate(trail, axis=1)
+    gather_rows(rows, weights, chips, capacity, outs)
     store_new.wait()
 
 
-def gather_kernel(chips, capacity, place, rows, weights, *outs):
-    gather_rows(rows[...], weights[...], place[0], place[1], chips, capacity, outs)
+def gather_kernel(chips, capacity, experts, features, payload, *outs):
+    weights = unpacked(payload, features, experts)
+    gather_rows(payload[:, :features], weights, chips, capacity, outs)
 
 
 def expert_kernel(capacity, counts, *refs):
@@ -161,12 +190,14 @@
     scatter_out(total, capacity, outs)
 
 
-def combine_kernel(chips, capacity, place, weights, *refs):
-    refs[-1][...] = combined(refs[:-1], weights[...], place[0], place[1], chips, capacity).astype(jnp.bfloat16)
-
-
-def final_kernel(chips, capacity, counts, place, weights, stream, *refs):
-    total = combined(refs[:counts], weights[...], place[0], place[1], chips, capacity)
+def combine_kernel(chips, capacity, experts, features, payload, *refs):
+    weights = unpacked(payload, features, experts)
+    refs[-1][...] = combined(refs[:-1], weights, chips, capacity).astype(jnp.bfloat16)
+
+
+def final_kernel(chips, capacity, experts, features, counts, payload, stream, *refs):
+    weights = unpacked(payload, features, experts)
+    total = combined(refs[:counts], weights, chips, capacity)
     for ref in refs[counts:-1]:
         total = total + ref[...].astype(jnp.float32)
     refs[-1][...] = (stream[...] + total).astype(jnp.bfloat16)
@@ -177,15 +208,13 @@
 
 
 SMEM_SPEC = pl.BlockSpec(memory_space=pltpu.SMEM)
-ANY_SPEC = pl.BlockSpec(memory_space=pl.ANY)
+HBM_SPEC = pl.BlockSpec(memory_space=pltpu.HBM)
 
 
 def shards(
     queries, new_kv, cache, lengths, residual, out_weight, norm_gain, expert_ids, gates, w_gate, w_up, w_down,
 ):
     planes, chips, cores = (lax.axis_size(axis) for axis in ALL)
-    mine = lax.axis_index("chip")
-    base = lax.axis_index("req") * chips
     experts = planes * chips
     group, features = queries.shape[1:]
     slots = cache.shape[1]
@@ -193,7 +222,7 @@
     capacity = 5 * group * top_k // (4 * experts)
     tiled = capacity % 8 == 0
     bf16 = jnp.bfloat16
-    place = jnp.stack([base, mine]).astype(jnp.int32)
+    width = features + -(-2 * experts // 128) * 128
 
     def params(mib):
         return pltpu.CompilerParams(vmem_limit_bytes=mib << 20)
@@ -219,25 +248,18 @@
 
     own_halves = [w_gate[0], w_up[0], w_down[0]]
     other_halves = [across(half, "core", 1) for half in own_halves]
-
-    weights = jnp.sum(
-        jnp.where(
-            expert_ids[0][:, :, None] == jnp.arange(experts, dtype=jnp.int32), gates[0][:, :, None], 0.0
-        ),
-        axis=1,
-    )
-    weights_of = [weights] + [across(weights, "req", s) for s in range(1, planes)]
-
-    stream, normed, appended, *outgoing = pl.pallas_call(
-        functools.partial(attention_kernel, chips, capacity),
+    halves = [pltpu.with_memory_space_constraint(half, VMEM) for half in own_halves + other_halves]
+
+    stream, payload, appended, *outgoing = pl.pallas_call(
+        functools.partial(attention_kernel, chips, capacity, experts),
         out_shape=[
             jax.ShapeDtypeStruct((group, features), jnp.float32),
-            jax.ShapeDtypeStruct((group, features), bf16),
+            jax.ShapeDtypeStruct((group, width), bf16),
             jax.ShapeDtypeStruct(cache.shape[1:], cache.dtype),
         ]
         + block_shapes,
-        in_specs=[SMEM_SPEC, SMEM_SPEC] + [ANY_SPEC] * 5 + in_vmem(2),
-        out_specs=in_vmem(2) + [ANY_SPEC] + in_vmem(blocks_n),
+        in_specs=[SMEM_SPEC] + [HBM_SPEC] * 5 + in_vmem(3),
+        out_specs=in_vmem(2) + [HBM_SPEC] + in_vmem(blocks_n),
         scratch_shapes=[
             VMEM(cache.shape[1:], bf16),
             VMEM(new_kv.shape[1:], bf16),
@@ -249,57 +271,69 @@
             VMEM((group, features), bf16),
             pltpu.SemaphoreType.DMA((9,)),
         ],
-        compiler_params=params(40),
+        compiler_params=params(24),
+        cost_estimate=pl.CostEstimate(
+            flops=12_000_000_000, bytes_accessed=24 * features * features // 4, transcendentals=0
+        ),
         name="attention",
-    )(place, lengths, queries[0], new_kv[0], cache[0], residual[0], out_weight, norm_gain[None], weights)
-
-    rows_of = [normed] + [across(normed, "req", s) for s in range(1, planes)]
+    )(
+        lengths,
+        *[
+            pltpu.with_memory_space_constraint(x, pltpu.HBM)
+            for x in (queries[0], new_kv[0], cache[0], residual[0], out_weight)
+        ],
+        norm_gain[None],
+        expert_ids[0].T,
+        gates[0].T,
+    )
+
+    payload_of = [payload] + [across(payload, "req", s) for s in range(1, planes)]
     partials = []
     for s in range(planes):
         if s > 0:
             outgoing = pl.pallas_call(
-                functools.partial(gather_kernel, chips, capacity),
+                functools.partial(gather_kernel, chips, capacity, experts, features),
                 out_shape=block_shapes,
-                in_specs=[SMEM_SPEC] + in_vmem(2),
+                in_specs=in_vmem(1),
                 out_specs=in_vmem(blocks_n),
-                compiler_params=params(16),
+                compiler_params=params(8),
                 name="gather",
-            )(place, rows_of[s], weights_of[s])
+            )(payload_of[s])
         arrived = joined(to_chips(cut(outgoing)))
         results = pl.pallas_call(
             functools.partial(expert_kernel, capacity, blocks_n),
             out_shape=block_shapes,
             in_specs=in_vmem(blocks_n + 6),
             out_specs=in_vmem(blocks_n),
-            compiler_params=params(24),
+            compiler_params=params(8),
             cost_estimate=pl.CostEstimate(
                 flops=12 * chips * capacity * features * w_gate.shape[2],
                 bytes_accessed=12 * features * w_gate.shape[2],
                 transcendentals=0,
             ),
             name="experts",
-        )(*arrived, *own_halves, *other_halves)
+        )(*arrived, *halves)
         returned = joined(to_chips(cut(results)))
         if s == 0:
             own_returned = returned
         else:
             partial = pl.pallas_call(
-                functools.partial(combine_kernel, chips, capacity),
+                functools.partial(combine_kernel, chips, capacity, experts, features),
                 out_shape=jax.ShapeDtypeStruct((group, features), bf16),
-                in_specs=[SMEM_SPEC] + in_vmem(1 + blocks_n),
+                in_specs=in_vmem(1 + blocks_n),
                 out_specs=pl.BlockSpec(memory_space=VMEM),
-                compiler_params=params(16),
+                compiler_params=params(8),
                 name="combine",
-            )(place, weights_of[s], *returned)
+            )(payload_of[s], *returned)
             partials.append(across(partial, "req", s))
     layer_out = pl.pallas_call(
-        functools.partial(final_kernel, chips, capacity, blocks_n),
+        functools.partial(final_kernel, chips, capacity, experts, features, blocks_n),
         out_shape=jax.ShapeDtypeStruct((group, features), bf16),
-        in_specs=[SMEM_SPEC] + in_vmem(2 + blocks_n + len(partials)),
+        in_specs=in_vmem(2 + blocks_n + len(partials)),
         out_specs=pl.BlockSpec(memory_space=VMEM),
-        compiler_params=params(16),
+        compiler_params=params(8),
         name="final",
-    )(place, weights, stream, *own_returned, *partials)
+    )(payload, stream, *own_returned, *partials)
     return (layer_out[None], appended[None])
 
 

time: 133 us -> 121 us (0.910)
  Pallas kernels: 36.7 us -> 25.3 us
  waiting for transfers between devices: 34.2 us -> 39.5 us
  local copies, waits for them, and re-layouts: 5.92 us -> 2.07 us
    pallas_call x4, Pallas kernels: 18.4 us -> 9.42 us  [shards(): pl.pallas_call(functools.partial(expert_kernel, capacity, blocks_n), out_...]
    ppermute x36 -> x33, waiting for transfers between devices: 34.2 us -> 39.5 us  [across(): return lax.ppermute(x, axis, [(i, i ^ j) for i in range(size)])]
    unnamed x16 -> x12, local copies, waits for them, and re-layouts: 5.84 us -> 2.07 us
    pallas_call x8, Pallas kernels: 18.3 us -> 15.8 us  [the longest x1 10.8 us: shards(): pl.pallas_call(functools.partial(attention_kernel, chips, capacity, exper...]
    ppermute x36 -> x33, starting transfers between devices: 53.3 us -> 52.9 us  [across(): return lax.ppermute(x, axis, [(i, i ^ j) for i in range(size)])]
  transfers between devices with their start and end apart: 36 -> 33, of which waited for: 10 -> 11; matrix products, arithmetic and copies ran while one was open for 1% -> 0% of each run, Pallas kernels for 26% -> 20%
where the time goes in v2:
time: 121 us
  starting transfers between devices  52.9 us (44%)
  waiting for transfers between devices  39.5 us (33%)
  Pallas kernels  25.3 us (21%)
  local copies, waits for them, and re-layouts  2.07 us (2%)
  between operations  1.49 us (1%)
    ppermute x33, starting transfers between devices, across(): return lax.ppermute(x, axis, [(i, i ^ j) for i in range(size)])  52.9 us
    ppermute x33, waiting for transfers between devices, across(): return lax.ppermute(x, axis, [(i, i ^ j) for i in range(size)])  39.5 us
    pallas_call x1, Pallas kernels, shards(): pl.pallas_call(functools.partial(attention_kernel, chips, capacity, exper...  10.8 us
    pallas_call x4, Pallas kernels, shards(): pl.pallas_call(functools.partial(expert_kernel, capacity, blocks_n), out_...  9.42 us
  transfers between devices with their start and end apart: 33, of which 11 were waited for; matrix products, arithmetic and copies ran while one was open for 0% of the time, Pallas kernels for 20%

profile of v2, /device:TPU:0, one launch (start us, length us, event | category | flops | bytes accessed | tf_op | source)
XLA Modules:
  0.0 121.2 jit_solution(5350529977347184138)
XLA Ops:
  4.4 10.8 %attention.1 = (f32[64,2048]{1,0:T(8,128)S(1)}, bf16[64,2176]{1,0:T(8,128)(2,1)S(1)}, bf16[512,2,2048]{2,1,0:T(2,128)(2,1)}, bf16[40,2048]{1,0:T(8,128)(2,1)S(1)...) custom-call(s32[1]{0:T(128)S(6)} %copy.14.length, ...), custom_call_target="tpu_custom_call" | custom-call | flops 12000000000 | bytes 25165824 | tf_op jit(solution)/shard_map/attention/pallas_call | solution.py:253
  15.2 4.7 %collective-permute-start.25 = (bf16[64,2176]{1,0:T(8,128)(2,1)S(1)}, bf16[64,2176]{1,0:T(8,128)(2,1)S(1)}, u32[]{:S(2)}, u32[]{:S(2)}) collective-permute-start(bf16[64,2176]{1,0:T(8,128)(2,1)S(1)} %get-tuple-element.37.payload), channel_id=1, source_target_pairs={{0,24},{8,16},{16,8},{24,0},{1,25},{9,17},{17,9},{25,1},{2,26},{10... | collective-permute-start | bytes 835592 | tf_op jit(solution)/shard_map/ppermute | solution.py:232
  19.9 7.6 %collective-permute-done.25.payload = bf16[64,2176]{1,0:T(8,128)(2,1)S(1)} collective-permute-done((bf16[64,2176]{1,0:T(8,128)(2,1)S(1)}, bf16[64,2176]{1,0:T(8,128)(2,1)S(1)}, u32[]{:S(2)}, u32[]{:S(2)}) %collective-permute-start.25) | collective-permute-done | bytes 278560 | tf_op jit(solution)/shard_map/ppermute | solution.py:232
  27.5 11.8 %collective-permute-start.9 = (bf16[64,2176]{1,0:T(8,128)(2,1)S(1)}, bf16[64,2176]{1,0:T(8,128)(2,1)S(1)}, u32[]{:S(2)}, u32[]{:S(2)}) collective-permute-start(bf16[64,2176]{1,0:T(8,128)(2,1)S(1)} %get-tuple-element.37.payload), channel_id=1, source_target_pairs={{0,8},{8,0},{16,24},{24,16},{1,9},{9,1},{17,25},{25,17},{2,10},{10... | collective-permute-start | bytes 835592 | tf_op jit(solution)/shard_map/ppermute | solution.py:232
  39.9 4.4 %collective-permute-done.17.payload = bf16[64,2176]{1,0:T(8,128)(2,1)S(1)} collective-permute-done((bf16[64,2176]{1,0:T(8,128)(2,1)S(1)}, bf16[64,2176]{1,0:T(8,128)(2,1)S(1)}, u32[]{:S(2)}, u32[]{:S(2)}) %collective-permute-start.17) | collective-permute-done | bytes 278560 | tf_op jit(solution)/shard_map/ppermute | solution.py:232
  44.3 1.5 %collective-permute-start.26 = (bf16[40,2048]{1,0:T(8,128)(2,1)S(1)}, bf16[40,2048]{1,0:T(8,128)(2,1)S(1)}, u32[]{:S(2)}, u32[]{:S(2)}) collective-permute-start(bf16[40,2048]{1,0:T(8,128)(2,1)S(1)} %get-tuple-element.64), channel_id=1, source_target_pairs={{0,2},{2,0},{4,6},{6,4},{1,3},{3,1},{5,7},{7,5},{8,10},{10,8},{12,... | collective-permute-start | bytes 491528 | tf_op jit(solution)/shard_map/ppermute | solution.py:232
  45.8 4.4 %collective-permute-done.9.payload = bf16[64,2176]{1,0:T(8,128)(2,1)S(1)} collective-permute-done((bf16[64,2176]{1,0:T(8,128)(2,1)S(1)}, bf16[64,2176]{1,0:T(8,128)(2,1)S(1)}, u32[]{:S(2)}, u32[]{:S(2)}) %collective-permute-start.9) | collective-permute-done | bytes 278560 | tf_op jit(solution)/shard_map/ppermute | solution.py:232
  50.2 1.5 %collective-permute-start.27 = (bf16[40,2048]{1,0:T(8,128)(2,1)S(1)}, bf16[40,2048]{1,0:T(8,128)(2,1)S(1)}, u32[]{:S(2)}, u32[]{:S(2)}) collective-permute-start(bf16[40,2048]{1,0:T(8,128)(2,1)S(1)} %get-tuple-element.65), channel_id=1, source_target_pairs={{0,4},{2,6},{4,0},{6,2},{1,5},{3,7},{5,1},{7,3},{8,12},{10,14},{12... | collective-permute-start | bytes 491528 | tf_op jit(solution)/shard_map/ppermute | solution.py:232
  51.7 1.4 %collective-permute-start.28 = (bf16[40,2048]{1,0:T(8,128)(2,1)S(1)}, bf16[40,2048]{1,0:T(8,128)(2,1)S(1)}, u32[]{:S(2)}, u32[]{:S(2)}) collective-permute-start(bf16[40,2048]{1,0:T(8,128)(2,1)S(1)} %get-tuple-element.66), channel_id=1, source_target_pairs={{0,6},{2,4},{4,2},{6,0},{1,7},{3,5},{5,3},{7,1},{8,14},{10,12},{12... | collective-permute-start | bytes 491528 | tf_op jit(solution)/shard_map/ppermute | solution.py:232
  54.5 5.3 %collective-permute-done.27.refs_2_ = bf16[40,2048]{1,0:T(8,128)(2,1)S(1)} collective-permute-done((bf16[40,2048]{1,0:T(8,128)(2,1)S(1)}, bf16[40,2048]{1,0:T(8,128)(2,1)S(1)}, u32[]{:S(2)}, u32[]{:S(2)}) %collective-permute-start.27) | collective-permute-done | bytes 163872 | tf_op jit(solution)/shard_map/ppermute | solution.py:232
  59.8 1.5 %collective-permute-start = (bf16[40,2048]{1,0:T(8,128)(2,1)S(1)}, bf16[40,2048]{1,0:T(8,128)(2,1)S(1)}, u32[]{:S(2)}, u32[]{:S(2)}) collective-permute-start(bf16[40,2048]{1,0:T(8,128)(2,1)S(1)} %get-tuple-element.40), channel_id=1, source_target_pairs={{0,2},{2,0},{4,6},{6,4},{1,3},{3,1},{5,7},{7,5},{8,10},{10,8},{12,... | collective-permute-start | bytes 491528 | tf_op jit(solution)/shard_map/ppermute | solution.py:232
  61.3 1.5 %collective-permute-start.1 = (bf16[40,2048]{1,0:T(8,128)(2,1)S(1)}, bf16[40,2048]{1,0:T(8,128)(2,1)S(1)}, u32[]{:S(2)}, u32[]{:S(2)}) collective-permute-start(bf16[40,2048]{1,0:T(8,128)(2,1)S(1)} %get-tuple-element.41), channel_id=1, source_target_pairs={{0,4},{2,6},{4,0},{6,2},{1,5},{3,7},{5,1},{7,3},{8,12},{10,14},{12... | collective-permute-start | bytes 491528 | tf_op jit(solution)/shard_map/ppermute | solution.py:232
  63.9 2.5 %collective-permute-start.20 = (bf16[40,2048]{1,0:T(8,128)(2,1)S(1)}, bf16[40,2048]{1,0:T(8,128)(2,1)S(1)}, u32[]{:S(2)}, u32[]{:S(2)}) collective-permute-start(bf16[40,2048]{1,0:T(8,128)(2,1)S(1)} %get-tuple-element.58), channel_id=1, source_target_pairs={{0,6},{2,4},{4,2},{6,0},{1,7},{3,5},{5,3},{7,1},{8,14},{10,12},{12... | collective-permute-start | bytes 491528 | tf_op jit(solution)/shard_map/ppermute | solution.py:232
  66.4 2.3 %experts.7 = (bf16[40,2048]{1,0:T(8,128)(2,1)S(1)}, bf16[40,2048]{1,0:T(8,128)(2,1)S(1)}, bf16[40,2048]{1,0:T(8,128)(2,1)S(1)}, bf16[40,2048]{1,0:T(8,128)(2,1)S(1)}) custom-call(bf16[40,2048]{1,0:T(8,128)(2,1)S(1)} %get-tuple-element.63.refs_0_, bf16[40,2048]{1,0:T(8,128)(2,1)S(1)} %collective-permute-done.26.refs_1_, ...), custom_call_target="tpu_custom_call" | custom-call | flops 2013265920 | bytes 12582912 | tf_op jit(solution)/shard_map/experts/pallas_call | solution.py:303
  70.0 2.0 %collective-permute-start.10 = (bf16[40,2048]{1,0:T(8,128)(2,1)S(1)}, bf16[40,2048]{1,0:T(8,128)(2,1)S(1)}, u32[]{:S(2)}, u32[]{:S(2)}) collective-permute-start(bf16[40,2048]{1,0:T(8,128)(2,1)S(1)} %get-tuple-element.48), channel_id=1, source_target_pairs={{0,2},{2,0},{4,6},{6,4},{1,3},{3,1},{5,7},{7,5},{8,10},{10,8},{12,... | collective-permute-start | bytes 491528 | tf_op jit(solution)/shard_map/ppermute | solution.py:232
  72.0 1.5 %collective-permute-done.19.refs_2_ = bf16[40,2048]{1,0:T(8,128)(2,1)S(1)} collective-permute-done((bf16[40,2048]{1,0:T(8,128)(2,1)S(1)}, bf16[40,2048]{1,0:T(8,128)(2,1)S(1)}, u32[]{:S(2)}, u32[]{:S(2)}) %collective-permute-start.19) | collective-permute-done | bytes 163872 | tf_op jit(solution)/shard_map/ppermute | solution.py:232
  73.5 2.5 %collective-permute-start.11 = (bf16[40,2048]{1,0:T(8,128)(2,1)S(1)}, bf16[40,2048]{1,0:T(8,128)(2,1)S(1)}, u32[]{:S(2)}, u32[]{:S(2)}) collective-permute-start(bf16[40,2048]{1,0:T(8,128)(2,1)S(1)} %get-tuple-element.49), channel_id=1, source_target_pairs={{0,4},{2,6},{4,0},{6,2},{1,5},{3,7},{5,1},{7,3},{8,12},{10,14},{12... | collective-permute-start | bytes 491528 | tf_op jit(solution)/shard_map/ppermute | solution.py:232
  76.5 2.3 %experts.6 = (bf16[40,2048]{1,0:T(8,128)(2,1)S(1)}, bf16[40,2048]{1,0:T(8,128)(2,1)S(1)}, bf16[40,2048]{1,0:T(8,128)(2,1)S(1)}, bf16[40,2048]{1,0:T(8,128)(2,1)S(1)}) custom-call(bf16[40,2048]{1,0:T(8,128)(2,1)S(1)} %get-tuple-element.55.refs_0_, bf16[40,2048]{1,0:T(8,128)(2,1)S(1)} %collective-permute-done.18.refs_1_, ...), custom_call_target="tpu_custom_call" | custom-call | flops 2013265920 | bytes 12582912 | tf_op jit(solution)/shard_map/experts/pallas_call | solution.py:303
  78.8 2.5 %collective-permute-start.2 = (bf16[40,2048]{1,0:T(8,128)(2,1)S(1)}, bf16[40,2048]{1,0:T(8,128)(2,1)S(1)}, u32[]{:S(2)}, u32[]{:S(2)}) collective-permute-start(bf16[40,2048]{1,0:T(8,128)(2,1)S(1)} %get-tuple-element.42), channel_id=1, source_target_pairs={{0,6},{2,4},{4,2},{6,0},{1,7},{3,5},{5,3},{7,1},{8,14},{10,12},{12... | collective-permute-start | bytes 491528 | tf_op jit(solution)/shard_map/ppermute | solution.py:232
  82.4 5.3 %collective-permute-done.11.refs_2_ = bf16[40,2048]{1,0:T(8,128)(2,1)S(1)} collective-permute-done((bf16[40,2048]{1,0:T(8,128)(2,1)S(1)}, bf16[40,2048]{1,0:T(8,128)(2,1)S(1)}, u32[]{:S(2)}, u32[]{:S(2)}) %collective-permute-start.11) | collective-permute-done | bytes 163872 | tf_op jit(solution)/shard_map/ppermute | solution.py:232
  87.7 3.6 %collective-permute-start.21 = (bf16[40,2048]{1,0:T(8,128)(2,1)S(1)}, bf16[40,2048]{1,0:T(8,128)(2,1)S(1)}, u32[]{:S(2)}, u32[]{:S(2)}) collective-permute-start(bf16[40,2048]{1,0:T(8,128)(2,1)S(1)} %get-tuple-element.60), channel_id=1, source_target_pairs={{0,2},{2,0},{4,6},{6,4},{1,3},{3,1},{5,7},{7,5},{8,10},{10,8},{12,... | collective-permute-start | bytes 491528 | tf_op jit(solution)/shard_map/ppermute | solution.py:232
  91.3 2.5 %experts.5 = (bf16[40,2048]{1,0:T(8,128)(2,1)S(1)}, bf16[40,2048]{1,0:T(8,128)(2,1)S(1)}, bf16[40,2048]{1,0:T(8,128)(2,1)S(1)}, bf16[40,2048]{1,0:T(8,128)(2,1)S(1)}) custom-call(bf16[40,2048]{1,0:T(8,128)(2,1)S(1)} %get-tuple-element.47.refs_0_, bf16[40,2048]{1,0:T(8,128)(2,1)S(1)} %collective-permute-done.10.refs_1_, ...), custom_call_target="tpu_custom_call" | custom-call | flops 2013265920 | bytes 12582912 | tf_op jit(solution)/shard_map/experts/pallas_call | solution.py:303
  93.9 1.4 %collective-permute-start.23 = (bf16[40,2048]{1,0:T(8,128)(2,1)S(1)}, bf16[40,2048]{1,0:T(8,128)(2,1)S(1)}, u32[]{:S(2)}, u32[]{:S(2)}) collective-permute-start(bf16[40,2048]{1,0:T(8,128)(2,1)S(1)} %get-tuple-element.62), channel_id=1, source_target_pairs={{0,6},{2,4},{4,2},{6,0},{1,7},{3,5},{5,3},{7,1},{8,14},{10,12},{12... | collective-permute-start | bytes 491528 | tf_op jit(solution)/shard_map/ppermute | solution.py:232
  95.4 2.0 %collective-permute-start.13 = (bf16[40,2048]{1,0:T(8,128)(2,1)S(1)}, bf16[40,2048]{1,0:T(8,128)(2,1)S(1)}, u32[]{:S(2)}, u32[]{:S(2)}) collective-permute-start(bf16[40,2048]{1,0:T(8,128)(2,1)S(1)} %get-tuple-element.52), channel_id=1, source_target_pairs={{0,2},{2,0},{4,6},{6,4},{1,3},{3,1},{5,7},{7,5},{8,10},{10,8},{12,... | collective-permute-start | bytes 491528 | tf_op jit(solution)/shard_map/ppermute | solution.py:232
  98.0 2.0 %collective-permute-done.21.refs_1_ = bf16[40,2048]{1,0:T(8,128)(2,1)S(1)} collective-permute-done((bf16[40,2048]{1,0:T(8,128)(2,1)S(1)}, bf16[40,2048]{1,0:T(8,128)(2,1)S(1)}, u32[]{:S(2)}, u32[]{:S(2)}) %collective-permute-start.21) | collective-permute-done | bytes 163872 | tf_op jit(solution)/shard_map/ppermute | solution.py:232
  100.0 2.3 %experts.4 = (bf16[40,2048]{1,0:T(8,128)(2,1)S(1)}, bf16[40,2048]{1,0:T(8,128)(2,1)S(1)}, bf16[40,2048]{1,0:T(8,128)(2,1)S(1)}, bf16[40,2048]{1,0:T(8,128)(2,1)S(1)}) custom-call(bf16[40,2048]{1,0:T(8,128)(2,1)S(1)} %get-tuple-element.39.refs_0_, bf16[40,2048]{1,0:T(8,128)(2,1)S(1)} %collective-permute-done.refs_1_, ...), custom_call_target="tpu_custom_call" | custom-call | flops 2013265920 | bytes 12582912 | tf_op jit(solution)/shard_map/experts/pallas_call | solution.py:303
  104.3 2.5 %collective-permute-start.32 = (bf16[64,2048]{1,0:T(8,128)(2,1)S(1)}, bf16[64,2048]{1,0:T(8,128)(2,1)S(1)}, u32[]{:S(2)}, u32[]{:S(2)}) collective-permute-start(bf16[64,2048]{1,0:T(8,128)(2,1)S(1)} %combine.5), channel_id=1, source_target_pairs={{0,24},{8,16},{16,8},{24,0},{1,25},{9,17},{17,9},{25,1},{2,26},{10... | collective-permute-start | bytes 786440 | tf_op jit(solution)/shard_map/ppermute | solution.py:232
  108.1 2.0 %collective-permute-start.16 = (bf16[64,2048]{1,0:T(8,128)(2,1)S(1)}, bf16[64,2048]{1,0:T(8,128)(2,1)S(1)}, u32[]{:S(2)}, u32[]{:S(2)}) collective-permute-start(bf16[64,2048]{1,0:T(8,128)(2,1)S(1)} %combine.3), channel_id=1, source_target_pairs={{0,8},{8,0},{16,24},{24,16},{1,9},{9,1},{17,25},{25,17},{2,10},{10... | collective-permute-start | bytes 786440 | tf_op jit(solution)/shard_map/ppermute | solution.py:232
  110.1 2.2 %collective-permute-start.7 = (bf16[40,2048]{1,0:T(8,128)(2,1)S(1)}, bf16[40,2048]{1,0:T(8,128)(2,1)S(1)}, u32[]{:S(2)}, u32[]{:S(2)}) collective-permute-start(bf16[40,2048]{1,0:T(8,128)(2,1)S(1)} %get-tuple-element.45), channel_id=1, source_target_pairs={{0,4},{2,6},{4,0},{6,2},{1,5},{3,7},{5,1},{7,3},{8,12},{10,14},{12... | collective-permute-start | bytes 491528 | tf_op jit(solution)/shard_map/ppermute | solution.py:232
  112.3 4.6 %collective-permute-done.7.refs_2_ = bf16[40,2048]{1,0:T(8,128)(2,1)S(1)} collective-permute-done((bf16[40,2048]{1,0:T(8,128)(2,1)S(1)}, bf16[40,2048]{1,0:T(8,128)(2,1)S(1)}, u32[]{:S(2)}, u32[]{:S(2)}) %collective-permute-start.7) | collective-permute-done | bytes 163872 | tf_op jit(solution)/shard_map/ppermute | solution.py:232
  116.9 1.6 %collective-permute-done.8.refs_3_ = bf16[40,2048]{1,0:T(8,128)(2,1)S(1)} collective-permute-done((bf16[40,2048]{1,0:T(8,128)(2,1)S(1)}, bf16[40,2048]{1,0:T(8,128)(2,1)S(1)}, u32[]{:S(2)}, u32[]{:S(2)}) %collective-permute-start.8) | collective-permute-done | bytes 163872 | tf_op jit(solution)/shard_map/ppermute | solution.py:232
  118.5 1.4 %collective-permute-done.24.refs_5_ = bf16[64,2048]{1,0:T(8,128)(2,1)S(1)} collective-permute-done((bf16[64,2048]{1,0:T(8,128)(2,1)S(1)}, bf16[64,2048]{1,0:T(8,128)(2,1)S(1)}, u32[]{:S(2)}, u32[]{:S(2)}) %collective-permute-start.24) | collective-permute-done | bytes 262176 | tf_op jit(solution)/shard_map/ppermute | solution.py:232
  (58 shorter events, 14.3 us)
Async XLA Ops:
  0.6 62.2 %collective-permute-start.3 = (bf16[2048,512]{1,0:T(8,128)(2,1)}, bf16[2048,512]{1,0:T(8,128)(2,1)S(1)}, u32[]{:S(2)}, u32[]{:S(2)}) collective-permute-start(bf16[2048,512]{1,0:T(8,128)(2,1)} %bitcast.16), channel_id=1, source_target_pairs={{0,1},{1,0},{2,3},{3,2},{4,5},{5,4},{6,7},{7,6},{8,9},{9,8},{10,11... | collective-permute-start | bytes 6291464 | tf_op jit(solution)/shard_map/ppermute | solution.py:232
  1.2 62.2 %collective-permute-start.4 = (bf16[2048,512]{1,0:T(8,128)(2,1)}, bf16[2048,512]{1,0:T(8,128)(2,1)S(1)}, u32[]{:S(2)}, u32[]{:S(2)}) collective-permute-start(bf16[2048,512]{1,0:T(8,128)(2,1)} %bitcast.21), channel_id=1, source_target_pairs={{0,1},{1,0},{2,3},{3,2},{4,5},{5,4},{6,7},{7,6},{8,9},{9,8},{10,11... | collective-permute-start | bytes 6291464 | tf_op jit(solution)/shard_map/ppermute | solution.py:232
  1.2 62.7 %collective-permute-start.5 = (bf16[512,2048]{1,0:T(8,128)(2,1)}, bf16[512,2048]{1,0:T(8,128)(2,1)S(1)}, u32[]{:S(2)}, u32[]{:S(2)}) collective-permute-start(bf16[512,2048]{1,0:T(8,128)(2,1)} %bitcast.26), channel_id=1, source_target_pairs={{0,1},{1,0},{2,3},{3,2},{4,5},{5,4},{6,7},{7,6},{8,9},{9,8},{10,11... | collective-permute-start | bytes 6291464 | tf_op jit(solution)/shard_map/ppermute | solution.py:232
  15.2 12.3 %collective-permute-start.25 = (bf16[64,2176]{1,0:T(8,128)(2,1)S(1)}, bf16[64,2176]{1,0:T(8,128)(2,1)S(1)}, u32[]{:S(2)}, u32[]{:S(2)}) collective-permute-start(bf16[64,2176]{1,0:T(8,128)(2,1)S(1)} %get-tuple-element.37.payload), channel_id=1, source_target_pairs={{0,24},{8,16},{16,8},{24,0},{1,25},{9,17},{17,9},{25,1},{2,26},{10... | collective-permute-start | bytes 835592 | tf_op jit(solution)/shard_map/ppermute | solution.py:232
  19.9 24.4 %collective-permute-start.17 = (bf16[64,2176]{1,0:T(8,128)(2,1)S(1)}, bf16[64,2176]{1,0:T(8,128)(2,1)S(1)}, u32[]{:S(2)}, u32[]{:S(2)}) collective-permute-start(bf16[64,2176]{1,0:T(8,128)(2,1)S(1)} %get-tuple-element.37.payload), channel_id=1, source_target_pairs={{0,16},{8,24},{16,0},{24,8},{1,17},{9,25},{17,1},{25,9},{2,18},{10... | collective-permute-start | bytes 835592 | tf_op jit(solution)/shard_map/ppermute | solution.py:232
  27.5 22.7 %collective-permute-start.9 = (bf16[64,2176]{1,0:T(8,128)(2,1)S(1)}, bf16[64,2176]{1,0:T(8,128)(2,1)S(1)}, u32[]{:S(2)}, u32[]{:S(2)}) collective-permute-start(bf16[64,2176]{1,0:T(8,128)(2,1)S(1)} %get-tuple-element.37.payload), channel_id=1, source_target_pairs={{0,8},{8,0},{16,24},{24,16},{1,9},{9,1},{17,25},{25,17},{2,10},{10... | collective-permute-start | bytes 835592 | tf_op jit(solution)/shard_map/ppermute | solution.py:232
  44.3 7.4 %collective-permute-start.26 = (bf16[40,2048]{1,0:T(8,128)(2,1)S(1)}, bf16[40,2048]{1,0:T(8,128)(2,1)S(1)}, u32[]{:S(2)}, u32[]{:S(2)}) collective-permute-start(bf16[40,2048]{1,0:T(8,128)(2,1)S(1)} %get-tuple-element.64), channel_id=1, source_target_pairs={{0,2},{2,0},{4,6},{6,4},{1,3},{3,1},{5,7},{7,5},{8,10},{10,8},{12,... | collective-permute-start | bytes 491528 | tf_op jit(solution)/shard_map/ppermute | solution.py:232
  50.2 9.6 %collective-permute-start.27 = (bf16[40,2048]{1,0:T(8,128)(2,1)S(1)}, bf16[40,2048]{1,0:T(8,128)(2,1)S(1)}, u32[]{:S(2)}, u32[]{:S(2)}) collective-permute-start(bf16[40,2048]{1,0:T(8,128)(2,1)S(1)} %get-tuple-element.65), channel_id=1, source_target_pairs={{0,4},{2,6},{4,0},{6,2},{1,5},{3,7},{5,1},{7,3},{8,12},{10,14},{12... | collective-permute-start | bytes 491528 | tf_op jit(solution)/shard_map/ppermute | solution.py:232
  51.7 9.6 %collective-permute-start.28 = (bf16[40,2048]{1,0:T(8,128)(2,1)S(1)}, bf16[40,2048]{1,0:T(8,128)(2,1)S(1)}, u32[]{:S(2)}, u32[]{:S(2)}) collective-permute-start(bf16[40,2048]{1,0:T(8,128)(2,1)S(1)} %get-tuple-element.66), channel_id=1, source_target_pairs={{0,6},{2,4},{4,2},{6,0},{1,7},{3,5},{5,3},{7,1},{8,14},{10,12},{12... | collective-permute-start | bytes 491528 | tf_op jit(solution)/shard_map/ppermute | solution.py:232
  59.8 19.0 %collective-permute-start = (bf16[40,2048]{1,0:T(8,128)(2,1)S(1)}, bf16[40,2048]{1,0:T(8,128)(2,1)S(1)}, u32[]{:S(2)}, u32[]{:S(2)}) collective-permute-start(bf16[40,2048]{1,0:T(8,128)(2,1)S(1)} %get-tuple-element.40), channel_id=1, source_target_pairs={{0,2},{2,0},{4,6},{6,4},{1,3},{3,1},{5,7},{7,5},{8,10},{10,8},{12,... | collective-permute-start | bytes 491528 | tf_op jit(solution)/shard_map/ppermute | solution.py:232
  61.3 19.9 %collective-permute-start.1 = (bf16[40,2048]{1,0:T(8,128)(2,1)S(1)}, bf16[40,2048]{1,0:T(8,128)(2,1)S(1)}, u32[]{:S(2)}, u32[]{:S(2)}) collective-permute-start(bf16[40,2048]{1,0:T(8,128)(2,1)S(1)} %get-tuple-element.41), channel_id=1, source_target_pairs={{0,4},{2,6},{4,0},{6,2},{1,5},{3,7},{5,1},{7,3},{8,12},{10,14},{12... | collective-permute-start | bytes 491528 | tf_op jit(solution)/shard_map/ppermute | solution.py:232
  62.9 7.1 %collective-permute-start.18 = (bf16[40,2048]{1,0:T(8,128)(2,1)S(1)}, bf16[40,2048]{1,0:T(8,128)(2,1)S(1)}, u32[]{:S(2)}, u32[]{:S(2)}) collective-permute-start(bf16[40,2048]{1,0:T(8,128)(2,1)S(1)} %get-tuple-element.56), channel_id=1, source_target_pairs={{0,2},{2,0},{4,6},{6,4},{1,3},{3,1},{5,7},{7,5},{8,10},{10,8},{12,... | collective-permute-start | bytes 491528 | tf_op jit(solution)/shard_map/ppermute | solution.py:232
  63.4 10.1 %collective-permute-start.19 = (bf16[40,2048]{1,0:T(8,128)(2,1)S(1)}, bf16[40,2048]{1,0:T(8,128)(2,1)S(1)}, u32[]{:S(2)}, u32[]{:S(2)}) collective-permute-start(bf16[40,2048]{1,0:T(8,128)(2,1)S(1)} %get-tuple-element.57), channel_id=1, source_target_pairs={{0,4},{2,6},{4,0},{6,2},{1,5},{3,7},{5,1},{7,3},{8,12},{10,14},{12... | collective-permute-start | bytes 491528 | tf_op jit(solution)/shard_map/ppermute | solution.py:232
  63.9 12.0 %collective-permute-start.20 = (bf16[40,2048]{1,0:T(8,128)(2,1)S(1)}, bf16[40,2048]{1,0:T(8,128)(2,1)S(1)}, u32[]{:S(2)}, u32[]{:S(2)}) collective-permute-start(bf16[40,2048]{1,0:T(8,128)(2,1)S(1)} %get-tuple-element.58), channel_id=1, source_target_pairs={{0,6},{2,4},{4,2},{6,0},{1,7},{3,5},{5,3},{7,1},{8,14},{10,12},{12... | collective-permute-start | bytes 491528 | tf_op jit(solution)/shard_map/ppermute | solution.py:232
  70.0 11.8 %collective-permute-start.10 = (bf16[40,2048]{1,0:T(8,128)(2,1)S(1)}, bf16[40,2048]{1,0:T(8,128)(2,1)S(1)}, u32[]{:S(2)}, u32[]{:S(2)}) collective-permute-start(bf16[40,2048]{1,0:T(8,128)(2,1)S(1)} %get-tuple-element.48), channel_id=1, source_target_pairs={{0,2},{2,0},{4,6},{6,4},{1,3},{3,1},{5,7},{7,5},{8,10},{10,8},{12,... | collective-permute-start | bytes 491528 | tf_op jit(solution)/shard_map/ppermute | solution.py:232
  73.5 14.2 %collective-permute-start.11 = (bf16[40,2048]{1,0:T(8,128)(2,1)S(1)}, bf16[40,2048]{1,0:T(8,128)(2,1)S(1)}, u32[]{:S(2)}, u32[]{:S(2)}) collective-permute-start(bf16[40,2048]{1,0:T(8,128)(2,1)S(1)} %get-tuple-element.49), channel_id=1, source_target_pairs={{0,4},{2,6},{4,0},{6,2},{1,5},{3,7},{5,1},{7,3},{8,12},{10,14},{12... | collective-permute-start | bytes 491528 | tf_op jit(solution)/shard_map/ppermute | solution.py:232
  76.0 11.7 %collective-permute-start.12 = (bf16[40,2048]{1,0:T(8,128)(2,1)S(1)}, bf16[40,2048]{1,0:T(8,128)(2,1)S(1)}, u32[]{:S(2)}, u32[]{:S(2)}) collective-permute-start(bf16[40,2048]{1,0:T(8,128)(2,1)S(1)} %get-tuple-element.50), channel_id=1, source_target_pairs={{0,6},{2,4},{4,2},{6,0},{1,7},{3,5},{5,3},{7,1},{8,14},{10,12},{12... | collective-permute-start | bytes 491528 | tf_op jit(solution)/shard_map/ppermute | solution.py:232
  78.8 15.0 %collective-permute-start.2 = (bf16[40,2048]{1,0:T(8,128)(2,1)S(1)}, bf16[40,2048]{1,0:T(8,128)(2,1)S(1)}, u32[]{:S(2)}, u32[]{:S(2)}) collective-permute-start(bf16[40,2048]{1,0:T(8,128)(2,1)S(1)} %get-tuple-element.42), channel_id=1, source_target_pairs={{0,6},{2,4},{4,2},{6,0},{1,7},{3,5},{5,3},{7,1},{8,14},{10,12},{12... | collective-permute-start | bytes 491528 | tf_op jit(solution)/shard_map/ppermute | solution.py:232
  81.3 12.6 %collective-permute-start.29 = (bf16[40,2048]{1,0:T(8,128)(2,1)S(1)}, bf16[40,2048]{1,0:T(8,128)(2,1)S(1)}, u32[]{:S(2)}, u32[]{:S(2)}) collective-permute-start(bf16[40,2048]{1,0:T(8,128)(2,1)S(1)} %get-tuple-element.68), channel_id=1, source_target_pairs={{0,2},{2,0},{4,6},{6,4},{1,3},{3,1},{5,7},{7,5},{8,10},{10,8},{12,... | collective-permute-start | bytes 491528 | tf_op jit(solution)/shard_map/ppermute | solution.py:232
  81.8 13.6 %collective-permute-start.30 = (bf16[40,2048]{1,0:T(8,128)(2,1)S(1)}, bf16[40,2048]{1,0:T(8,128)(2,1)S(1)}, u32[]{:S(2)}, u32[]{:S(2)}) collective-permute-start(bf16[40,2048]{1,0:T(8,128)(2,1)S(1)} %get-tuple-element.69), channel_id=1, source_target_pairs={{0,4},{2,6},{4,0},{6,2},{1,5},{3,7},{5,1},{7,3},{8,12},{10,14},{12... | collective-permute-start | bytes 491528 | tf_op jit(solution)/shard_map/ppermute | solution.py:232
  87.7 9.7 %collective-permute-start.31 = (bf16[40,2048]{1,0:T(8,128)(2,1)S(1)}, bf16[40,2048]{1,0:T(8,128)(2,1)S(1)}, u32[]{:S(2)}, u32[]{:S(2)}) collective-permute-start(bf16[40,2048]{1,0:T(8,128)(2,1)S(1)} %get-tuple-element.70), channel_id=1, source_target_pairs={{0,6},{2,4},{4,2},{6,0},{1,7},{3,5},{5,3},{7,1},{8,14},{10,12},{12... | collective-permute-start | bytes 491528 | tf_op jit(solution)/shard_map/ppermute | solution.py:232
  87.7 12.3 %collective-permute-start.21 = (bf16[40,2048]{1,0:T(8,128)(2,1)S(1)}, bf16[40,2048]{1,0:T(8,128)(2,1)S(1)}, u32[]{:S(2)}, u32[]{:S(2)}) collective-permute-start(bf16[40,2048]{1,0:T(8,128)(2,1)S(1)} %get-tuple-element.60), channel_id=1, source_target_pairs={{0,2},{2,0},{4,6},{6,4},{1,3},{3,1},{5,7},{7,5},{8,10},{10,8},{12,... | collective-permute-start | bytes 491528 | tf_op jit(solution)/shard_map/ppermute | solution.py:232
  93.8 8.5 %collective-permute-start.22 = (bf16[40,2048]{1,0:T(8,128)(2,1)S(1)}, bf16[40,2048]{1,0:T(8,128)(2,1)S(1)}, u32[]{:S(2)}, u32[]{:S(2)}) collective-permute-start(bf16[40,2048]{1,0:T(8,128)(2,1)S(1)} %get-tuple-element.61), channel_id=1, source_target_pairs={{0,4},{2,6},{4,0},{6,2},{1,5},{3,7},{5,1},{7,3},{8,12},{10,14},{12... | collective-permute-start | bytes 491528 | tf_op jit(solution)/shard_map/ppermute | solution.py:232
  93.9 10.3 %collective-permute-start.23 = (bf16[40,2048]{1,0:T(8,128)(2,1)S(1)}, bf16[40,2048]{1,0:T(8,128)(2,1)S(1)}, u32[]{:S(2)}, u32[]{:S(2)}) collective-permute-start(bf16[40,2048]{1,0:T(8,128)(2,1)S(1)} %get-tuple-element.62), channel_id=1, source_target_pairs={{0,6},{2,4},{4,2},{6,0},{1,7},{3,5},{5,3},{7,1},{8,14},{10,12},{12... | collective-permute-start | bytes 491528 | tf_op jit(solution)/shard_map/ppermute | solution.py:232
  95.4 12.0 %collective-permute-start.13 = (bf16[40,2048]{1,0:T(8,128)(2,1)S(1)}, bf16[40,2048]{1,0:T(8,128)(2,1)S(1)}, u32[]{:S(2)}, u32[]{:S(2)}) collective-permute-start(bf16[40,2048]{1,0:T(8,128)(2,1)S(1)} %get-tuple-element.52), channel_id=1, source_target_pairs={{0,2},{2,0},{4,6},{6,4},{1,3},{3,1},{5,7},{7,5},{8,10},{10,8},{12,... | collective-permute-start | bytes 491528 | tf_op jit(solution)/shard_map/ppermute | solution.py:232
  97.4 10.1 %collective-permute-start.14 = (bf16[40,2048]{1,0:T(8,128)(2,1)S(1)}, bf16[40,2048]{1,0:T(8,128)(2,1)S(1)}, u32[]{:S(2)}, u32[]{:S(2)}) collective-permute-start(bf16[40,2048]{1,0:T(8,128)(2,1)S(1)} %get-tuple-element.53), channel_id=1, source_target_pairs={{0,4},{2,6},{4,0},{6,2},{1,5},{3,7},{5,1},{7,3},{8,12},{10,14},{12... | collective-permute-start | bytes 491528 | tf_op jit(solution)/shard_map/ppermute | solution.py:232
  100.0 7.5 %collective-permute-start.15 = (bf16[40,2048]{1,0:T(8,128)(2,1)S(1)}, bf16[40,2048]{1,0:T(8,128)(2,1)S(1)}, u32[]{:S(2)}, u32[]{:S(2)}) collective-permute-start(bf16[40,2048]{1,0:T(8,128)(2,1)S(1)} %get-tuple-element.54), channel_id=1, source_target_pairs={{0,6},{2,4},{4,2},{6,0},{1,7},{3,5},{5,3},{7,1},{8,14},{10,12},{12... | collective-permute-start | bytes 491528 | tf_op jit(solution)/shard_map/ppermute | solution.py:232
  102.3 10.0 %collective-permute-start.6 = (bf16[40,2048]{1,0:T(8,128)(2,1)S(1)}, bf16[40,2048]{1,0:T(8,128)(2,1)S(1)}, u32[]{:S(2)}, u32[]{:S(2)}) collective-permute-start(bf16[40,2048]{1,0:T(8,128)(2,1)S(1)} %get-tuple-element.44), channel_id=1, source_target_pairs={{0,2},{2,0},{4,6},{6,4},{1,3},{3,1},{5,7},{7,5},{8,10},{10,8},{12,... | collective-permute-start | bytes 491528 | tf_op jit(solution)/shard_map/ppermute | solution.py:232
  104.3 14.2 %collective-permute-start.32 = (bf16[64,2048]{1,0:T(8,128)(2,1)S(1)}, bf16[64,2048]{1,0:T(8,128)(2,1)S(1)}, u32[]{:S(2)}, u32[]{:S(2)}) collective-permute-start(bf16[64,2048]{1,0:T(8,128)(2,1)S(1)} %combine.5), channel_id=1, source_target_pairs={{0,24},{8,16},{16,8},{24,0},{1,25},{9,17},{17,9},{25,1},{2,26},{10... | collective-permute-start | bytes 786440 | tf_op jit(solution)/shard_map/ppermute | solution.py:232
  107.4 12.5 %collective-permute-start.24 = (bf16[64,2048]{1,0:T(8,128)(2,1)S(1)}, bf16[64,2048]{1,0:T(8,128)(2,1)S(1)}, u32[]{:S(2)}, u32[]{:S(2)}) collective-permute-start(bf16[64,2048]{1,0:T(8,128)(2,1)S(1)} %combine.4), channel_id=1, source_target_pairs={{0,16},{8,24},{16,0},{24,8},{1,17},{9,25},{17,1},{25,9},{2,18},{10... | collective-permute-start | bytes 786440 | tf_op jit(solution)/shard_map/ppermute | solution.py:232
  108.1 11.8 %collective-permute-start.16 = (bf16[64,2048]{1,0:T(8,128)(2,1)S(1)}, bf16[64,2048]{1,0:T(8,128)(2,1)S(1)}, u32[]{:S(2)}, u32[]{:S(2)}) collective-permute-start(bf16[64,2048]{1,0:T(8,128)(2,1)S(1)} %combine.3), channel_id=1, source_target_pairs={{0,8},{8,0},{16,24},{24,16},{1,9},{9,1},{17,25},{25,17},{2,10},{10... | collective-permute-start | bytes 786440 | tf_op jit(solution)/shard_map/ppermute | solution.py:232
  110.1 6.8 %collective-permute-start.7 = (bf16[40,2048]{1,0:T(8,128)(2,1)S(1)}, bf16[40,2048]{1,0:T(8,128)(2,1)S(1)}, u32[]{:S(2)}, u32[]{:S(2)}) collective-permute-start(bf16[40,2048]{1,0:T(8,128)(2,1)S(1)} %get-tuple-element.45), channel_id=1, source_target_pairs={{0,4},{2,6},{4,0},{6,2},{1,5},{3,7},{5,1},{7,3},{8,12},{10,14},{12... | collective-permute-start | bytes 491528 | tf_op jit(solution)/shard_map/ppermute | solution.py:232
  (7 other events, 194.2 us)

commit v3 on v2

--- a/solution.py
+++ b/solution.py
@@ -93,11 +93,11 @@
 
 
 def attention_kernel(
-    chips, capacity, experts, length, queries, new_kv, cache, residual, out_weight, gain, ids, gates,
+    chips, capacity, experts, length, queries, new_kv, cache, residual, out_weight, gain_in, ids_in, gates_in,
     stream, payload, appended, *rest,
 ):
-    outs, scratch = rest[:-9], rest[-9:]
-    cached, newest, queried, resid, projection, keys, values, mixed, sems = scratch
+    outs, scratch = rest[:-12], rest[-12:]
+    cached, newest, queried, resid, projection, gain, ids, gates, keys, values, mixed, sems = scratch
     slots = cache.shape[0]
     group = new_kv.shape[0]
     pieces = 4
@@ -112,12 +112,18 @@
     load_queries = pltpu.make_async_copy(queries, queried, sems.at[pieces + 1])
     load_resid = pltpu.make_async_copy(residual, resid, sems.at[pieces + 2])
     load_projection = pltpu.make_async_copy(out_weight, projection, sems.at[pieces + 3])
+    load_small = [
+        pltpu.make_async_copy(source, target, sems.at[pieces + 5 + i])
+        for i, (source, target) in enumerate([(gain_in, gain), (ids_in, ids), (gates_in, gates)])
+    ]
     load_new.start()
     for load in loads:
         load.start()
     load_queries.start()
     load_resid.start()
     load_projection.start()
+    for load in load_small:
+        load.start()
 
     def split(source, first, target):
         planes = jnp.swapaxes(source[pl.ds(first, 16)], 0, 1)
@@ -156,6 +162,8 @@
     store_new.start()
     load_resid.wait()
     load_projection.wait()
+    for load in load_small:
+        load.wait()
     total = resid[...].astype(jnp.float32) + dot(mixed[...], projection[...])
     stream[...] = total
     mean_square = jnp.mean(total * total, axis=-1, keepdims=True)
@@ -211,6 +219,11 @@
 HBM_SPEC = pl.BlockSpec(memory_space=pltpu.HBM)
 
 
+Z_FIRST = (1, 2, 3)
+ORDER = (("in", 0), ("in", 1), ("out", 0), ("in", 2), ("out", 1), ("in", 3), ("out", 2), ("out", 3))
+LAG = 2
+
+
 def shards(
     queries, new_kv, cache, lengths, residual, out_weight, norm_gain, expert_ids, gates, w_gate, w_up, w_down,
 ):
@@ -248,7 +261,6 @@
 
     own_halves = [w_gate[0], w_up[0], w_down[0]]
     other_halves = [across(half, "core", 1) for half in own_halves]
-    halves = [pltpu.with_memory_space_constraint(half, VMEM) for half in own_halves + other_halves]
 
     stream, payload, appended, *outgoing = pl.pallas_call(
         functools.partial(attention_kernel, chips, capacity, experts),
@@ -258,7 +270,7 @@
             jax.ShapeDtypeStruct(cache.shape[1:], cache.dtype),
         ]
         + block_shapes,
-        in_specs=[SMEM_SPEC] + [HBM_SPEC] * 5 + in_vmem(3),
+        in_specs=[SMEM_SPEC] + [HBM_SPEC] * 8,
         out_specs=in_vmem(2) + [HBM_SPEC] + in_vmem(blocks_n),
         scratch_shapes=[
             VMEM(cache.shape[1:], bf16),
@@ -266,10 +278,13 @@
             VMEM((group, features), bf16),
             VMEM((group, features), bf16),
             VMEM(out_weight.shape, bf16),
+            VMEM((1, features), jnp.float32),
+            VMEM((top_k, group), jnp.int32),
+            VMEM((top_k, group), jnp.float32),
             VMEM((slots + group, features), bf16),
             VMEM((slots + group, features), bf16),
             VMEM((group, features), bf16),
-            pltpu.SemaphoreType.DMA((9,)),
+            pltpu.SemaphoreType.DMA((12,)),
         ],
         compiler_params=params(24),
         cost_estimate=pl.CostEstimate(
@@ -280,27 +295,27 @@
         lengths,
         *[
             pltpu.with_memory_space_constraint(x, pltpu.HBM)
-            for x in (queries[0], new_kv[0], cache[0], residual[0], out_weight)
+            for x in (
+                queries[0], new_kv[0], cache[0], residual[0], out_weight, norm_gain[None], expert_ids[0].T, gates[0].T,
+            )
         ],
-        norm_gain[None],
-        expert_ids[0].T,
-        gates[0].T,
     )
 
-    payload_of = [payload] + [across(payload, "req", s) for s in range(1, planes)]
-    partials = []
-    for s in range(planes):
-        if s > 0:
-            outgoing = pl.pallas_call(
-                functools.partial(gather_kernel, chips, capacity, experts, features),
-                out_shape=block_shapes,
-                in_specs=in_vmem(1),
-                out_specs=in_vmem(blocks_n),
-                compiler_params=params(8),
-                name="gather",
-            )(payload_of[s])
-        arrived = joined(to_chips(cut(outgoing)))
-        results = pl.pallas_call(
+    payload, outgoing, other_halves = lax.optimization_barrier((payload, outgoing, other_halves))
+    halves = [pltpu.with_memory_space_constraint(half, VMEM) for half in own_halves + other_halves]
+
+    def gather(packed):
+        return pl.pallas_call(
+            functools.partial(gather_kernel, chips, capacity, experts, features),
+            out_shape=block_shapes,
+            in_specs=in_vmem(1),
+            out_specs=in_vmem(blocks_n),
+            compiler_params=params(8),
+            name="gather",
+        )(packed)
+
+    def run_experts(arrived):
+        return pl.pallas_call(
             functools.partial(expert_kernel, capacity, blocks_n),
             out_shape=block_shapes,
             in_specs=in_vmem(blocks_n + 6),
@@ -313,19 +328,39 @@
             ),
             name="experts",
         )(*arrived, *halves)
-        returned = joined(to_chips(cut(results)))
-        if s == 0:
-            own_returned = returned
+
+    def combine(packed, returned):
+        return pl.pallas_call(
+            functools.partial(combine_kernel, chips, capacity, experts, features),
+            out_shape=jax.ShapeDtypeStruct((group, features), bf16),
+            in_specs=in_vmem(1 + blocks_n),
+            out_specs=pl.BlockSpec(memory_space=VMEM),
+            compiler_params=params(8),
+            name="combine",
+        )(packed, *returned)
+
+    payload_of = {0: payload}
+    for s in Z_FIRST:
+        payload_of[s] = across(payload, "req", s)
+    arrived_of, returned_of, partials, moved = {}, {}, [], []
+    for k, (way, s) in enumerate(ORDER):
+        if way == "in":
+            if s not in payload_of:
+                later, moved[-1] = lax.optimization_barrier((payload, moved[-1]))
+                payload_of[s] = across(later, "req", s)
+            blocks = outgoing if s == 0 else gather(payload_of[s])
         else:
-            partial = pl.pallas_call(
-                functools.partial(combine_kernel, chips, capacity, experts, features),
-                out_shape=jax.ShapeDtypeStruct((group, features), bf16),
-                in_specs=in_vmem(1 + blocks_n),
-                out_specs=pl.BlockSpec(memory_space=VMEM),
-                compiler_params=params(8),
-                name="combine",
-            )(payload_of[s], *returned)
-            partials.append(across(partial, "req", s))
+            blocks = run_experts(arrived_of[s])
+        if k >= LAG:
+            blocks, moved[k - LAG] = lax.optimization_barrier((blocks, moved[k - LAG]))
+            pw, ps = ORDER[k - LAG]
+            (arrived_of if pw == "in" else returned_of)[ps] = moved[k - LAG]
+        got = joined(to_chips(cut(blocks)))
+        moved.append(got)
+        (arrived_of if way == "in" else returned_of)[s] = got
+        if way == "out" and s > 0:
+            partials.append(across(combine(payload_of[s], got), "req", s))
+    own_returned = returned_of[0]
     layer_out = pl.pallas_call(
         functools.partial(final_kernel, chips, capacity, experts, features, blocks_n),
         out_shape=jax.ShapeDtypeStruct((group, features), bf16),

time: 121 us -> 96.9 us (0.80); the launches traced: 121 us -> 95.2 us
  waiting for transfers between devices: 39.5 us -> 25.1 us
  starting transfers between devices: 52.9 us -> 43.3 us
  local copies, waits for them, and re-layouts: 2.07 us -> 0.01 us
    ppermute x33, waiting for transfers between devices: 39.5 us -> 25.1 us  [across(): return lax.ppermute(x, axis, [(i, i ^ j) for i in range(size)])]
    ppermute x33, starting transfers between devices: 52.9 us -> 43.3 us  [across(): return lax.ppermute(x, axis, [(i, i ^ j) for i in range(size)])]
    unnamed x12 -> x6, local copies, waits for them, and re-layouts: 2.07 us -> 0.01 us
  transfers between devices with their start and end apart: 33 -> 33, of which waited for: 11 -> 12; matrix products, arithmetic and copies ran while one was open for 0% -> 0% of each run, Pallas kernels for 20% -> 25%
where the time goes in v3:
time: 96.9 us; the launch traced here: 95.2 us
  starting transfers between devices  43.3 us (45%)
  Pallas kernels  25.3 us (26%)
  waiting for transfers between devices  25.1 us (26%)
  between operations  1.48 us (2%)
    ppermute x33, starting transfers between devices, across(): return lax.ppermute(x, axis, [(i, i ^ j) for i in range(size)])  43.3 us
    ppermute x33, waiting for transfers between devices, across(): return lax.ppermute(x, axis, [(i, i ^ j) for i in range(size)])  25.1 us
    pallas_call x1, Pallas kernels, shards(): pl.pallas_call(functools.partial(attention_kernel, chips, capacity, exper...  10.8 us
    pallas_call x4, Pallas kernels, run_experts(): pl.pallas_call(functools.partial(expert_kernel, capacity, blocks_n), out_...  9.45 us
    pallas_call x3, Pallas kernels, gather(): pl.pallas_call(functools.partial(gather_kernel, chips, capacity, experts,...  1.97 us
  transfers between devices with their start and end apart: 33, of which 12 were waited for; matrix products, arithmetic and copies ran while one was open for 0% of the time, Pallas kernels for 25%

profile of v3, /device:TPU:0, one launch (start us, length us, event | category | flops | bytes accessed | tf_op | source)
XLA Modules:
  0.0 95.2 jit_solution(3238019056322896555)
XLA Ops:
  2.3 10.8 %attention.1 = (f32[64,2048]{1,0:T(8,128)S(1)}, bf16[64,2176]{1,0:T(8,128)(2,1)S(1)}, bf16[512,2,2048]{2,1,0:T(2,128)(2,1)}, bf16[40,2048]{1,0:T(8,128)(2,1)S(1)...) custom-call(s32[1]{0:T(128)S(6)} %copy.14.length, ...), custom_call_target="tpu_custom_call" | custom-call | flops 12000000000 | bytes 25165824 | tf_op jit(solution)/shard_map/attention/pallas_call | solution.py:265
  13.2 2.7 %collective-permute-start.4 = (bf16[64,2176]{1,0:T(8,128)(2,1)S(1)}, bf16[64,2176]{1,0:T(8,128)(2,1)S(1)}, u32[]{:S(2)}, u32[]{:S(2)}) collective-permute-start(bf16[64,2176]{1,0:T(8,128)(2,1)S(1)} %get-tuple-element.86.payload), channel_id=1, source_target_pairs={{0,8},{8,0},{16,24},{24,16},{1,9},{9,1},{17,25},{25,17},{2,10},{10... | collective-permute-start | bytes 835592 | tf_op jit(solution)/shard_map/ppermute | solution.py:245
  15.9 1.5 %collective-permute-start.8 = (bf16[40,2048]{1,0:T(8,128)(2,1)S(1)}, bf16[40,2048]{1,0:T(8,128)(2,1)S(1)}, u32[]{:S(2)}, u32[]{:S(2)}) collective-permute-start(bf16[40,2048]{1,0:T(8,128)(2,1)S(1)} %get-tuple-element.108), channel_id=1, source_target_pairs={{0,2},{2,0},{4,6},{6,4},{1,3},{3,1},{5,7},{7,5},{8,10},{10,8},{12,... | collective-permute-start | bytes 491528 | tf_op jit(solution)/shard_map/ppermute | solution.py:245
  17.4 1.5 %collective-permute-start.9 = (bf16[40,2048]{1,0:T(8,128)(2,1)S(1)}, bf16[40,2048]{1,0:T(8,128)(2,1)S(1)}, u32[]{:S(2)}, u32[]{:S(2)}) collective-permute-start(bf16[40,2048]{1,0:T(8,128)(2,1)S(1)} %get-tuple-element.109), channel_id=1, source_target_pairs={{0,4},{2,6},{4,0},{6,2},{1,5},{3,7},{5,1},{7,3},{8,12},{10,14},{12... | collective-permute-start | bytes 491528 | tf_op jit(solution)/shard_map/ppermute | solution.py:245
  19.4 2.6 %collective-permute-start.3 = (bf16[64,2176]{1,0:T(8,128)(2,1)S(1)}, bf16[64,2176]{1,0:T(8,128)(2,1)S(1)}, u32[]{:S(2)}, u32[]{:S(2)}) collective-permute-start(bf16[64,2176]{1,0:T(8,128)(2,1)S(1)} %get-tuple-element.86.payload), channel_id=1, source_target_pairs={{0,16},{8,24},{16,0},{24,8},{1,17},{9,25},{17,1},{25,9},{2,18},{10... | collective-permute-start | bytes 835592 | tf_op jit(solution)/shard_map/ppermute | solution.py:245
  22.0 4.4 %collective-permute-done.4.payload = bf16[64,2176]{1,0:T(8,128)(2,1)S(1)} collective-permute-done((bf16[64,2176]{1,0:T(8,128)(2,1)S(1)}, bf16[64,2176]{1,0:T(8,128)(2,1)S(1)}, u32[]{:S(2)}, u32[]{:S(2)}) %collective-permute-start.4) | collective-permute-done | bytes 278560 | tf_op jit(solution)/shard_map/ppermute | solution.py:245
  27.0 1.7 %collective-permute-start.5 = (bf16[40,2048]{1,0:T(8,128)(2,1)S(1)}, bf16[40,2048]{1,0:T(8,128)(2,1)S(1)}, u32[]{:S(2)}, u32[]{:S(2)}) collective-permute-start(bf16[40,2048]{1,0:T(8,128)(2,1)S(1)} %get-tuple-element.93), channel_id=1, source_target_pairs={{0,2},{2,0},{4,6},{6,4},{1,3},{3,1},{5,7},{7,5},{8,10},{10,8},{12,... | collective-permute-start | bytes 491528 | tf_op jit(solution)/shard_map/ppermute | solution.py:245
  28.8 1.5 %collective-permute-start.6 = (bf16[40,2048]{1,0:T(8,128)(2,1)S(1)}, bf16[40,2048]{1,0:T(8,128)(2,1)S(1)}, u32[]{:S(2)}, u32[]{:S(2)}) collective-permute-start(bf16[40,2048]{1,0:T(8,128)(2,1)S(1)} %get-tuple-element.94), channel_id=1, source_target_pairs={{0,4},{2,6},{4,0},{6,2},{1,5},{3,7},{5,1},{7,3},{8,12},{10,14},{12... | collective-permute-start | bytes 491528 | tf_op jit(solution)/shard_map/ppermute | solution.py:245
  30.6 2.3 %experts.5 = (bf16[40,2048]{1,0:T(8,128)(2,1)S(1)}, bf16[40,2048]{1,0:T(8,128)(2,1)S(1)}, bf16[40,2048]{1,0:T(8,128)(2,1)S(1)}, bf16[40,2048]{1,0:T(8,128)(2,1)S(1)}) custom-call(bf16[40,2048]{1,0:T(8,128)(2,1)S(1)} %get-tuple-element.107.refs_0_, bf16[40,2048]{1,0:T(8,128)(2,1)S(1)} %collective-permute-done.8.refs_1_, ...), custom_call_target="tpu_custom_call" | custom-call | flops 2013265920 | bytes 12582912 | tf_op jit(solution)/shard_map/experts/pallas_call | solution.py:318
  32.9 1.7 %collective-permute-start.11 = (bf16[40,2048]{1,0:T(8,128)(2,1)S(1)}, bf16[40,2048]{1,0:T(8,128)(2,1)S(1)}, u32[]{:S(2)}, u32[]{:S(2)}) collective-permute-start(bf16[40,2048]{1,0:T(8,128)(2,1)S(1)} %get-tuple-element.116), channel_id=1, source_target_pairs={{0,2},{2,0},{4,6},{6,4},{1,3},{3,1},{5,7},{7,5},{8,10},{10,8},{12,... | collective-permute-start | bytes 491528 | tf_op jit(solution)/shard_map/ppermute | solution.py:245
  34.7 1.5 %collective-permute-start.12 = (bf16[40,2048]{1,0:T(8,128)(2,1)S(1)}, bf16[40,2048]{1,0:T(8,128)(2,1)S(1)}, u32[]{:S(2)}, u32[]{:S(2)}) collective-permute-start(bf16[40,2048]{1,0:T(8,128)(2,1)S(1)} %get-tuple-element.117), channel_id=1, source_target_pairs={{0,4},{2,6},{4,0},{6,2},{1,5},{3,7},{5,1},{7,3},{8,12},{10,14},{12... | collective-permute-start | bytes 491528 | tf_op jit(solution)/shard_map/ppermute | solution.py:245
  36.9 2.5 %collective-permute-start.18 = (bf16[64,2176]{1,0:T(8,128)(2,1)S(1)}, bf16[64,2176]{1,0:T(8,128)(2,1)S(1)}, u32[]{:S(2)}, u32[]{:S(2)}) collective-permute-start(bf16[64,2176]{1,0:T(8,128)(2,1)S(1)} %get-tuple-element.86.payload), channel_id=1, source_target_pairs={{0,24},{8,16},{16,8},{24,0},{1,25},{9,17},{17,9},{25,1},{2,26},{10... | collective-permute-start | bytes 835592 | tf_op jit(solution)/shard_map/ppermute | solution.py:245
  40.4 1.3 %collective-permute-start.19 = (bf16[40,2048]{1,0:T(8,128)(2,1)S(1)}, bf16[40,2048]{1,0:T(8,128)(2,1)S(1)}, u32[]{:S(2)}, u32[]{:S(2)}) collective-permute-start(bf16[40,2048]{1,0:T(8,128)(2,1)S(1)} %get-tuple-element.132), channel_id=1, source_target_pairs={{0,2},{2,0},{4,6},{6,4},{1,3},{3,1},{5,7},{7,5},{8,10},{10,8},{12,... | collective-permute-start | bytes 491528 | tf_op jit(solution)/shard_map/ppermute | solution.py:245
  41.7 1.2 %collective-permute-start.20 = (bf16[40,2048]{1,0:T(8,128)(2,1)S(1)}, bf16[40,2048]{1,0:T(8,128)(2,1)S(1)}, u32[]{:S(2)}, u32[]{:S(2)}) collective-permute-start(bf16[40,2048]{1,0:T(8,128)(2,1)S(1)} %get-tuple-element.133), channel_id=1, source_target_pairs={{0,4},{2,6},{4,0},{6,2},{1,5},{3,7},{5,1},{7,3},{8,12},{10,14},{12... | collective-permute-start | bytes 491528 | tf_op jit(solution)/shard_map/ppermute | solution.py:245
  43.3 1.4 %collective-permute-start.21 = (bf16[40,2048]{1,0:T(8,128)(2,1)S(1)}, bf16[40,2048]{1,0:T(8,128)(2,1)S(1)}, u32[]{:S(2)}, u32[]{:S(2)}) collective-permute-start(bf16[40,2048]{1,0:T(8,128)(2,1)S(1)} %get-tuple-element.134), channel_id=1, source_target_pairs={{0,6},{2,4},{4,2},{6,0},{1,7},{3,5},{5,3},{7,1},{8,14},{10,12},{12... | collective-permute-start | bytes 491528 | tf_op jit(solution)/shard_map/ppermute | solution.py:245
  44.7 2.3 %experts.4 = (bf16[40,2048]{1,0:T(8,128)(2,1)S(1)}, bf16[40,2048]{1,0:T(8,128)(2,1)S(1)}, bf16[40,2048]{1,0:T(8,128)(2,1)S(1)}, bf16[40,2048]{1,0:T(8,128)(2,1)S(1)}) custom-call(bf16[40,2048]{1,0:T(8,128)(2,1)S(1)} %get-tuple-element.96.refs_0_, bf16[40,2048]{1,0:T(8,128)(2,1)S(1)} %collective-permute-done.5.refs_1_, ...), custom_call_target="tpu_custom_call" | custom-call | flops 2013265920 | bytes 12582912 | tf_op jit(solution)/shard_map/experts/pallas_call | solution.py:318
  47.5 3.6 %collective-permute-start.14 = (bf16[40,2048]{1,0:T(8,128)(2,1)S(1)}, bf16[40,2048]{1,0:T(8,128)(2,1)S(1)}, u32[]{:S(2)}, u32[]{:S(2)}) collective-permute-start(bf16[40,2048]{1,0:T(8,128)(2,1)S(1)} %get-tuple-element.124), channel_id=1, source_target_pairs={{0,2},{2,0},{4,6},{6,4},{1,3},{3,1},{5,7},{7,5},{8,10},{10,8},{12,... | collective-permute-start | bytes 491528 | tf_op jit(solution)/shard_map/ppermute | solution.py:245
  51.9 1.5 %collective-permute-start.16 = (bf16[40,2048]{1,0:T(8,128)(2,1)S(1)}, bf16[40,2048]{1,0:T(8,128)(2,1)S(1)}, u32[]{:S(2)}, u32[]{:S(2)}) collective-permute-start(bf16[40,2048]{1,0:T(8,128)(2,1)S(1)} %get-tuple-element.126), channel_id=1, source_target_pairs={{0,6},{2,4},{4,2},{6,0},{1,7},{3,5},{5,3},{7,1},{8,14},{10,12},{12... | collective-permute-start | bytes 491528 | tf_op jit(solution)/shard_map/ppermute | solution.py:245
  53.3 1.3 %collective-permute-done.21.refs_3_ = bf16[40,2048]{1,0:T(8,128)(2,1)S(1)} collective-permute-done((bf16[40,2048]{1,0:T(8,128)(2,1)S(1)}, bf16[40,2048]{1,0:T(8,128)(2,1)S(1)}, u32[]{:S(2)}, u32[]{:S(2)}) %collective-permute-start.21) | collective-permute-done | bytes 163872 | tf_op jit(solution)/shard_map/ppermute | solution.py:245
  56.0 1.1 %collective-permute-done.14.refs_1_ = bf16[40,2048]{1,0:T(8,128)(2,1)S(1)} collective-permute-done((bf16[40,2048]{1,0:T(8,128)(2,1)S(1)}, bf16[40,2048]{1,0:T(8,128)(2,1)S(1)}, u32[]{:S(2)}, u32[]{:S(2)}) %collective-permute-start.14) | collective-permute-done | bytes 163872 | tf_op jit(solution)/shard_map/ppermute | solution.py:245
  57.0 2.1 %collective-permute-start.28 = (bf16[40,2048]{1,0:T(8,128)(2,1)S(1)}, bf16[40,2048]{1,0:T(8,128)(2,1)S(1)}, u32[]{:S(2)}, u32[]{:S(2)}) collective-permute-start(bf16[40,2048]{1,0:T(8,128)(2,1)S(1)} %get-tuple-element.150), channel_id=1, source_target_pairs={{0,6},{2,4},{4,2},{6,0},{1,7},{3,5},{5,3},{7,1},{8,14},{10,12},{12... | collective-permute-start | bytes 491528 | tf_op jit(solution)/shard_map/ppermute | solution.py:245
  59.1 2.5 %experts.6 = (bf16[40,2048]{1,0:T(8,128)(2,1)S(1)}, bf16[40,2048]{1,0:T(8,128)(2,1)S(1)}, bf16[40,2048]{1,0:T(8,128)(2,1)S(1)}, bf16[40,2048]{1,0:T(8,128)(2,1)S(1)}) custom-call(bf16[40,2048]{1,0:T(8,128)(2,1)S(1)} %get-tuple-element.135.refs_0_, bf16[40,2048]{1,0:T(8,128)(2,1)S(1)} %collective-permute-done.19.refs_1_, ...), custom_call_target="tpu_custom_call" | custom-call | flops 2013265920 | bytes 12582912 | tf_op jit(solution)/shard_map/experts/pallas_call | solution.py:318
  64.1 2.1 %collective-permute-start.24 = (bf16[40,2048]{1,0:T(8,128)(2,1)S(1)}, bf16[40,2048]{1,0:T(8,128)(2,1)S(1)}, u32[]{:S(2)}, u32[]{:S(2)}) collective-permute-start(bf16[40,2048]{1,0:T(8,128)(2,1)S(1)} %get-tuple-element.146), channel_id=1, source_target_pairs={{0,6},{2,4},{4,2},{6,0},{1,7},{3,5},{5,3},{7,1},{8,14},{10,12},{12... | collective-permute-start | bytes 491528 | tf_op jit(solution)/shard_map/ppermute | solution.py:245
  66.1 3.1 %collective-permute-done.27.refs_2_ = bf16[40,2048]{1,0:T(8,128)(2,1)S(1)} collective-permute-done((bf16[40,2048]{1,0:T(8,128)(2,1)S(1)}, bf16[40,2048]{1,0:T(8,128)(2,1)S(1)}, u32[]{:S(2)}, u32[]{:S(2)}) %collective-permute-start.27) | collective-permute-done | bytes 163872 | tf_op jit(solution)/shard_map/ppermute | solution.py:245
  69.2 2.3 %experts.7 = (bf16[40,2048]{1,0:T(8,128)(2,1)S(1)}, bf16[40,2048]{1,0:T(8,128)(2,1)S(1)}, bf16[40,2048]{1,0:T(8,128)(2,1)S(1)}, bf16[40,2048]{1,0:T(8,128)(2,1)S(1)}) custom-call(bf16[40,2048]{1,0:T(8,128)(2,1)S(1)} %get-tuple-element.147.refs_0_, bf16[40,2048]{1,0:T(8,128)(2,1)S(1)} %collective-permute-done.26.refs_1_, ...), custom_call_target="tpu_custom_call" | custom-call | flops 2013265920 | bytes 12582912 | tf_op jit(solution)/shard_map/experts/pallas_call | solution.py:318
  72.8 2.3 %collective-permute-start.31 = (bf16[40,2048]{1,0:T(8,128)(2,1)S(1)}, bf16[40,2048]{1,0:T(8,128)(2,1)S(1)}, u32[]{:S(2)}, u32[]{:S(2)}) collective-permute-start(bf16[40,2048]{1,0:T(8,128)(2,1)S(1)} %get-tuple-element.158), channel_id=1, source_target_pairs={{0,6},{2,4},{4,2},{6,0},{1,7},{3,5},{5,3},{7,1},{8,14},{10,12},{12... | collective-permute-start | bytes 491528 | tf_op jit(solution)/shard_map/ppermute | solution.py:245
  76.5 1.8 %collective-permute-start.25 = (bf16[64,2048]{1,0:T(8,128)(2,1)S(1)}, bf16[64,2048]{1,0:T(8,128)(2,1)S(1)}, u32[]{:S(2)}, u32[]{:S(2)}) collective-permute-start(bf16[64,2048]{1,0:T(8,128)(2,1)S(1)} %combine.4), channel_id=1, source_target_pairs={{0,16},{8,24},{16,0},{24,8},{1,17},{9,25},{17,1},{25,9},{2,18},{10... | collective-permute-start | bytes 786440 | tf_op jit(solution)/shard_map/ppermute | solution.py:245
  78.3 1.9 %collective-permute-done.30.refs_2_ = bf16[40,2048]{1,0:T(8,128)(2,1)S(1)} collective-permute-done((bf16[40,2048]{1,0:T(8,128)(2,1)S(1)}, bf16[40,2048]{1,0:T(8,128)(2,1)S(1)}, u32[]{:S(2)}, u32[]{:S(2)}) %collective-permute-start.30) | collective-permute-done | bytes 163872 | tf_op jit(solution)/shard_map/ppermute | solution.py:245
  80.8 2.5 %collective-permute-start.32 = (bf16[64,2048]{1,0:T(8,128)(2,1)S(1)}, bf16[64,2048]{1,0:T(8,128)(2,1)S(1)}, u32[]{:S(2)}, u32[]{:S(2)}) collective-permute-start(bf16[64,2048]{1,0:T(8,128)(2,1)S(1)} %combine.5), channel_id=1, source_target_pairs={{0,24},{8,16},{16,8},{24,0},{1,25},{9,17},{17,9},{25,1},{2,26},{10... | collective-permute-start | bytes 786440 | tf_op jit(solution)/shard_map/ppermute | solution.py:245
  83.2 1.4 %collective-permute-done.17.refs_4_ = bf16[64,2048]{1,0:T(8,128)(2,1)S(1)} collective-permute-done((bf16[64,2048]{1,0:T(8,128)(2,1)S(1)}, bf16[64,2048]{1,0:T(8,128)(2,1)S(1)}, u32[]{:S(2)}, u32[]{:S(2)}) %collective-permute-start.17) | collective-permute-done | bytes 262176 | tf_op jit(solution)/shard_map/ppermute | solution.py:245
  84.6 9.2 %collective-permute-done.25.refs_5_ = bf16[64,2048]{1,0:T(8,128)(2,1)S(1)} collective-permute-done((bf16[64,2048]{1,0:T(8,128)(2,1)S(1)}, bf16[64,2048]{1,0:T(8,128)(2,1)S(1)}, u32[]{:S(2)}, u32[]{:S(2)}) %collective-permute-start.25) | collective-permute-done | bytes 262176 | tf_op jit(solution)/shard_map/ppermute | solution.py:245
  93.9 1.3 %final.1 = bf16[64,2048]{1,0:T(8,128)(2,1)} custom-call(bf16[64,2176]{1,0:T(8,128)(2,1)S(1)} %get-tuple-element.86.payload, f32[64,2048]{1,0:T(8,128)S(1)} %get-tuple-element.87.stream, bf16[40,2048]{1,0:T(8,128)(2,1)S(1)} %get-tuple-element.119.refs_0_, bf16[40,2048]{1,0:T(8,128)(2,1)S(1)} %collective-permute-done.11.refs_1_, ...), custom_call_target="tpu_custom_call" | custom-call | tf_op jit(solution)/shard_map/final/pallas_call | solution.py:364
  (52 shorter events, 12.9 us)
Async XLA Ops:
  0.6 12.5 %collective-permute-start = (bf16[2048,512]{1,0:T(8,128)(2,1)}, bf16[2048,512]{1,0:T(8,128)(2,1)S(1)}, u32[]{:S(2)}, u32[]{:S(2)}) collective-permute-start(bf16[2048,512]{1,0:T(8,128)(2,1)} %bitcast.16), channel_id=1, source_target_pairs={{0,1},{1,0},{2,3},{3,2},{4,5},{5,4},{6,7},{7,6},{8,9},{9,8},{10,11... | collective-permute-start | bytes 6291464 | tf_op jit(solution)/shard_map/ppermute | solution.py:245
  1.2 12.0 %collective-permute-start.1 = (bf16[2048,512]{1,0:T(8,128)(2,1)}, bf16[2048,512]{1,0:T(8,128)(2,1)S(1)}, u32[]{:S(2)}, u32[]{:S(2)}) collective-permute-start(bf16[2048,512]{1,0:T(8,128)(2,1)} %bitcast.21), channel_id=1, source_target_pairs={{0,1},{1,0},{2,3},{3,2},{4,5},{5,4},{6,7},{7,6},{8,9},{9,8},{10,11... | collective-permute-start | bytes 6291464 | tf_op jit(solution)/shard_map/ppermute | solution.py:245
  1.2 11.9 %collective-permute-start.2 = (bf16[512,2048]{1,0:T(8,128)(2,1)}, bf16[512,2048]{1,0:T(8,128)(2,1)S(1)}, u32[]{:S(2)}, u32[]{:S(2)}) collective-permute-start(bf16[512,2048]{1,0:T(8,128)(2,1)} %bitcast.26), channel_id=1, source_target_pairs={{0,1},{1,0},{2,3},{3,2},{4,5},{5,4},{6,7},{7,6},{8,9},{9,8},{10,11... | collective-permute-start | bytes 6291464 | tf_op jit(solution)/shard_map/ppermute | solution.py:245
  13.2 13.2 %collective-permute-start.4 = (bf16[64,2176]{1,0:T(8,128)(2,1)S(1)}, bf16[64,2176]{1,0:T(8,128)(2,1)S(1)}, u32[]{:S(2)}, u32[]{:S(2)}) collective-permute-start(bf16[64,2176]{1,0:T(8,128)(2,1)S(1)} %get-tuple-element.86.payload), channel_id=1, source_target_pairs={{0,8},{8,0},{16,24},{24,16},{1,9},{9,1},{17,25},{25,17},{2,10},{10... | collective-permute-start | bytes 835592 | tf_op jit(solution)/shard_map/ppermute | solution.py:245
  15.9 12.9 %collective-permute-start.8 = (bf16[40,2048]{1,0:T(8,128)(2,1)S(1)}, bf16[40,2048]{1,0:T(8,128)(2,1)S(1)}, u32[]{:S(2)}, u32[]{:S(2)}) collective-permute-start(bf16[40,2048]{1,0:T(8,128)(2,1)S(1)} %get-tuple-element.108), channel_id=1, source_target_pairs={{0,2},{2,0},{4,6},{6,4},{1,3},{3,1},{5,7},{7,5},{8,10},{10,8},{12,... | collective-permute-start | bytes 491528 | tf_op jit(solution)/shard_map/ppermute | solution.py:245
  17.4 12.9 %collective-permute-start.9 = (bf16[40,2048]{1,0:T(8,128)(2,1)S(1)}, bf16[40,2048]{1,0:T(8,128)(2,1)S(1)}, u32[]{:S(2)}, u32[]{:S(2)}) collective-permute-start(bf16[40,2048]{1,0:T(8,128)(2,1)S(1)} %get-tuple-element.109), channel_id=1, source_target_pairs={{0,4},{2,6},{4,0},{6,2},{1,5},{3,7},{5,1},{7,3},{8,12},{10,14},{12... | collective-permute-start | bytes 491528 | tf_op jit(solution)/shard_map/ppermute | solution.py:245
  18.9 11.7 %collective-permute-start.10 = (bf16[40,2048]{1,0:T(8,128)(2,1)S(1)}, bf16[40,2048]{1,0:T(8,128)(2,1)S(1)}, u32[]{:S(2)}, u32[]{:S(2)}) collective-permute-start(bf16[40,2048]{1,0:T(8,128)(2,1)S(1)} %get-tuple-element.110), channel_id=1, source_target_pairs={{0,6},{2,4},{4,2},{6,0},{1,7},{3,5},{5,3},{7,1},{8,14},{10,12},{12... | collective-permute-start | bytes 491528 | tf_op jit(solution)/shard_map/ppermute | solution.py:245
  19.4 15.3 %collective-permute-start.3 = (bf16[64,2176]{1,0:T(8,128)(2,1)S(1)}, bf16[64,2176]{1,0:T(8,128)(2,1)S(1)}, u32[]{:S(2)}, u32[]{:S(2)}) collective-permute-start(bf16[64,2176]{1,0:T(8,128)(2,1)S(1)} %get-tuple-element.86.payload), channel_id=1, source_target_pairs={{0,16},{8,24},{16,0},{24,8},{1,17},{9,25},{17,1},{25,9},{2,18},{10... | collective-permute-start | bytes 835592 | tf_op jit(solution)/shard_map/ppermute | solution.py:245
  27.0 9.8 %collective-permute-start.5 = (bf16[40,2048]{1,0:T(8,128)(2,1)S(1)}, bf16[40,2048]{1,0:T(8,128)(2,1)S(1)}, u32[]{:S(2)}, u32[]{:S(2)}) collective-permute-start(bf16[40,2048]{1,0:T(8,128)(2,1)S(1)} %get-tuple-element.93), channel_id=1, source_target_pairs={{0,2},{2,0},{4,6},{6,4},{1,3},{3,1},{5,7},{7,5},{8,10},{10,8},{12,... | collective-permute-start | bytes 491528 | tf_op jit(solution)/shard_map/ppermute | solution.py:245
  28.8 10.6 %collective-permute-start.6 = (bf16[40,2048]{1,0:T(8,128)(2,1)S(1)}, bf16[40,2048]{1,0:T(8,128)(2,1)S(1)}, u32[]{:S(2)}, u32[]{:S(2)}) collective-permute-start(bf16[40,2048]{1,0:T(8,128)(2,1)S(1)} %get-tuple-element.94), channel_id=1, source_target_pairs={{0,4},{2,6},{4,0},{6,2},{1,5},{3,7},{5,1},{7,3},{8,12},{10,14},{12... | collective-permute-start | bytes 491528 | tf_op jit(solution)/shard_map/ppermute | solution.py:245
  30.3 10.1 %collective-permute-start.7 = (bf16[40,2048]{1,0:T(8,128)(2,1)S(1)}, bf16[40,2048]{1,0:T(8,128)(2,1)S(1)}, u32[]{:S(2)}, u32[]{:S(2)}) collective-permute-start(bf16[40,2048]{1,0:T(8,128)(2,1)S(1)} %get-tuple-element.95), channel_id=1, source_target_pairs={{0,6},{2,4},{4,2},{6,0},{1,7},{3,5},{5,3},{7,1},{8,14},{10,12},{12... | collective-permute-start | bytes 491528 | tf_op jit(solution)/shard_map/ppermute | solution.py:245
  32.9 8.8 %collective-permute-start.11 = (bf16[40,2048]{1,0:T(8,128)(2,1)S(1)}, bf16[40,2048]{1,0:T(8,128)(2,1)S(1)}, u32[]{:S(2)}, u32[]{:S(2)}) collective-permute-start(bf16[40,2048]{1,0:T(8,128)(2,1)S(1)} %get-tuple-element.116), channel_id=1, source_target_pairs={{0,2},{2,0},{4,6},{6,4},{1,3},{3,1},{5,7},{7,5},{8,10},{10,8},{12,... | collective-permute-start | bytes 491528 | tf_op jit(solution)/shard_map/ppermute | solution.py:245
  34.7 8.6 %collective-permute-start.12 = (bf16[40,2048]{1,0:T(8,128)(2,1)S(1)}, bf16[40,2048]{1,0:T(8,128)(2,1)S(1)}, u32[]{:S(2)}, u32[]{:S(2)}) collective-permute-start(bf16[40,2048]{1,0:T(8,128)(2,1)S(1)} %get-tuple-element.117), channel_id=1, source_target_pairs={{0,4},{2,6},{4,0},{6,2},{1,5},{3,7},{5,1},{7,3},{8,12},{10,14},{12... | collective-permute-start | bytes 491528 | tf_op jit(solution)/shard_map/ppermute | solution.py:245
  36.9 14.3 %collective-permute-start.18 = (bf16[64,2176]{1,0:T(8,128)(2,1)S(1)}, bf16[64,2176]{1,0:T(8,128)(2,1)S(1)}, u32[]{:S(2)}, u32[]{:S(2)}) collective-permute-start(bf16[64,2176]{1,0:T(8,128)(2,1)S(1)} %get-tuple-element.86.payload), channel_id=1, source_target_pairs={{0,24},{8,16},{16,8},{24,0},{1,25},{9,17},{17,9},{25,1},{2,26},{10... | collective-permute-start | bytes 835592 | tf_op jit(solution)/shard_map/ppermute | solution.py:245
  39.4 8.1 %collective-permute-start.13 = (bf16[40,2048]{1,0:T(8,128)(2,1)S(1)}, bf16[40,2048]{1,0:T(8,128)(2,1)S(1)}, u32[]{:S(2)}, u32[]{:S(2)}) collective-permute-start(bf16[40,2048]{1,0:T(8,128)(2,1)S(1)} %get-tuple-element.118), channel_id=1, source_target_pairs={{0,6},{2,4},{4,2},{6,0},{1,7},{3,5},{5,3},{7,1},{8,14},{10,12},{12... | collective-permute-start | bytes 491528 | tf_op jit(solution)/shard_map/ppermute | solution.py:245
  40.4 11.5 %collective-permute-start.19 = (bf16[40,2048]{1,0:T(8,128)(2,1)S(1)}, bf16[40,2048]{1,0:T(8,128)(2,1)S(1)}, u32[]{:S(2)}, u32[]{:S(2)}) collective-permute-start(bf16[40,2048]{1,0:T(8,128)(2,1)S(1)} %get-tuple-element.132), channel_id=1, source_target_pairs={{0,2},{2,0},{4,6},{6,4},{1,3},{3,1},{5,7},{7,5},{8,10},{10,8},{12,... | collective-permute-start | bytes 491528 | tf_op jit(solution)/shard_map/ppermute | solution.py:245
  41.7 11.6 %collective-permute-start.20 = (bf16[40,2048]{1,0:T(8,128)(2,1)S(1)}, bf16[40,2048]{1,0:T(8,128)(2,1)S(1)}, u32[]{:S(2)}, u32[]{:S(2)}) collective-permute-start(bf16[40,2048]{1,0:T(8,128)(2,1)S(1)} %get-tuple-element.133), channel_id=1, source_target_pairs={{0,4},{2,6},{4,0},{6,2},{1,5},{3,7},{5,1},{7,3},{8,12},{10,14},{12... | collective-permute-start | bytes 491528 | tf_op jit(solution)/shard_map/ppermute | solution.py:245
  43.3 11.4 %collective-permute-start.21 = (bf16[40,2048]{1,0:T(8,128)(2,1)S(1)}, bf16[40,2048]{1,0:T(8,128)(2,1)S(1)}, u32[]{:S(2)}, u32[]{:S(2)}) collective-permute-start(bf16[40,2048]{1,0:T(8,128)(2,1)S(1)} %get-tuple-element.134), channel_id=1, source_target_pairs={{0,6},{2,4},{4,2},{6,0},{1,7},{3,5},{5,3},{7,1},{8,14},{10,12},{12... | collective-permute-start | bytes 491528 | tf_op jit(solution)/shard_map/ppermute | solution.py:245
  47.5 9.5 %collective-permute-start.14 = (bf16[40,2048]{1,0:T(8,128)(2,1)S(1)}, bf16[40,2048]{1,0:T(8,128)(2,1)S(1)}, u32[]{:S(2)}, u32[]{:S(2)}) collective-permute-start(bf16[40,2048]{1,0:T(8,128)(2,1)S(1)} %get-tuple-element.124), channel_id=1, source_target_pairs={{0,2},{2,0},{4,6},{6,4},{1,3},{3,1},{5,7},{7,5},{8,10},{10,8},{12,... | collective-permute-start | bytes 491528 | tf_op jit(solution)/shard_map/ppermute | solution.py:245
  51.8 10.7 %collective-permute-start.15 = (bf16[40,2048]{1,0:T(8,128)(2,1)S(1)}, bf16[40,2048]{1,0:T(8,128)(2,1)S(1)}, u32[]{:S(2)}, u32[]{:S(2)}) collective-permute-start(bf16[40,2048]{1,0:T(8,128)(2,1)S(1)} %get-tuple-element.125), channel_id=1, source_target_pairs={{0,4},{2,6},{4,0},{6,2},{1,5},{3,7},{5,1},{7,3},{8,12},{10,14},{12... | collective-permute-start | bytes 491528 | tf_op jit(solution)/shard_map/ppermute | solution.py:245
  51.9 10.6 %collective-permute-start.16 = (bf16[40,2048]{1,0:T(8,128)(2,1)S(1)}, bf16[40,2048]{1,0:T(8,128)(2,1)S(1)}, u32[]{:S(2)}, u32[]{:S(2)}) collective-permute-start(bf16[40,2048]{1,0:T(8,128)(2,1)S(1)} %get-tuple-element.126), channel_id=1, source_target_pairs={{0,6},{2,4},{4,2},{6,0},{1,7},{3,5},{5,3},{7,1},{8,14},{10,12},{12... | collective-permute-start | bytes 491528 | tf_op jit(solution)/shard_map/ppermute | solution.py:245
  54.6 9.5 %collective-permute-start.26 = (bf16[40,2048]{1,0:T(8,128)(2,1)S(1)}, bf16[40,2048]{1,0:T(8,128)(2,1)S(1)}, u32[]{:S(2)}, u32[]{:S(2)}) collective-permute-start(bf16[40,2048]{1,0:T(8,128)(2,1)S(1)} %get-tuple-element.148), channel_id=1, source_target_pairs={{0,2},{2,0},{4,6},{6,4},{1,3},{3,1},{5,7},{7,5},{8,10},{10,8},{12,... | collective-permute-start | bytes 491528 | tf_op jit(solution)/shard_map/ppermute | solution.py:245
  55.6 13.6 %collective-permute-start.27 = (bf16[40,2048]{1,0:T(8,128)(2,1)S(1)}, bf16[40,2048]{1,0:T(8,128)(2,1)S(1)}, u32[]{:S(2)}, u32[]{:S(2)}) collective-permute-start(bf16[40,2048]{1,0:T(8,128)(2,1)S(1)} %get-tuple-element.149), channel_id=1, source_target_pairs={{0,4},{2,6},{4,0},{6,2},{1,5},{3,7},{5,1},{7,3},{8,12},{10,14},{12... | collective-permute-start | bytes 491528 | tf_op jit(solution)/shard_map/ppermute | solution.py:245
  57.0 12.2 %collective-permute-start.28 = (bf16[40,2048]{1,0:T(8,128)(2,1)S(1)}, bf16[40,2048]{1,0:T(8,128)(2,1)S(1)}, u32[]{:S(2)}, u32[]{:S(2)}) collective-permute-start(bf16[40,2048]{1,0:T(8,128)(2,1)S(1)} %get-tuple-element.150), channel_id=1, source_target_pairs={{0,6},{2,4},{4,2},{6,0},{1,7},{3,5},{5,3},{7,1},{8,14},{10,12},{12... | collective-permute-start | bytes 491528 | tf_op jit(solution)/shard_map/ppermute | solution.py:245
  62.5 10.3 %collective-permute-start.22 = (bf16[40,2048]{1,0:T(8,128)(2,1)S(1)}, bf16[40,2048]{1,0:T(8,128)(2,1)S(1)}, u32[]{:S(2)}, u32[]{:S(2)}) collective-permute-start(bf16[40,2048]{1,0:T(8,128)(2,1)S(1)} %get-tuple-element.144), channel_id=1, source_target_pairs={{0,2},{2,0},{4,6},{6,4},{1,3},{3,1},{5,7},{7,5},{8,10},{10,8},{12,... | collective-permute-start | bytes 491528 | tf_op jit(solution)/shard_map/ppermute | solution.py:245
  62.7 13.2 %collective-permute-start.23 = (bf16[40,2048]{1,0:T(8,128)(2,1)S(1)}, bf16[40,2048]{1,0:T(8,128)(2,1)S(1)}, u32[]{:S(2)}, u32[]{:S(2)}) collective-permute-start(bf16[40,2048]{1,0:T(8,128)(2,1)S(1)} %get-tuple-element.145), channel_id=1, source_target_pairs={{0,4},{2,6},{4,0},{6,2},{1,5},{3,7},{5,1},{7,3},{8,12},{10,14},{12... | collective-permute-start | bytes 491528 | tf_op jit(solution)/shard_map/ppermute | solution.py:245
  64.1 11.8 %collective-permute-start.24 = (bf16[40,2048]{1,0:T(8,128)(2,1)S(1)}, bf16[40,2048]{1,0:T(8,128)(2,1)S(1)}, u32[]{:S(2)}, u32[]{:S(2)}) collective-permute-start(bf16[40,2048]{1,0:T(8,128)(2,1)S(1)} %get-tuple-element.146), channel_id=1, source_target_pairs={{0,6},{2,4},{4,2},{6,0},{1,7},{3,5},{5,3},{7,1},{8,14},{10,12},{12... | collective-permute-start | bytes 491528 | tf_op jit(solution)/shard_map/ppermute | solution.py:245
  72.1 8.0 %collective-permute-start.30 = (bf16[40,2048]{1,0:T(8,128)(2,1)S(1)}, bf16[40,2048]{1,0:T(8,128)(2,1)S(1)}, u32[]{:S(2)}, u32[]{:S(2)}) collective-permute-start(bf16[40,2048]{1,0:T(8,128)(2,1)S(1)} %get-tuple-element.157), channel_id=1, source_target_pairs={{0,4},{2,6},{4,0},{6,2},{1,5},{3,7},{5,1},{7,3},{8,12},{10,14},{12... | collective-permute-start | bytes 491528 | tf_op jit(solution)/shard_map/ppermute | solution.py:245
  72.8 7.4 %collective-permute-start.31 = (bf16[40,2048]{1,0:T(8,128)(2,1)S(1)}, bf16[40,2048]{1,0:T(8,128)(2,1)S(1)}, u32[]{:S(2)}, u32[]{:S(2)}) collective-permute-start(bf16[40,2048]{1,0:T(8,128)(2,1)S(1)} %get-tuple-element.158), channel_id=1, source_target_pairs={{0,6},{2,4},{4,2},{6,0},{1,7},{3,5},{5,3},{7,1},{8,14},{10,12},{12... | collective-permute-start | bytes 491528 | tf_op jit(solution)/shard_map/ppermute | solution.py:245
  75.9 8.7 %collective-permute-start.17 = (bf16[64,2048]{1,0:T(8,128)(2,1)S(1)}, bf16[64,2048]{1,0:T(8,128)(2,1)S(1)}, u32[]{:S(2)}, u32[]{:S(2)}) collective-permute-start(bf16[64,2048]{1,0:T(8,128)(2,1)S(1)} %combine.3), channel_id=1, source_target_pairs={{0,8},{8,0},{16,24},{24,16},{1,9},{9,1},{17,25},{25,17},{2,10},{10... | collective-permute-start | bytes 786440 | tf_op jit(solution)/shard_map/ppermute | solution.py:245
  76.5 17.4 %collective-permute-start.25 = (bf16[64,2048]{1,0:T(8,128)(2,1)S(1)}, bf16[64,2048]{1,0:T(8,128)(2,1)S(1)}, u32[]{:S(2)}, u32[]{:S(2)}) collective-permute-start(bf16[64,2048]{1,0:T(8,128)(2,1)S(1)} %combine.4), channel_id=1, source_target_pairs={{0,16},{8,24},{16,0},{24,8},{1,17},{9,25},{17,1},{25,9},{2,18},{10... | collective-permute-start | bytes 786440 | tf_op jit(solution)/shard_map/ppermute | solution.py:245
  80.8 13.1 %collective-permute-start.32 = (bf16[64,2048]{1,0:T(8,128)(2,1)S(1)}, bf16[64,2048]{1,0:T(8,128)(2,1)S(1)}, u32[]{:S(2)}, u32[]{:S(2)}) collective-permute-start(bf16[64,2048]{1,0:T(8,128)(2,1)S(1)} %combine.5), channel_id=1, source_target_pairs={{0,24},{8,16},{16,8},{24,0},{1,25},{9,17},{17,9},{25,1},{2,26},{10... | collective-permute-start | bytes 786440 | tf_op jit(solution)/shard_map/ppermute | solution.py:245
  (4 other events, 91.6 us)

commit v4 on v3

--- a/solution.py
+++ b/solution.py
@@ -12,6 +12,7 @@
 masked_value = -1e30
 ALL = ("req", "chip", "core")
 VMEM = pltpu.VMEM
+HEAD_PARTS = 2
 
 
 def dot(a, b):
@@ -94,90 +95,82 @@
 
 def attention_kernel(
     chips, capacity, experts, length, queries, new_kv, cache, residual, out_weight, gain_in, ids_in, gates_in,
-    stream, payload, appended, *rest,
+    stream, payload, cached, newest, *rest,
 ):
-    outs, scratch = rest[:-12], rest[-12:]
-    cached, newest, queried, resid, projection, gain, ids, gates, keys, values, mixed, sems = scratch
+    outs, scratch = rest[:-10], rest[-10:]
+    queried, resid, projection, gain, ids, gates, keys, values, mixed, sems = scratch
     slots = cache.shape[0]
-    group = new_kv.shape[0]
-    pieces = 4
-    part = slots // pieces
-    loads = [
-        pltpu.make_async_copy(
-            cache.at[pl.ds(i * part, part)], cached.at[pl.ds(i * part, part)], sems.at[i]
-        )
-        for i in range(pieces)
-    ]
-    load_new = pltpu.make_async_copy(new_kv, newest, sems.at[pieces])
-    load_queries = pltpu.make_async_copy(queries, queried, sems.at[pieces + 1])
-    load_resid = pltpu.make_async_copy(residual, resid, sems.at[pieces + 2])
-    load_projection = pltpu.make_async_copy(out_weight, projection, sems.at[pieces + 3])
-    load_small = [
-        pltpu.make_async_copy(source, target, sems.at[pieces + 5 + i])
-        for i, (source, target) in enumerate([(gain_in, gain), (ids_in, ids), (gates_in, gates)])
-    ]
-    load_new.start()
+    group, features = queries.shape
+    parts = HEAD_PARTS
+    wide = features // parts
+    small = [(ids_in, ids), (gates_in, gates), (gain_in, gain)]
+    first = [(new_kv, newest), (queries, queried)]
+    spans = [pl.ds(i * wide, wide) for i in range(parts)]
+    pairs = small + first + [(cache.at[:, :, span], cached.at[:, :, span]) for span in spans]
+    pairs += [(residual, resid)] + [(out_weight.at[span], projection.at[span]) for span in spans]
+    loads = [pltpu.make_async_copy(source, target, sems.at[i]) for i, (source, target) in enumerate(pairs)]
     for load in loads:
         load.start()
-    load_queries.start()
-    load_resid.start()
-    load_projection.start()
+    load_small, load_first, load_cache = loads[:3], loads[3:5], loads[5 : 5 + parts]
+    load_resid, load_projection = loads[5 + parts], loads[6 + parts :]
+
+    def split(source, start, target, span):
+        both = jnp.swapaxes(source[pl.ds(start, 16), :, span], 0, 1)
+        keys[pl.ds(target, 16), span] = both[0]
+        values[pl.ds(target, 16), span] = both[1]
+
     for load in load_small:
-        load.start()
-
-    def split(source, first, target):
-        planes = jnp.swapaxes(source[pl.ds(first, 16)], 0, 1)
-        keys[pl.ds(target, 16), :] = planes[0]
-        values[pl.ds(target, 16), :] = planes[1]
-
-    load_new.wait()
+        load.wait()
+    weights = routing(ids[...], gates[...], experts)
+    high = weights.astype(jnp.bfloat16)
+    low = (weights - high.astype(jnp.float32)).astype(jnp.bfloat16)
+    spare = payload.shape[1] - features - 2 * experts
+    trail = [high, low] + ([jnp.zeros((group, spare), jnp.bfloat16)] if spare else [])
+    payload[:, features:] = jnp.concatenate(trail, axis=1)
+    for load in load_first:
+        load.wait()
     for i in range(group // 16):
-        split(newest, i * 16, slots + i * 16)
-    for i in range(pieces):
-        loads[i].wait()
-
-        def step(k, carry):
-            first = pl.multiple_of(i * part + k * 16, 16)
-            split(cached, first, first)
-            return carry
-
-        lax.fori_loop(0, part // 16, step, 0)
-    store_cache = pltpu.make_async_copy(cached, appended, sems.at[pieces + 4])
-    store_cache.start()
-    load_queries.wait()
+        split(newest, i * 16, slots + i * 16, slice(None))
     positions = slots + group
     slot_place = lax.broadcasted_iota(jnp.int32, (1, positions), 1)
     counted = (slot_place < length[0]) | (slot_place >= slots)
-    for h in range(HEADS):
-        head = slice(h * HEAD_DIM, (h + 1) * HEAD_DIM)
-        scores = lax.dot_general(
-            queried[:, head], keys[:, head], (((1,), (1,)), ((), ())), preferred_element_type=jnp.float32
+    heads_part = HEADS // parts
+    for part in range(parts):
+        load_cache[part].wait()
+        span = slice(part * wide, (part + 1) * wide)
+
+        def step(k, carry):
+            start = pl.multiple_of(k * 16, 16)
+            split(cached, start, start, span)
+            return carry
+
+        lax.fori_loop(0, slots // 16, step, 0, unroll=4)
+        heads = [slice(h * HEAD_DIM, (h + 1) * HEAD_DIM) for h in range(part * heads_part, (part + 1) * heads_part)]
+        scores = jnp.concatenate(
+            [
+                lax.dot_general(
+                    queried[:, head], keys[:, head], (((1,), (1,)), ((), ())), preferred_element_type=jnp.float32
+                )
+                for head in heads
+            ],
+            axis=0,
         ) * HEAD_DIM ** (-0.5)
         scores = jnp.where(counted, scores, masked_value)
         raised = jnp.exp(scores - jnp.max(scores, axis=-1, keepdims=True))
         softmax_bf = (raised / jnp.sum(raised, axis=-1, keepdims=True)).astype(jnp.bfloat16)
-        mixed[:, head] = dot(softmax_bf, values[:, head]).astype(jnp.bfloat16)
-    store_cache.wait()
-    store_new = pltpu.make_async_copy(newest, appended.at[pl.ds(length[0], group)], sems.at[pieces + 4])
-    store_new.start()
+        for i, head in enumerate(heads):
+            mixed[:, head] = dot(softmax_bf[i * group : (i + 1) * group], values[:, head]).astype(jnp.bfloat16)
     load_resid.wait()
-    load_projection.wait()
-    for load in load_small:
-        load.wait()
-    total = resid[...].astype(jnp.float32) + dot(mixed[...], projection[...])
+    total = resid[...].astype(jnp.float32)
+    for part in range(parts):
+        load_projection[part].wait()
+        span = slice(part * wide, (part + 1) * wide)
+        total = total + dot(mixed[:, span], projection[span, :])
     stream[...] = total
     mean_square = jnp.mean(total * total, axis=-1, keepdims=True)
     rows = (total * lax.rsqrt(mean_square + 1e-06) * gain[...]).astype(jnp.bfloat16)
-    features = rows.shape[1]
-    weights = routing(ids[...], gates[...], experts)
-    high = weights.astype(jnp.bfloat16)
-    low = (weights - high.astype(jnp.float32)).astype(jnp.bfloat16)
-    spare = payload.shape[1] - features - 2 * experts
-    trail = [high, low] + ([jnp.zeros((rows.shape[0], spare), jnp.bfloat16)] if spare else [])
     payload[:, :features] = rows
-    payload[:, features:] = jnp.concatenate(trail, axis=1)
     gather_rows(rows, weights, chips, capacity, outs)
-    store_new.wait()
 
 
 def gather_kernel(chips, capacity, experts, features, payload, *outs):
@@ -185,8 +178,17 @@
     gather_rows(payload[:, :features], weights, chips, capacity, outs)
 
 
-def expert_kernel(capacity, counts, *refs):
-    ins, halves, outs = refs[:counts], refs[counts : counts + 6], refs[counts + 6 :]
+def expert_kernel(capacity, counts, span, length, cached, newest, *refs):
+    if span is None or span[0] > 0:
+        refs = refs[1:]
+    ins, halves, outs = refs[:counts], refs[counts : counts + 6], refs[counts + 6 : -2]
+    appended, sem = refs[-2:]
+    if span is None:
+        write = pltpu.make_async_copy(newest, appended.at[pl.ds(length[0], newest.shape[0])], sem)
+    else:
+        piece = pl.ds(span[0], span[1] - span[0])
+        write = pltpu.make_async_copy(cached.at[piece], appended.at[piece], sem)
+    write.start()
     rows = stacked(ins)
     total = None
     for i in range(2):
@@ -196,6 +198,7 @@
         partial = dot(hidden, down_half[...])
         total = partial if total is None else total + partial
     scatter_out(total, capacity, outs)
+    write.wait()
 
 
 def combine_kernel(chips, capacity, experts, features, payload, *refs):
@@ -203,12 +206,9 @@
     refs[-1][...] = combined(refs[:-1], weights, chips, capacity).astype(jnp.bfloat16)
 
 
-def final_kernel(chips, capacity, experts, features, counts, payload, stream, *refs):
+def own_kernel(chips, capacity, experts, features, payload, stream, *refs):
     weights = unpacked(payload, features, experts)
-    total = combined(refs[:counts], weights, chips, capacity)
-    for ref in refs[counts:-1]:
-        total = total + ref[...].astype(jnp.float32)
-    refs[-1][...] = (stream[...] + total).astype(jnp.bfloat16)
+    refs[-1][...] = stream[...] + combined(refs[:-1], weights, chips, capacity)
 
 
 def in_vmem(count):
@@ -262,19 +262,18 @@
     own_halves = [w_gate[0], w_up[0], w_down[0]]
     other_halves = [across(half, "core", 1) for half in own_halves]
 
-    stream, payload, appended, *outgoing = pl.pallas_call(
+    stream, payload, cached, newest, *outgoing = pl.pallas_call(
         functools.partial(attention_kernel, chips, capacity, experts),
         out_shape=[
             jax.ShapeDtypeStruct((group, features), jnp.float32),
             jax.ShapeDtypeStruct((group, width), bf16),
-            jax.ShapeDtypeStruct(cache.shape[1:], cache.dtype),
+            jax.ShapeDtypeStruct(cache.shape[1:], bf16),
+            jax.ShapeDtypeStruct(new_kv.shape[1:], bf16),
         ]
         + block_shapes,
         in_specs=[SMEM_SPEC] + [HBM_SPEC] * 8,
-        out_specs=in_vmem(2) + [HBM_SPEC] + in_vmem(blocks_n),
+        out_specs=in_vmem(4 + blocks_n),
         scratch_shapes=[
-            VMEM(cache.shape[1:], bf16),
-            VMEM(new_kv.shape[1:], bf16),
             VMEM((group, features), bf16),
             VMEM((group, features), bf16),
             VMEM(out_weight.shape, bf16),
@@ -284,7 +283,7 @@
             VMEM((slots + group, features), bf16),
             VMEM((slots + group, features), bf16),
             VMEM((group, features), bf16),
-            pltpu.SemaphoreType.DMA((12,)),
+            pltpu.SemaphoreType.DMA((6 + 2 * HEAD_PARTS,)),
         ],
         compiler_params=params(24),
         cost_estimate=pl.CostEstimate(
@@ -314,12 +313,19 @@
             name="gather",
         )(packed)
 
-    def run_experts(arrived):
-        return pl.pallas_call(
-            functools.partial(expert_kernel, capacity, blocks_n),
-            out_shape=block_shapes,
-            in_specs=in_vmem(blocks_n + 6),
-            out_specs=in_vmem(blocks_n),
+    held = [pltpu.with_memory_space_constraint(x, VMEM) for x in (cached, newest)]
+    cuts = [slots * i // (planes - 1) for i in range(planes)]
+    spans = list(zip(cuts[:-1], cuts[1:])) + [None]
+
+    def run_experts(arrived, call, appended):
+        before = [] if call == 0 else [pltpu.with_memory_space_constraint(appended, pltpu.HBM)]
+        *results, appended = pl.pallas_call(
+            functools.partial(expert_kernel, capacity, blocks_n, spans[call]),
+            out_shape=block_shapes + [jax.ShapeDtypeStruct(cache.shape[1:], cache.dtype)],
+            in_specs=[SMEM_SPEC] + in_vmem(2) + [HBM_SPEC] * len(before) + in_vmem(blocks_n + 6),
+            out_specs=in_vmem(blocks_n) + [HBM_SPEC],
+            scratch_shapes=[pltpu.SemaphoreType.DMA],
+            input_output_aliases={3: blocks_n} if before else {},
             compiler_params=params(8),
             cost_estimate=pl.CostEstimate(
                 flops=12 * chips * capacity * features * w_gate.shape[2],
@@ -327,7 +333,8 @@
                 transcendentals=0,
             ),
             name="experts",
-        )(*arrived, *halves)
+        )(lengths, *held, *before, *arrived, *halves)
+        return results, appended
 
     def combine(packed, returned):
         return pl.pallas_call(
@@ -340,9 +347,10 @@
         )(packed, *returned)
 
     payload_of = {0: payload}
+    calls, appended = 0, None
     for s in Z_FIRST:
         payload_of[s] = across(payload, "req", s)
-    arrived_of, returned_of, partials, moved = {}, {}, [], []
+    arrived_of, returned_of, partials, moved, due = {}, {}, [], [], []
     for k, (way, s) in enumerate(ORDER):
         if way == "in":
             if s not in payload_of:
@@ -350,25 +358,40 @@
                 payload_of[s] = across(later, "req", s)
             blocks = outgoing if s == 0 else gather(payload_of[s])
         else:
-            blocks = run_experts(arrived_of[s])
+            blocks, appended = run_experts(arrived_of[s], calls, appended)
+            calls += 1
         if k >= LAG:
-            blocks, moved[k - LAG] = lax.optimization_barrier((blocks, moved[k - LAG]))
             pw, ps = ORDER[k - LAG]
-            (arrived_of if pw == "in" else returned_of)[ps] = moved[k - LAG]
+            if pw == "out" and ps > 0:
+                partial = combine(payload_of[ps], moved[k - LAG])
+                blocks, partial = lax.optimization_barrier((blocks, partial))
+                due.append(({1: 7, 2: 99, 3: 99}[ps], len(partials)))
+                partials.append(across(partial, "req", ps))
+                returned_of.pop(ps)
+            else:
+                blocks, moved[k - LAG] = lax.optimization_barrier((blocks, moved[k - LAG]))
+                (arrived_of if pw == "in" else returned_of)[ps] = moved[k - LAG]
+        while due and due[0][0] <= k:
+            at = due.pop(0)[1]
+            blocks, partials[at] = lax.optimization_barrier((blocks, partials[at]))
         got = joined(to_chips(cut(blocks)))
         moved.append(got)
         (arrived_of if way == "in" else returned_of)[s] = got
-        if way == "out" and s > 0:
-            partials.append(across(combine(payload_of[s], got), "req", s))
+    for s in sorted(returned_of):
+        if s > 0:
+            partials.append(across(combine(payload_of[s], returned_of[s]), "req", s))
     own_returned = returned_of[0]
-    layer_out = pl.pallas_call(
-        functools.partial(final_kernel, chips, capacity, experts, features, blocks_n),
-        out_shape=jax.ShapeDtypeStruct((group, features), bf16),
-        in_specs=in_vmem(2 + blocks_n + len(partials)),
+    total = pl.pallas_call(
+        functools.partial(own_kernel, chips, capacity, experts, features),
+        out_shape=jax.ShapeDtypeStruct((group, features), jnp.float32),
+        in_specs=in_vmem(2 + blocks_n),
         out_specs=pl.BlockSpec(memory_space=VMEM),
         compiler_params=params(8),
-        name="final",
-    )(payload, stream, *own_returned, *partials)
+        name="own",
+    )(payload, stream, *own_returned)
+    for partial in partials:
+        total = total + partial.astype(jnp.float32)
+    layer_out = total.astype(bf16)
     return (layer_out[None], appended[None])
 
 

time: 96.9 us -> 92.2 us (0.951); the launches traced: 95.2 us -> 91.7 us
  Pallas kernels: 25.3 us -> 21.1 us
    pallas_call x1, Pallas kernels: 10.8 us -> 7.23 us  [shards(): pl.pallas_call(functools.partial(attention_kernel, chips, capacity, exper...]
  transfers between devices with their start and end apart: 33 -> 33, of which waited for: 12 -> 12; matrix products, arithmetic and copies ran while one was open for 0% -> 0% of each run, Pallas kernels for 25% -> 23%
where the time goes in v4:
time: 92.2 us; the launch traced here: 91.7 us
  starting transfers between devices  42.7 us (46%)
  waiting for transfers between devices  25.5 us (28%)
  Pallas kernels  21.1 us (23%)
  between operations  1.49 us (2%)
    ppermute x33, starting transfers between devices, across(): return lax.ppermute(x, axis, [(i, i ^ j) for i in range(size)])  42.7 us
    ppermute x33, waiting for transfers between devices, across(): return lax.ppermute(x, axis, [(i, i ^ j) for i in range(size)])  25.5 us
    pallas_call x4, Pallas kernels, run_experts(): pl.pallas_call(functools.partial(expert_kernel, capacity, blocks_n, spans...  9.52 us
    pallas_call x1, Pallas kernels, shards(): pl.pallas_call(functools.partial(attention_kernel, chips, capacity, exper...  7.23 us
    pallas_call x3, Pallas kernels, gather(): pl.pallas_call(functools.partial(gather_kernel, chips, capacity, experts,...  1.98 us
  transfers between devices with their start and end apart: 33, of which 12 were waited for; matrix products, arithmetic and copies ran while one was open for 0% of the time, Pallas kernels for 23%

profile of v4, /device:TPU:0, one launch (start us, length us, event | category | flops | bytes accessed | tf_op | source)
XLA Modules:
  0.0 91.7 jit_solution(8930478779910791127)
XLA Ops:
  2.3 7.2 %attention.1 = (f32[64,2048]{1,0:T(8,128)S(1)}, bf16[64,2176]{1,0:T(8,128)(2,1)S(1)}, bf16[512,2,2048]{2,1,0:T(2,128)(2,1)S(1)}, bf16[64,2,2048]{2,1,0:T(2,128)(...) custom-call(s32[1]{0:T(128)S(6)} %copy.20.length, ...), custom_call_target="tpu_custom_call" | custom-call | flops 12000000000 | bytes 25165824 | tf_op jit(solution)/shard_map/attention/pallas_call | solution.py:265
  9.6 1.5 %collective-permute-done.2.refs_9_.refs_10_ = bf16[512,2048]{1,0:T(8,128)(2,1)S(1)} collective-permute-done((bf16[512,2048]{1,0:T(8,128)(2,1)}, bf16[512,2048]{1,0:T(8,128)(2,1)S(1)}, u32[]{:S(2)}, u32[]{:S(2)}) %collective-permute-start.2) | collective-permute-done | bytes 2097184 | tf_op jit(solution)/shard_map/ppermute | solution.py:245
  11.1 2.9 %collective-permute-start.7 = (bf16[64,2176]{1,0:T(8,128)(2,1)S(1)}, bf16[64,2176]{1,0:T(8,128)(2,1)S(1)}, u32[]{:S(2)}, u32[]{:S(2)}) collective-permute-start(bf16[64,2176]{1,0:T(8,128)(2,1)S(1)} %get-tuple-element.97.payload), channel_id=1, source_target_pairs={{0,8},{8,0},{16,24},{24,16},{1,9},{9,1},{17,25},{25,17},{2,10},{10... | collective-permute-start | bytes 835592 | tf_op jit(solution)/shard_map/ppermute | solution.py:245
  14.1 1.5 %collective-permute-start.3 = (bf16[40,2048]{1,0:T(8,128)(2,1)S(1)}, bf16[40,2048]{1,0:T(8,128)(2,1)S(1)}, u32[]{:S(2)}, u32[]{:S(2)}) collective-permute-start(bf16[40,2048]{1,0:T(8,128)(2,1)S(1)} %get-tuple-element.102), channel_id=1, source_target_pairs={{0,2},{2,0},{4,6},{6,4},{1,3},{3,1},{5,7},{7,5},{8,10},{10,8},{12,... | collective-permute-start | bytes 491528 | tf_op jit(solution)/shard_map/ppermute | solution.py:245
  15.6 1.5 %collective-permute-start.4 = (bf16[40,2048]{1,0:T(8,128)(2,1)S(1)}, bf16[40,2048]{1,0:T(8,128)(2,1)S(1)}, u32[]{:S(2)}, u32[]{:S(2)}) collective-permute-start(bf16[40,2048]{1,0:T(8,128)(2,1)S(1)} %get-tuple-element.103), channel_id=1, source_target_pairs={{0,4},{2,6},{4,0},{6,2},{1,5},{3,7},{5,1},{7,3},{8,12},{10,14},{12... | collective-permute-start | bytes 491528 | tf_op jit(solution)/shard_map/ppermute | solution.py:245
  17.6 2.6 %collective-permute-start.6 = (bf16[64,2176]{1,0:T(8,128)(2,1)S(1)}, bf16[64,2176]{1,0:T(8,128)(2,1)S(1)}, u32[]{:S(2)}, u32[]{:S(2)}) collective-permute-start(bf16[64,2176]{1,0:T(8,128)(2,1)S(1)} %get-tuple-element.97.payload), channel_id=1, source_target_pairs={{0,16},{8,24},{16,0},{24,8},{1,17},{9,25},{17,1},{25,9},{2,18},{10... | collective-permute-start | bytes 835592 | tf_op jit(solution)/shard_map/ppermute | solution.py:245
  20.2 4.1 %collective-permute-done.7.payload = bf16[64,2176]{1,0:T(8,128)(2,1)S(1)} collective-permute-done((bf16[64,2176]{1,0:T(8,128)(2,1)S(1)}, bf16[64,2176]{1,0:T(8,128)(2,1)S(1)}, u32[]{:S(2)}, u32[]{:S(2)}) %collective-permute-start.7) | collective-permute-done | bytes 278560 | tf_op jit(solution)/shard_map/ppermute | solution.py:245
  24.9 2.7 %collective-permute-start.10 = (bf16[40,2048]{1,0:T(8,128)(2,1)S(1)}, bf16[40,2048]{1,0:T(8,128)(2,1)S(1)}, u32[]{:S(2)}, u32[]{:S(2)}) collective-permute-start(bf16[40,2048]{1,0:T(8,128)(2,1)S(1)} %get-tuple-element.116), channel_id=1, source_target_pairs={{0,6},{2,4},{4,2},{6,0},{1,7},{3,5},{5,3},{7,1},{8,14},{10,12},{12... | collective-permute-start | bytes 491528 | tf_op jit(solution)/shard_map/ppermute | solution.py:245
  28.5 2.3 %experts.4 = (bf16[40,2048]{1,0:T(8,128)(2,1)S(1)}, bf16[40,2048]{1,0:T(8,128)(2,1)S(1)}, bf16[40,2048]{1,0:T(8,128)(2,1)S(1)}, bf16[40,2048]{1,0:T(8,128)(2,1)S(1)}, bf16[512,2,2048]{2,1,0:T(2,128)(2,1)}) custom-call(s32[1]{0:T(128)S(6)} %copy.20.length, bf16[512,2,2048]{2,1,0:T(2,128)(2,1)S(1)} %get-tuple-element.99.cached, ...), custom_call_target="tpu_custom_call" | custom-call | flops 2013265920 | bytes 12582912 | tf_op jit(solution)/shard_map/experts/pallas_call | solution.py:322
  30.8 1.7 %collective-permute-start.11 = (bf16[40,2048]{1,0:T(8,128)(2,1)S(1)}, bf16[40,2048]{1,0:T(8,128)(2,1)S(1)}, u32[]{:S(2)}, u32[]{:S(2)}) collective-permute-start(bf16[40,2048]{1,0:T(8,128)(2,1)S(1)} %get-tuple-element.130), channel_id=1, source_target_pairs={{0,2},{2,0},{4,6},{6,4},{1,3},{3,1},{5,7},{7,5},{8,10},{10,8},{12,... | collective-permute-start | bytes 491528 | tf_op jit(solution)/shard_map/ppermute | solution.py:245
  32.6 1.5 %collective-permute-start.12 = (bf16[40,2048]{1,0:T(8,128)(2,1)S(1)}, bf16[40,2048]{1,0:T(8,128)(2,1)S(1)}, u32[]{:S(2)}, u32[]{:S(2)}) collective-permute-start(bf16[40,2048]{1,0:T(8,128)(2,1)S(1)} %get-tuple-element.131), channel_id=1, source_target_pairs={{0,4},{2,6},{4,0},{6,2},{1,5},{3,7},{5,1},{7,3},{8,12},{10,14},{12... | collective-permute-start | bytes 491528 | tf_op jit(solution)/shard_map/ppermute | solution.py:245
  34.8 2.5 %collective-permute-start.14 = (bf16[64,2176]{1,0:T(8,128)(2,1)S(1)}, bf16[64,2176]{1,0:T(8,128)(2,1)S(1)}, u32[]{:S(2)}, u32[]{:S(2)}) collective-permute-start(bf16[64,2176]{1,0:T(8,128)(2,1)S(1)} %get-tuple-element.97.payload), channel_id=1, source_target_pairs={{0,24},{8,16},{16,8},{24,0},{1,25},{9,17},{17,9},{25,1},{2,26},{10... | collective-permute-start | bytes 835592 | tf_op jit(solution)/shard_map/ppermute | solution.py:245
  38.2 1.0 %collective-permute-start.15 = (bf16[40,2048]{1,0:T(8,128)(2,1)S(1)}, bf16[40,2048]{1,0:T(8,128)(2,1)S(1)}, u32[]{:S(2)}, u32[]{:S(2)}) collective-permute-start(bf16[40,2048]{1,0:T(8,128)(2,1)S(1)} %get-tuple-element.143), channel_id=1, source_target_pairs={{0,2},{2,0},{4,6},{6,4},{1,3},{3,1},{5,7},{7,5},{8,10},{10,8},{12,... | collective-permute-start | bytes 491528 | tf_op jit(solution)/shard_map/ppermute | solution.py:245
  39.3 1.5 %collective-permute-start.16 = (bf16[40,2048]{1,0:T(8,128)(2,1)S(1)}, bf16[40,2048]{1,0:T(8,128)(2,1)S(1)}, u32[]{:S(2)}, u32[]{:S(2)}) collective-permute-start(bf16[40,2048]{1,0:T(8,128)(2,1)S(1)} %get-tuple-element.144), channel_id=1, source_target_pairs={{0,4},{2,6},{4,0},{6,2},{1,5},{3,7},{5,1},{7,3},{8,12},{10,14},{12... | collective-permute-start | bytes 491528 | tf_op jit(solution)/shard_map/ppermute | solution.py:245
  41.7 2.3 %experts.5 = (bf16[40,2048]{1,0:T(8,128)(2,1)S(1)}, bf16[40,2048]{1,0:T(8,128)(2,1)S(1)}, bf16[40,2048]{1,0:T(8,128)(2,1)S(1)}, bf16[40,2048]{1,0:T(8,128)(2,1)S(1)}, bf16[512,2,2048]{2,1,0:T(2,128)(2,1)}) custom-call(s32[1]{0:T(128)S(6)} %copy.20.length, bf16[512,2,2048]{2,1,0:T(2,128)(2,1)S(1)} %get-tuple-element.99.cached, ...), custom_call_target="tpu_custom_call", output_to_operand_aliasing={{4}: (3, {})} | custom-call | flops 2013265920 | bytes 12582912 | tf_op jit(solution)/shard_map/experts/pallas_call | solution.py:322
  44.1 1.4 %collective-permute-done.13.refs_3_ = bf16[40,2048]{1,0:T(8,128)(2,1)S(1)} collective-permute-done((bf16[40,2048]{1,0:T(8,128)(2,1)S(1)}, bf16[40,2048]{1,0:T(8,128)(2,1)S(1)}, u32[]{:S(2)}, u32[]{:S(2)}) %collective-permute-start.13) | collective-permute-done | bytes 163872 | tf_op jit(solution)/shard_map/ppermute | solution.py:245
  47.9 1.9 %collective-permute-start.23 = (bf16[40,2048]{1,0:T(8,128)(2,1)S(1)}, bf16[40,2048]{1,0:T(8,128)(2,1)S(1)}, u32[]{:S(2)}, u32[]{:S(2)}) collective-permute-start(bf16[40,2048]{1,0:T(8,128)(2,1)S(1)} %get-tuple-element.170), channel_id=1, source_target_pairs={{0,6},{2,4},{4,2},{6,0},{1,7},{3,5},{5,3},{7,1},{8,14},{10,12},{12... | collective-permute-start | bytes 491528 | tf_op jit(solution)/shard_map/ppermute | solution.py:245
  49.9 2.6 %collective-permute-done.17.refs_4_ = bf16[40,2048]{1,0:T(8,128)(2,1)S(1)} collective-permute-done((bf16[40,2048]{1,0:T(8,128)(2,1)S(1)}, bf16[40,2048]{1,0:T(8,128)(2,1)S(1)}, u32[]{:S(2)}, u32[]{:S(2)}) %collective-permute-start.17) | collective-permute-done | bytes 163872 | tf_op jit(solution)/shard_map/ppermute | solution.py:245
  54.0 1.0 %collective-permute-done.21.refs_1_ = bf16[40,2048]{1,0:T(8,128)(2,1)S(1)} collective-permute-done((bf16[40,2048]{1,0:T(8,128)(2,1)S(1)}, bf16[40,2048]{1,0:T(8,128)(2,1)S(1)}, u32[]{:S(2)}, u32[]{:S(2)}) %collective-permute-start.21) | collective-permute-done | bytes 163872 | tf_op jit(solution)/shard_map/ppermute | solution.py:245
  55.0 1.9 %collective-permute-start.20 = (bf16[40,2048]{1,0:T(8,128)(2,1)S(1)}, bf16[40,2048]{1,0:T(8,128)(2,1)S(1)}, u32[]{:S(2)}, u32[]{:S(2)}) collective-permute-start(bf16[40,2048]{1,0:T(8,128)(2,1)S(1)} %get-tuple-element.154), channel_id=1, source_target_pairs={{0,6},{2,4},{4,2},{6,0},{1,7},{3,5},{5,3},{7,1},{8,14},{10,12},{12... | collective-permute-start | bytes 491528 | tf_op jit(solution)/shard_map/ppermute | solution.py:245
  57.0 2.3 %experts.6 = (bf16[40,2048]{1,0:T(8,128)(2,1)S(1)}, bf16[40,2048]{1,0:T(8,128)(2,1)S(1)}, bf16[40,2048]{1,0:T(8,128)(2,1)S(1)}, bf16[40,2048]{1,0:T(8,128)(2,1)S(1)}, bf16[512,2,2048]{2,1,0:T(2,128)(2,1)}) custom-call(s32[1]{0:T(128)S(6)} %copy.20.length, bf16[512,2,2048]{2,1,0:T(2,128)(2,1)S(1)} %get-tuple-element.99.cached, ...), custom_call_target="tpu_custom_call", output_to_operand_aliasing={{4}: (3, {})} | custom-call | flops 2013265920 | bytes 12582912 | tf_op jit(solution)/shard_map/experts/pallas_call | solution.py:322
  60.3 1.1 %collective-permute-start.25 = (bf16[40,2048]{1,0:T(8,128)(2,1)S(1)}, bf16[40,2048]{1,0:T(8,128)(2,1)S(1)}, u32[]{:S(2)}, u32[]{:S(2)}) collective-permute-start(bf16[40,2048]{1,0:T(8,128)(2,1)S(1)} %get-tuple-element.174), channel_id=1, source_target_pairs={{0,2},{2,0},{4,6},{6,4},{1,3},{3,1},{5,7},{7,5},{8,10},{10,8},{12,... | collective-permute-start | bytes 491528 | tf_op jit(solution)/shard_map/ppermute | solution.py:245
  62.1 1.5 %collective-permute-start.26 = (bf16[40,2048]{1,0:T(8,128)(2,1)S(1)}, bf16[40,2048]{1,0:T(8,128)(2,1)S(1)}, u32[]{:S(2)}, u32[]{:S(2)}) collective-permute-start(bf16[40,2048]{1,0:T(8,128)(2,1)S(1)} %get-tuple-element.175), channel_id=1, source_target_pairs={{0,4},{2,6},{4,0},{6,2},{1,5},{3,7},{5,1},{7,3},{8,12},{10,14},{12... | collective-permute-start | bytes 491528 | tf_op jit(solution)/shard_map/ppermute | solution.py:245
  63.6 1.8 %collective-permute-start.27 = (bf16[40,2048]{1,0:T(8,128)(2,1)S(1)}, bf16[40,2048]{1,0:T(8,128)(2,1)S(1)}, u32[]{:S(2)}, u32[]{:S(2)}) collective-permute-start(bf16[40,2048]{1,0:T(8,128)(2,1)S(1)} %get-tuple-element.176), channel_id=1, source_target_pairs={{0,6},{2,4},{4,2},{6,0},{1,7},{3,5},{5,3},{7,1},{8,14},{10,12},{12... | collective-permute-start | bytes 491528 | tf_op jit(solution)/shard_map/ppermute | solution.py:245
  65.4 1.2 %collective-permute-done.20.refs_4_ = bf16[40,2048]{1,0:T(8,128)(2,1)S(1)} collective-permute-done((bf16[40,2048]{1,0:T(8,128)(2,1)S(1)}, bf16[40,2048]{1,0:T(8,128)(2,1)S(1)}, u32[]{:S(2)}, u32[]{:S(2)}) %collective-permute-start.20) | collective-permute-done | bytes 163872 | tf_op jit(solution)/shard_map/ppermute | solution.py:245
  66.6 2.5 %experts.7 = (bf16[40,2048]{1,0:T(8,128)(2,1)S(1)}, bf16[40,2048]{1,0:T(8,128)(2,1)S(1)}, bf16[40,2048]{1,0:T(8,128)(2,1)S(1)}, bf16[40,2048]{1,0:T(8,128)(2,1)S(1)}, bf16[512,2,2048]{2,1,0:T(2,128)(2,1)}) custom-call(s32[1]{0:T(128)S(6)} %copy.20.length, bf16[512,2,2048]{2,1,0:T(2,128)(2,1)S(1)} %get-tuple-element.99.cached, ...), custom_call_target="tpu_custom_call", output_to_operand_aliasing={{4}: (3, {})} | custom-call | flops 2013265920 | bytes 12582912 | tf_op jit(solution)/shard_map/experts/pallas_call | solution.py:322
  69.2 1.1 %collective-permute-start.29 = (bf16[40,2048]{1,0:T(8,128)(2,1)S(1)}, bf16[40,2048]{1,0:T(8,128)(2,1)S(1)}, u32[]{:S(2)}, u32[]{:S(2)}) collective-permute-start(bf16[40,2048]{1,0:T(8,128)(2,1)S(1)} %get-tuple-element.178), channel_id=1, source_target_pairs={{0,2},{2,0},{4,6},{6,4},{1,3},{3,1},{5,7},{7,5},{8,10},{10,8},{12,... | collective-permute-start | bytes 491528 | tf_op jit(solution)/shard_map/ppermute | solution.py:245
  70.6 2.1 %collective-permute-start.31 = (bf16[40,2048]{1,0:T(8,128)(2,1)S(1)}, bf16[40,2048]{1,0:T(8,128)(2,1)S(1)}, u32[]{:S(2)}, u32[]{:S(2)}) collective-permute-start(bf16[40,2048]{1,0:T(8,128)(2,1)S(1)} %get-tuple-element.180), channel_id=1, source_target_pairs={{0,6},{2,4},{4,2},{6,0},{1,7},{3,5},{5,3},{7,1},{8,14},{10,12},{12... | collective-permute-start | bytes 491528 | tf_op jit(solution)/shard_map/ppermute | solution.py:245
  74.2 1.1 %collective-permute-start.28 = (bf16[64,2048]{1,0:T(8,128)(2,1)S(1)}, bf16[64,2048]{1,0:T(8,128)(2,1)S(1)}, u32[]{:S(2)}, u32[]{:S(2)}) collective-permute-start(bf16[64,2048]{1,0:T(8,128)(2,1)S(1)} %combine.4), channel_id=1, source_target_pairs={{0,16},{8,24},{16,0},{24,8},{1,17},{9,25},{17,1},{25,9},{2,18},{10... | collective-permute-start | bytes 786440 | tf_op jit(solution)/shard_map/ppermute | solution.py:245
  75.3 2.0 %collective-permute-done.30.refs_2_ = bf16[40,2048]{1,0:T(8,128)(2,1)S(1)} collective-permute-done((bf16[40,2048]{1,0:T(8,128)(2,1)S(1)}, bf16[40,2048]{1,0:T(8,128)(2,1)S(1)}, u32[]{:S(2)}, u32[]{:S(2)}) %collective-permute-start.30) | collective-permute-done | bytes 163872 | tf_op jit(solution)/shard_map/ppermute | solution.py:245
  77.9 2.9 %collective-permute-start.32 = (bf16[64,2048]{1,0:T(8,128)(2,1)S(1)}, bf16[64,2048]{1,0:T(8,128)(2,1)S(1)}, u32[]{:S(2)}, u32[]{:S(2)}) collective-permute-start(bf16[64,2048]{1,0:T(8,128)(2,1)S(1)} %combine.5), channel_id=1, source_target_pairs={{0,24},{8,16},{16,8},{24,0},{1,25},{9,17},{17,9},{25,1},{2,26},{10... | collective-permute-start | bytes 786440 | tf_op jit(solution)/shard_map/ppermute | solution.py:245
  81.5 9.4 %collective-permute-done.28 = bf16[64,2048]{1,0:T(8,128)(2,1)S(1)} collective-permute-done((bf16[64,2048]{1,0:T(8,128)(2,1)S(1)}, bf16[64,2048]{1,0:T(8,128)(2,1)S(1)}, u32[]{:S(2)}, u32[]{:S(2)}) %collective-permute-start.28) | collective-permute-done | bytes 262176 | tf_op jit(solution)/shard_map/ppermute | solution.py:245
  (53 shorter events, 15.1 us)
Async XLA Ops:
  0.6 9.0 %collective-permute-start = (bf16[2048,512]{1,0:T(8,128)(2,1)}, bf16[2048,512]{1,0:T(8,128)(2,1)S(1)}, u32[]{:S(2)}, u32[]{:S(2)}) collective-permute-start(bf16[2048,512]{1,0:T(8,128)(2,1)} %bitcast.17), channel_id=1, source_target_pairs={{0,1},{1,0},{2,3},{3,2},{4,5},{5,4},{6,7},{7,6},{8,9},{9,8},{10,11... | collective-permute-start | bytes 6291464 | tf_op jit(solution)/shard_map/ppermute | solution.py:245
  1.2 8.4 %collective-permute-start.1 = (bf16[2048,512]{1,0:T(8,128)(2,1)}, bf16[2048,512]{1,0:T(8,128)(2,1)S(1)}, u32[]{:S(2)}, u32[]{:S(2)}) collective-permute-start(bf16[2048,512]{1,0:T(8,128)(2,1)} %bitcast.22), channel_id=1, source_target_pairs={{0,1},{1,0},{2,3},{3,2},{4,5},{5,4},{6,7},{7,6},{8,9},{9,8},{10,11... | collective-permute-start | bytes 6291464 | tf_op jit(solution)/shard_map/ppermute | solution.py:245
  1.2 9.9 %collective-permute-start.2 = (bf16[512,2048]{1,0:T(8,128)(2,1)}, bf16[512,2048]{1,0:T(8,128)(2,1)S(1)}, u32[]{:S(2)}, u32[]{:S(2)}) collective-permute-start(bf16[512,2048]{1,0:T(8,128)(2,1)} %bitcast.27), channel_id=1, source_target_pairs={{0,1},{1,0},{2,3},{3,2},{4,5},{5,4},{6,7},{7,6},{8,9},{9,8},{10,11... | collective-permute-start | bytes 6291464 | tf_op jit(solution)/shard_map/ppermute | solution.py:245
  11.1 13.1 %collective-permute-start.7 = (bf16[64,2176]{1,0:T(8,128)(2,1)S(1)}, bf16[64,2176]{1,0:T(8,128)(2,1)S(1)}, u32[]{:S(2)}, u32[]{:S(2)}) collective-permute-start(bf16[64,2176]{1,0:T(8,128)(2,1)S(1)} %get-tuple-element.97.payload), channel_id=1, source_target_pairs={{0,8},{8,0},{16,24},{24,16},{1,9},{9,1},{17,25},{25,17},{2,10},{10... | collective-permute-start | bytes 835592 | tf_op jit(solution)/shard_map/ppermute | solution.py:245
  14.1 13.5 %collective-permute-start.3 = (bf16[40,2048]{1,0:T(8,128)(2,1)S(1)}, bf16[40,2048]{1,0:T(8,128)(2,1)S(1)}, u32[]{:S(2)}, u32[]{:S(2)}) collective-permute-start(bf16[40,2048]{1,0:T(8,128)(2,1)S(1)} %get-tuple-element.102), channel_id=1, source_target_pairs={{0,2},{2,0},{4,6},{6,4},{1,3},{3,1},{5,7},{7,5},{8,10},{10,8},{12,... | collective-permute-start | bytes 491528 | tf_op jit(solution)/shard_map/ppermute | solution.py:245
  15.6 12.6 %collective-permute-start.4 = (bf16[40,2048]{1,0:T(8,128)(2,1)S(1)}, bf16[40,2048]{1,0:T(8,128)(2,1)S(1)}, u32[]{:S(2)}, u32[]{:S(2)}) collective-permute-start(bf16[40,2048]{1,0:T(8,128)(2,1)S(1)} %get-tuple-element.103), channel_id=1, source_target_pairs={{0,4},{2,6},{4,0},{6,2},{1,5},{3,7},{5,1},{7,3},{8,12},{10,14},{12... | collective-permute-start | bytes 491528 | tf_op jit(solution)/shard_map/ppermute | solution.py:245
  17.1 11.4 %collective-permute-start.5 = (bf16[40,2048]{1,0:T(8,128)(2,1)S(1)}, bf16[40,2048]{1,0:T(8,128)(2,1)S(1)}, u32[]{:S(2)}, u32[]{:S(2)}) collective-permute-start(bf16[40,2048]{1,0:T(8,128)(2,1)S(1)} %get-tuple-element.104), channel_id=1, source_target_pairs={{0,6},{2,4},{4,2},{6,0},{1,7},{3,5},{5,3},{7,1},{8,14},{10,12},{12... | collective-permute-start | bytes 491528 | tf_op jit(solution)/shard_map/ppermute | solution.py:245
  17.6 15.0 %collective-permute-start.6 = (bf16[64,2176]{1,0:T(8,128)(2,1)S(1)}, bf16[64,2176]{1,0:T(8,128)(2,1)S(1)}, u32[]{:S(2)}, u32[]{:S(2)}) collective-permute-start(bf16[64,2176]{1,0:T(8,128)(2,1)S(1)} %get-tuple-element.97.payload), channel_id=1, source_target_pairs={{0,16},{8,24},{16,0},{24,8},{1,17},{9,25},{17,1},{25,9},{2,18},{10... | collective-permute-start | bytes 835592 | tf_op jit(solution)/shard_map/ppermute | solution.py:245
  24.9 9.8 %collective-permute-start.10 = (bf16[40,2048]{1,0:T(8,128)(2,1)S(1)}, bf16[40,2048]{1,0:T(8,128)(2,1)S(1)}, u32[]{:S(2)}, u32[]{:S(2)}) collective-permute-start(bf16[40,2048]{1,0:T(8,128)(2,1)S(1)} %get-tuple-element.116), channel_id=1, source_target_pairs={{0,6},{2,4},{4,2},{6,0},{1,7},{3,5},{5,3},{7,1},{8,14},{10,12},{12... | collective-permute-start | bytes 491528 | tf_op jit(solution)/shard_map/ppermute | solution.py:245
  27.6 9.7 %collective-permute-start.8 = (bf16[40,2048]{1,0:T(8,128)(2,1)S(1)}, bf16[40,2048]{1,0:T(8,128)(2,1)S(1)}, u32[]{:S(2)}, u32[]{:S(2)}) collective-permute-start(bf16[40,2048]{1,0:T(8,128)(2,1)S(1)} %get-tuple-element.114), channel_id=1, source_target_pairs={{0,2},{2,0},{4,6},{6,4},{1,3},{3,1},{5,7},{7,5},{8,10},{10,8},{12,... | collective-permute-start | bytes 491528 | tf_op jit(solution)/shard_map/ppermute | solution.py:245
  28.1 10.1 %collective-permute-start.9 = (bf16[40,2048]{1,0:T(8,128)(2,1)S(1)}, bf16[40,2048]{1,0:T(8,128)(2,1)S(1)}, u32[]{:S(2)}, u32[]{:S(2)}) collective-permute-start(bf16[40,2048]{1,0:T(8,128)(2,1)S(1)} %get-tuple-element.115), channel_id=1, source_target_pairs={{0,4},{2,6},{4,0},{6,2},{1,5},{3,7},{5,1},{7,3},{8,12},{10,14},{12... | collective-permute-start | bytes 491528 | tf_op jit(solution)/shard_map/ppermute | solution.py:245
  30.8 8.4 %collective-permute-start.11 = (bf16[40,2048]{1,0:T(8,128)(2,1)S(1)}, bf16[40,2048]{1,0:T(8,128)(2,1)S(1)}, u32[]{:S(2)}, u32[]{:S(2)}) collective-permute-start(bf16[40,2048]{1,0:T(8,128)(2,1)S(1)} %get-tuple-element.130), channel_id=1, source_target_pairs={{0,2},{2,0},{4,6},{6,4},{1,3},{3,1},{5,7},{7,5},{8,10},{10,8},{12,... | collective-permute-start | bytes 491528 | tf_op jit(solution)/shard_map/ppermute | solution.py:245
  32.6 8.2 %collective-permute-start.12 = (bf16[40,2048]{1,0:T(8,128)(2,1)S(1)}, bf16[40,2048]{1,0:T(8,128)(2,1)S(1)}, u32[]{:S(2)}, u32[]{:S(2)}) collective-permute-start(bf16[40,2048]{1,0:T(8,128)(2,1)S(1)} %get-tuple-element.131), channel_id=1, source_target_pairs={{0,4},{2,6},{4,0},{6,2},{1,5},{3,7},{5,1},{7,3},{8,12},{10,14},{12... | collective-permute-start | bytes 491528 | tf_op jit(solution)/shard_map/ppermute | solution.py:245
  34.8 11.7 %collective-permute-start.14 = (bf16[64,2176]{1,0:T(8,128)(2,1)S(1)}, bf16[64,2176]{1,0:T(8,128)(2,1)S(1)}, u32[]{:S(2)}, u32[]{:S(2)}) collective-permute-start(bf16[64,2176]{1,0:T(8,128)(2,1)S(1)} %get-tuple-element.97.payload), channel_id=1, source_target_pairs={{0,24},{8,16},{16,8},{24,0},{1,25},{9,17},{17,9},{25,1},{2,26},{10... | collective-permute-start | bytes 835592 | tf_op jit(solution)/shard_map/ppermute | solution.py:245
  37.3 8.1 %collective-permute-start.13 = (bf16[40,2048]{1,0:T(8,128)(2,1)S(1)}, bf16[40,2048]{1,0:T(8,128)(2,1)S(1)}, u32[]{:S(2)}, u32[]{:S(2)}) collective-permute-start(bf16[40,2048]{1,0:T(8,128)(2,1)S(1)} %get-tuple-element.132), channel_id=1, source_target_pairs={{0,6},{2,4},{4,2},{6,0},{1,7},{3,5},{5,3},{7,1},{8,14},{10,12},{12... | collective-permute-start | bytes 491528 | tf_op jit(solution)/shard_map/ppermute | solution.py:245
  38.2 9.7 %collective-permute-start.15 = (bf16[40,2048]{1,0:T(8,128)(2,1)S(1)}, bf16[40,2048]{1,0:T(8,128)(2,1)S(1)}, u32[]{:S(2)}, u32[]{:S(2)}) collective-permute-start(bf16[40,2048]{1,0:T(8,128)(2,1)S(1)} %get-tuple-element.143), channel_id=1, source_target_pairs={{0,2},{2,0},{4,6},{6,4},{1,3},{3,1},{5,7},{7,5},{8,10},{10,8},{12,... | collective-permute-start | bytes 491528 | tf_op jit(solution)/shard_map/ppermute | solution.py:245
  39.3 10.6 %collective-permute-start.16 = (bf16[40,2048]{1,0:T(8,128)(2,1)S(1)}, bf16[40,2048]{1,0:T(8,128)(2,1)S(1)}, u32[]{:S(2)}, u32[]{:S(2)}) collective-permute-start(bf16[40,2048]{1,0:T(8,128)(2,1)S(1)} %get-tuple-element.144), channel_id=1, source_target_pairs={{0,4},{2,6},{4,0},{6,2},{1,5},{3,7},{5,1},{7,3},{8,12},{10,14},{12... | collective-permute-start | bytes 491528 | tf_op jit(solution)/shard_map/ppermute | solution.py:245
  40.8 11.7 %collective-permute-start.17 = (bf16[40,2048]{1,0:T(8,128)(2,1)S(1)}, bf16[40,2048]{1,0:T(8,128)(2,1)S(1)}, u32[]{:S(2)}, u32[]{:S(2)}) collective-permute-start(bf16[40,2048]{1,0:T(8,128)(2,1)S(1)} %get-tuple-element.145), channel_id=1, source_target_pairs={{0,6},{2,4},{4,2},{6,0},{1,7},{3,5},{5,3},{7,1},{8,14},{10,12},{12... | collective-permute-start | bytes 491528 | tf_op jit(solution)/shard_map/ppermute | solution.py:245
  45.4 9.6 %collective-permute-start.21 = (bf16[40,2048]{1,0:T(8,128)(2,1)S(1)}, bf16[40,2048]{1,0:T(8,128)(2,1)S(1)}, u32[]{:S(2)}, u32[]{:S(2)}) collective-permute-start(bf16[40,2048]{1,0:T(8,128)(2,1)S(1)} %get-tuple-element.168), channel_id=1, source_target_pairs={{0,2},{2,0},{4,6},{6,4},{1,3},{3,1},{5,7},{7,5},{8,10},{10,8},{12,... | collective-permute-start | bytes 491528 | tf_op jit(solution)/shard_map/ppermute | solution.py:245
  47.1 12.2 %collective-permute-start.22 = (bf16[40,2048]{1,0:T(8,128)(2,1)S(1)}, bf16[40,2048]{1,0:T(8,128)(2,1)S(1)}, u32[]{:S(2)}, u32[]{:S(2)}) collective-permute-start(bf16[40,2048]{1,0:T(8,128)(2,1)S(1)} %get-tuple-element.169), channel_id=1, source_target_pairs={{0,4},{2,6},{4,0},{6,2},{1,5},{3,7},{5,1},{7,3},{8,12},{10,14},{12... | collective-permute-start | bytes 491528 | tf_op jit(solution)/shard_map/ppermute | solution.py:245
  47.9 11.6 %collective-permute-start.23 = (bf16[40,2048]{1,0:T(8,128)(2,1)S(1)}, bf16[40,2048]{1,0:T(8,128)(2,1)S(1)}, u32[]{:S(2)}, u32[]{:S(2)}) collective-permute-start(bf16[40,2048]{1,0:T(8,128)(2,1)S(1)} %get-tuple-element.170), channel_id=1, source_target_pairs={{0,6},{2,4},{4,2},{6,0},{1,7},{3,5},{5,3},{7,1},{8,14},{10,12},{12... | collective-permute-start | bytes 491528 | tf_op jit(solution)/shard_map/ppermute | solution.py:245
  52.5 9.6 %collective-permute-start.18 = (bf16[40,2048]{1,0:T(8,128)(2,1)S(1)}, bf16[40,2048]{1,0:T(8,128)(2,1)S(1)}, u32[]{:S(2)}, u32[]{:S(2)}) collective-permute-start(bf16[40,2048]{1,0:T(8,128)(2,1)S(1)} %get-tuple-element.152), channel_id=1, source_target_pairs={{0,2},{2,0},{4,6},{6,4},{1,3},{3,1},{5,7},{7,5},{8,10},{10,8},{12,... | collective-permute-start | bytes 491528 | tf_op jit(solution)/shard_map/ppermute | solution.py:245
  53.5 10.1 %collective-permute-start.19 = (bf16[40,2048]{1,0:T(8,128)(2,1)S(1)}, bf16[40,2048]{1,0:T(8,128)(2,1)S(1)}, u32[]{:S(2)}, u32[]{:S(2)}) collective-permute-start(bf16[40,2048]{1,0:T(8,128)(2,1)S(1)} %get-tuple-element.153), channel_id=1, source_target_pairs={{0,4},{2,6},{4,0},{6,2},{1,5},{3,7},{5,1},{7,3},{8,12},{10,14},{12... | collective-permute-start | bytes 491528 | tf_op jit(solution)/shard_map/ppermute | solution.py:245
  55.0 11.6 %collective-permute-start.20 = (bf16[40,2048]{1,0:T(8,128)(2,1)S(1)}, bf16[40,2048]{1,0:T(8,128)(2,1)S(1)}, u32[]{:S(2)}, u32[]{:S(2)}) collective-permute-start(bf16[40,2048]{1,0:T(8,128)(2,1)S(1)} %get-tuple-element.154), channel_id=1, source_target_pairs={{0,6},{2,4},{4,2},{6,0},{1,7},{3,5},{5,3},{7,1},{8,14},{10,12},{12... | collective-permute-start | bytes 491528 | tf_op jit(solution)/shard_map/ppermute | solution.py:245
  60.2 9.0 %collective-permute-start.24 = (bf16[64,2048]{1,0:T(8,128)(2,1)S(1)}, bf16[64,2048]{1,0:T(8,128)(2,1)S(1)}, u32[]{:S(2)}, u32[]{:S(2)}) collective-permute-start(bf16[64,2048]{1,0:T(8,128)(2,1)S(1)} %combine.3), channel_id=1, source_target_pairs={{0,8},{8,0},{16,24},{24,16},{1,9},{9,1},{17,25},{25,17},{2,10},{10... | collective-permute-start | bytes 786440 | tf_op jit(solution)/shard_map/ppermute | solution.py:245
  60.3 10.4 %collective-permute-start.25 = (bf16[40,2048]{1,0:T(8,128)(2,1)S(1)}, bf16[40,2048]{1,0:T(8,128)(2,1)S(1)}, u32[]{:S(2)}, u32[]{:S(2)}) collective-permute-start(bf16[40,2048]{1,0:T(8,128)(2,1)S(1)} %get-tuple-element.174), channel_id=1, source_target_pairs={{0,2},{2,0},{4,6},{6,4},{1,3},{3,1},{5,7},{7,5},{8,10},{10,8},{12,... | collective-permute-start | bytes 491528 | tf_op jit(solution)/shard_map/ppermute | solution.py:245
  62.1 10.7 %collective-permute-start.26 = (bf16[40,2048]{1,0:T(8,128)(2,1)S(1)}, bf16[40,2048]{1,0:T(8,128)(2,1)S(1)}, u32[]{:S(2)}, u32[]{:S(2)}) collective-permute-start(bf16[40,2048]{1,0:T(8,128)(2,1)S(1)} %get-tuple-element.175), channel_id=1, source_target_pairs={{0,4},{2,6},{4,0},{6,2},{1,5},{3,7},{5,1},{7,3},{8,12},{10,14},{12... | collective-permute-start | bytes 491528 | tf_op jit(solution)/shard_map/ppermute | solution.py:245
  63.6 10.0 %collective-permute-start.27 = (bf16[40,2048]{1,0:T(8,128)(2,1)S(1)}, bf16[40,2048]{1,0:T(8,128)(2,1)S(1)}, u32[]{:S(2)}, u32[]{:S(2)}) collective-permute-start(bf16[40,2048]{1,0:T(8,128)(2,1)S(1)} %get-tuple-element.176), channel_id=1, source_target_pairs={{0,6},{2,4},{4,2},{6,0},{1,7},{3,5},{5,3},{7,1},{8,14},{10,12},{12... | collective-permute-start | bytes 491528 | tf_op jit(solution)/shard_map/ppermute | solution.py:245
  70.3 7.1 %collective-permute-start.30 = (bf16[40,2048]{1,0:T(8,128)(2,1)S(1)}, bf16[40,2048]{1,0:T(8,128)(2,1)S(1)}, u32[]{:S(2)}, u32[]{:S(2)}) collective-permute-start(bf16[40,2048]{1,0:T(8,128)(2,1)S(1)} %get-tuple-element.179), channel_id=1, source_target_pairs={{0,4},{2,6},{4,0},{6,2},{1,5},{3,7},{5,1},{7,3},{8,12},{10,14},{12... | collective-permute-start | bytes 491528 | tf_op jit(solution)/shard_map/ppermute | solution.py:245
  70.6 6.7 %collective-permute-start.31 = (bf16[40,2048]{1,0:T(8,128)(2,1)S(1)}, bf16[40,2048]{1,0:T(8,128)(2,1)S(1)}, u32[]{:S(2)}, u32[]{:S(2)}) collective-permute-start(bf16[40,2048]{1,0:T(8,128)(2,1)S(1)} %get-tuple-element.180), channel_id=1, source_target_pairs={{0,6},{2,4},{4,2},{6,0},{1,7},{3,5},{5,3},{7,1},{8,14},{10,12},{12... | collective-permute-start | bytes 491528 | tf_op jit(solution)/shard_map/ppermute | solution.py:245
  74.2 16.7 %collective-permute-start.28 = (bf16[64,2048]{1,0:T(8,128)(2,1)S(1)}, bf16[64,2048]{1,0:T(8,128)(2,1)S(1)}, u32[]{:S(2)}, u32[]{:S(2)}) collective-permute-start(bf16[64,2048]{1,0:T(8,128)(2,1)S(1)} %combine.4), channel_id=1, source_target_pairs={{0,16},{8,24},{16,0},{24,8},{1,17},{9,25},{17,1},{25,9},{2,18},{10... | collective-permute-start | bytes 786440 | tf_op jit(solution)/shard_map/ppermute | solution.py:245
  77.9 12.9 %collective-permute-start.32 = (bf16[64,2048]{1,0:T(8,128)(2,1)S(1)}, bf16[64,2048]{1,0:T(8,128)(2,1)S(1)}, u32[]{:S(2)}, u32[]{:S(2)}) collective-permute-start(bf16[64,2048]{1,0:T(8,128)(2,1)S(1)} %combine.5), channel_id=1, source_target_pairs={{0,24},{8,16},{16,8},{24,0},{1,25},{9,17},{17,9},{25,1},{2,26},{10... | collective-permute-start | bytes 786440 | tf_op jit(solution)/shard_map/ppermute | solution.py:245
  (4 other events, 84.6 us)

commit v5 on v4

--- a/solution.py
+++ b/solution.py
@@ -201,9 +201,12 @@
     write.wait()
 
 
-def combine_kernel(chips, capacity, experts, features, payload, *refs):
+def combine_kernel(chips, capacity, experts, features, counts, payload, *refs):
     weights = unpacked(payload, features, experts)
-    refs[-1][...] = combined(refs[:-1], weights, chips, capacity).astype(jnp.bfloat16)
+    total = combined(refs[:counts], weights, chips, capacity)
+    for ref in refs[counts:-1]:
+        total = total + ref[...].astype(jnp.float32)
+    refs[-1][...] = total.astype(jnp.bfloat16)
 
 
 def own_kernel(chips, capacity, experts, features, payload, stream, *refs):
@@ -219,9 +222,9 @@
 HBM_SPEC = pl.BlockSpec(memory_space=pltpu.HBM)
 
 
-Z_FIRST = (1, 2, 3)
-ORDER = (("in", 0), ("in", 1), ("out", 0), ("in", 2), ("out", 1), ("in", 3), ("out", 2), ("out", 3))
+ORDER = (("in", 0), ("out", 0), ("in", 3), ("in", 1), ("out", 3), ("in", 2), ("out", 2), ("out", 1))
 LAG = 2
+DUE = {}
 
 
 def shards(
@@ -336,26 +339,30 @@
         )(lengths, *held, *before, *arrived, *halves)
         return results, appended
 
-    def combine(packed, returned):
+    def combine(packed, returned, extra):
         return pl.pallas_call(
-            functools.partial(combine_kernel, chips, capacity, experts, features),
+            functools.partial(combine_kernel, chips, capacity, experts, features, blocks_n),
             out_shape=jax.ShapeDtypeStruct((group, features), bf16),
-            in_specs=in_vmem(1 + blocks_n),
+            in_specs=in_vmem(1 + blocks_n + len(extra)),
             out_specs=pl.BlockSpec(memory_space=VMEM),
             compiler_params=params(8),
             name="combine",
-        )(packed, *returned)
-
-    payload_of = {0: payload}
+        )(packed, *returned, *extra)
+
+    payload_of = {0: payload, 1: across(payload, "req", 1), 3: across(payload, "req", 3)}
+    payload_of[2] = across(payload_of[3], "req", 1)
     calls, appended = 0, None
-    for s in Z_FIRST:
-        payload_of[s] = across(payload, "req", s)
-    arrived_of, returned_of, partials, moved, due = {}, {}, [], [], []
+    arrived_of, returned_of, partials, moved = {}, {}, {}, []
+
+    def send_back(s, hold):
+        extra = [partials.pop(3)] if s == 2 else []
+        partial = combine(payload_of[s], returned_of.pop(s), extra)
+        hold, partial = lax.optimization_barrier((hold, partial))
+        partials[s] = across(partial, "req", 2 if s == 2 else 1)
+        return hold
+
     for k, (way, s) in enumerate(ORDER):
         if way == "in":
-            if s not in payload_of:
-                later, moved[-1] = lax.optimization_barrier((payload, moved[-1]))
-                payload_of[s] = across(later, "req", s)
             blocks = outgoing if s == 0 else gather(payload_of[s])
         else:
             blocks, appended = run_experts(arrived_of[s], calls, appended)
@@ -363,23 +370,18 @@
         if k >= LAG:
             pw, ps = ORDER[k - LAG]
             if pw == "out" and ps > 0:
-                partial = combine(payload_of[ps], moved[k - LAG])
-                blocks, partial = lax.optimization_barrier((blocks, partial))
-                due.append(({1: 7, 2: 99, 3: 99}[ps], len(partials)))
-                partials.append(across(partial, "req", ps))
-                returned_of.pop(ps)
+                blocks = send_back(ps, blocks)
             else:
-                blocks, moved[k - LAG] = lax.optimization_barrier((blocks, moved[k - LAG]))
-                (arrived_of if pw == "in" else returned_of)[ps] = moved[k - LAG]
-        while due and due[0][0] <= k:
-            at = due.pop(0)[1]
-            blocks, partials[at] = lax.optimization_barrier((blocks, partials[at]))
+                blocks, got = lax.optimization_barrier((blocks, moved[k - LAG]))
+                (arrived_of if pw == "in" else returned_of)[ps] = got
+        if k in DUE:
+            blocks, partials[DUE[k]] = lax.optimization_barrier((blocks, partials[DUE[k]]))
         got = joined(to_chips(cut(blocks)))
         moved.append(got)
         (arrived_of if way == "in" else returned_of)[s] = got
-    for s in sorted(returned_of):
-        if s > 0:
-            partials.append(across(combine(payload_of[s], returned_of[s]), "req", s))
+    for way, s in ORDER:
+        if way == "out" and s > 0 and s in returned_of:
+            send_back(s, ())
     own_returned = returned_of[0]
     total = pl.pallas_call(
         functools.partial(own_kernel, chips, capacity, experts, features),
@@ -389,7 +391,7 @@
         compiler_params=params(8),
         name="own",
     )(payload, stream, *own_returned)
-    for partial in partials:
+    for partial in partials.values():
         total = total + partial.astype(jnp.float32)
     layer_out = total.astype(bf16)
     return (layer_out[None], appended[None])

time: 92.2 us -> 90.6 us (0.983)
  waiting for transfers between devices: 25.5 us -> 23 us
    ppermute x33, waiting for transfers between devices: 25.5 us -> 23 us  [across(): return lax.ppermute(x, axis, [(i, i ^ j) for i in range(size)])]
  transfers between devices with their start and end apart: 33 -> 33, of which waited for: 12 -> 13; matrix products, arithmetic and copies ran while one was open for 0% -> 0% of each run, Pallas kernels for 23% -> 23%
where the time goes in v5:
time: 90.6 us; the launch traced here: 89.9 us
  starting transfers between devices  43.5 us (48%)
  waiting for transfers between devices  23 us (25%)
  Pallas kernels  21.1 us (23%)
  between operations  1.47 us (2%)
    ppermute x33, starting transfers between devices, across(): return lax.ppermute(x, axis, [(i, i ^ j) for i in range(size)])  43.5 us
    ppermute x33, waiting for transfers between devices, across(): return lax.ppermute(x, axis, [(i, i ^ j) for i in range(size)])  23 us
    pallas_call x4, Pallas kernels, run_experts(): pl.pallas_call(functools.partial(expert_kernel, capacity, blocks_n, spans...  9.5 us
    pallas_call x1, Pallas kernels, shards(): pl.pallas_call(functools.partial(attention_kernel, chips, capacity, exper...  7.23 us
    pallas_call x3, Pallas kernels, gather(): pl.pallas_call(functools.partial(gather_kernel, chips, capacity, experts,...  1.98 us
  transfers between devices with their start and end apart: 33, of which 13 were waited for; matrix products, arithmetic and copies ran while one was open for 0% of the time, Pallas kernels for 23%

profile of v5, /device:TPU:0, one launch (start us, length us, event | category | flops | bytes accessed | tf_op | source)
XLA Modules:
  0.0 89.9 jit_solution(13079564344664946052)
XLA Ops:
  2.3 7.2 %attention.1 = (f32[64,2048]{1,0:T(8,128)S(1)}, bf16[64,2176]{1,0:T(8,128)(2,1)S(1)}, bf16[512,2,2048]{2,1,0:T(2,128)(2,1)S(1)}, bf16[64,2,2048]{2,1,0:T(2,128)(...) custom-call(s32[1]{0:T(128)S(6)} %copy.20.length, ...), custom_call_target="tpu_custom_call" | custom-call | flops 12000000000 | bytes 25165824 | tf_op jit(solution)/shard_map/attention/pallas_call | solution.py:268
  9.6 1.5 %collective-permute-done.2.refs_9_.refs_10_ = bf16[512,2048]{1,0:T(8,128)(2,1)S(1)} collective-permute-done((bf16[512,2048]{1,0:T(8,128)(2,1)}, bf16[512,2048]{1,0:T(8,128)(2,1)S(1)}, u32[]{:S(2)}, u32[]{:S(2)}) %collective-permute-start.2) | collective-permute-done | bytes 2097184 | tf_op jit(solution)/shard_map/ppermute | solution.py:248
  11.1 2.9 %collective-permute-start.4 = (bf16[40,2048]{1,0:T(8,128)(2,1)S(1)}, bf16[40,2048]{1,0:T(8,128)(2,1)S(1)}, u32[]{:S(2)}, u32[]{:S(2)}) collective-permute-start(bf16[40,2048]{1,0:T(8,128)(2,1)S(1)} %get-tuple-element.97), channel_id=1, source_target_pairs={{0,2},{2,0},{4,6},{6,4},{1,3},{3,1},{5,7},{7,5},{8,10},{10,8},{12,... | collective-permute-start | bytes 491528 | tf_op jit(solution)/shard_map/ppermute | solution.py:248
  14.0 1.5 %collective-permute-start.5 = (bf16[40,2048]{1,0:T(8,128)(2,1)S(1)}, bf16[40,2048]{1,0:T(8,128)(2,1)S(1)}, u32[]{:S(2)}, u32[]{:S(2)}) collective-permute-start(bf16[40,2048]{1,0:T(8,128)(2,1)S(1)} %get-tuple-element.98), channel_id=1, source_target_pairs={{0,4},{2,6},{4,0},{6,2},{1,5},{3,7},{5,1},{7,3},{8,12},{10,14},{12... | collective-permute-start | bytes 491528 | tf_op jit(solution)/shard_map/ppermute | solution.py:248
  15.5 4.1 %collective-permute-start.10 = (bf16[64,2176]{1,0:T(8,128)(2,1)S(1)}, bf16[64,2176]{1,0:T(8,128)(2,1)S(1)}, u32[]{:S(2)}, u32[]{:S(2)}) collective-permute-start(bf16[64,2176]{1,0:T(8,128)(2,1)S(1)} %get-tuple-element.88.payload), channel_id=1, source_target_pairs={{0,24},{8,16},{16,8},{24,0},{1,25},{9,17},{17,9},{25,1},{2,26},{10... | collective-permute-start | bytes 835592 | tf_op jit(solution)/shard_map/ppermute | solution.py:248
  19.6 3.9 %collective-permute-done.5.refs_2_ = bf16[40,2048]{1,0:T(8,128)(2,1)S(1)} collective-permute-done((bf16[40,2048]{1,0:T(8,128)(2,1)S(1)}, bf16[40,2048]{1,0:T(8,128)(2,1)S(1)}, u32[]{:S(2)}, u32[]{:S(2)}) %collective-permute-start.5) | collective-permute-done | bytes 163872 | tf_op jit(solution)/shard_map/ppermute | solution.py:248
  23.5 2.3 %experts.4 = (bf16[40,2048]{1,0:T(8,128)(2,1)S(1)}, bf16[40,2048]{1,0:T(8,128)(2,1)S(1)}, bf16[40,2048]{1,0:T(8,128)(2,1)S(1)}, bf16[40,2048]{1,0:T(8,128)(2,1)S(1)}, bf16[512,2,2048]{2,1,0:T(2,128)(2,1)}) custom-call(s32[1]{0:T(128)S(6)} %copy.20.length, bf16[512,2,2048]{2,1,0:T(2,128)(2,1)S(1)} %get-tuple-element.94.cached, ...), custom_call_target="tpu_custom_call" | custom-call | flops 2013265920 | bytes 12582912 | tf_op jit(solution)/shard_map/experts/pallas_call | solution.py:325
  25.8 1.3 %collective-permute-start.7 = (bf16[40,2048]{1,0:T(8,128)(2,1)S(1)}, bf16[40,2048]{1,0:T(8,128)(2,1)S(1)}, u32[]{:S(2)}, u32[]{:S(2)}) collective-permute-start(bf16[40,2048]{1,0:T(8,128)(2,1)S(1)} %get-tuple-element.104), channel_id=1, source_target_pairs={{0,2},{2,0},{4,6},{6,4},{1,3},{3,1},{5,7},{7,5},{8,10},{10,8},{12,... | collective-permute-start | bytes 491528 | tf_op jit(solution)/shard_map/ppermute | solution.py:248
  28.0 1.4 %collective-permute-start.9 = (bf16[40,2048]{1,0:T(8,128)(2,1)S(1)}, bf16[40,2048]{1,0:T(8,128)(2,1)S(1)}, u32[]{:S(2)}, u32[]{:S(2)}) collective-permute-start(bf16[40,2048]{1,0:T(8,128)(2,1)S(1)} %get-tuple-element.106), channel_id=1, source_target_pairs={{0,6},{2,4},{4,2},{6,0},{1,7},{3,5},{5,3},{7,1},{8,14},{10,12},{12... | collective-permute-start | bytes 491528 | tf_op jit(solution)/shard_map/ppermute | solution.py:248
  29.4 2.0 %collective-permute-start.11 = (bf16[64,2176]{1,0:T(8,128)(2,1)S(1)}, bf16[64,2176]{1,0:T(8,128)(2,1)S(1)}, u32[]{:S(2)}, u32[]{:S(2)}) collective-permute-start(bf16[64,2176]{1,0:T(8,128)(2,1)S(1)} %collective-permute-done.10.payload), channel_id=1, source_target_pairs={{0,8},{8,0},{16,24},{24,16},{1,9},{9,1},{17,25},{25,17},{2,10},{10... | collective-permute-start | bytes 835592 | tf_op jit(solution)/shard_map/ppermute | solution.py:248
  32.6 3.2 %collective-permute-done.8.refs_2_ = bf16[40,2048]{1,0:T(8,128)(2,1)S(1)} collective-permute-done((bf16[40,2048]{1,0:T(8,128)(2,1)S(1)}, bf16[40,2048]{1,0:T(8,128)(2,1)S(1)}, u32[]{:S(2)}, u32[]{:S(2)}) %collective-permute-start.8) | collective-permute-done | bytes 163872 | tf_op jit(solution)/shard_map/ppermute | solution.py:248
  36.7 1.3 %collective-permute-start.16 = (bf16[40,2048]{1,0:T(8,128)(2,1)S(1)}, bf16[40,2048]{1,0:T(8,128)(2,1)S(1)}, u32[]{:S(2)}, u32[]{:S(2)}) collective-permute-start(bf16[40,2048]{1,0:T(8,128)(2,1)S(1)} %get-tuple-element.127), channel_id=1, source_target_pairs={{0,4},{2,6},{4,0},{6,2},{1,5},{3,7},{5,1},{7,3},{8,12},{10,14},{12... | collective-permute-start | bytes 491528 | tf_op jit(solution)/shard_map/ppermute | solution.py:248
  37.9 1.4 %collective-permute-start.17 = (bf16[40,2048]{1,0:T(8,128)(2,1)S(1)}, bf16[40,2048]{1,0:T(8,128)(2,1)S(1)}, u32[]{:S(2)}, u32[]{:S(2)}) collective-permute-start(bf16[40,2048]{1,0:T(8,128)(2,1)S(1)} %get-tuple-element.128), channel_id=1, source_target_pairs={{0,6},{2,4},{4,2},{6,0},{1,7},{3,5},{5,3},{7,1},{8,14},{10,12},{12... | collective-permute-start | bytes 491528 | tf_op jit(solution)/shard_map/ppermute | solution.py:248
  40.9 2.0 %collective-permute-done.15.refs_2_ = bf16[40,2048]{1,0:T(8,128)(2,1)S(1)} collective-permute-done((bf16[40,2048]{1,0:T(8,128)(2,1)S(1)}, bf16[40,2048]{1,0:T(8,128)(2,1)S(1)}, u32[]{:S(2)}, u32[]{:S(2)}) %collective-permute-start.15) | collective-permute-done | bytes 163872 | tf_op jit(solution)/shard_map/ppermute | solution.py:248
  43.7 1.6 %collective-permute-start.14 = (bf16[40,2048]{1,0:T(8,128)(2,1)S(1)}, bf16[40,2048]{1,0:T(8,128)(2,1)S(1)}, u32[]{:S(2)}, u32[]{:S(2)}) collective-permute-start(bf16[40,2048]{1,0:T(8,128)(2,1)S(1)} %get-tuple-element.119), channel_id=1, source_target_pairs={{0,6},{2,4},{4,2},{6,0},{1,7},{3,5},{5,3},{7,1},{8,14},{10,12},{12... | collective-permute-start | bytes 491528 | tf_op jit(solution)/shard_map/ppermute | solution.py:248
  46.8 1.2 %collective-permute-start.18 = (bf16[40,2048]{1,0:T(8,128)(2,1)S(1)}, bf16[40,2048]{1,0:T(8,128)(2,1)S(1)}, u32[]{:S(2)}, u32[]{:S(2)}) collective-permute-start(bf16[40,2048]{1,0:T(8,128)(2,1)S(1)} %get-tuple-element.130), channel_id=1, source_target_pairs={{0,2},{2,0},{4,6},{6,4},{1,3},{3,1},{5,7},{7,5},{8,10},{10,8},{12,... | collective-permute-start | bytes 491528 | tf_op jit(solution)/shard_map/ppermute | solution.py:248
  49.9 1.6 %collective-permute-start.20 = (bf16[40,2048]{1,0:T(8,128)(2,1)S(1)}, bf16[40,2048]{1,0:T(8,128)(2,1)S(1)}, u32[]{:S(2)}, u32[]{:S(2)}) collective-permute-start(bf16[40,2048]{1,0:T(8,128)(2,1)S(1)} %get-tuple-element.132), channel_id=1, source_target_pairs={{0,6},{2,4},{4,2},{6,0},{1,7},{3,5},{5,3},{7,1},{8,14},{10,12},{12... | collective-permute-start | bytes 491528 | tf_op jit(solution)/shard_map/ppermute | solution.py:248
  51.5 2.4 %collective-permute-done.13.refs_3_ = bf16[40,2048]{1,0:T(8,128)(2,1)S(1)} collective-permute-done((bf16[40,2048]{1,0:T(8,128)(2,1)S(1)}, bf16[40,2048]{1,0:T(8,128)(2,1)S(1)}, u32[]{:S(2)}, u32[]{:S(2)}) %collective-permute-start.13) | collective-permute-done | bytes 163872 | tf_op jit(solution)/shard_map/ppermute | solution.py:248
  53.9 2.3 %experts.5 = (bf16[40,2048]{1,0:T(8,128)(2,1)S(1)}, bf16[40,2048]{1,0:T(8,128)(2,1)S(1)}, bf16[40,2048]{1,0:T(8,128)(2,1)S(1)}, bf16[40,2048]{1,0:T(8,128)(2,1)S(1)}, bf16[512,2,2048]{2,1,0:T(2,128)(2,1)}) custom-call(s32[1]{0:T(128)S(6)} %copy.20.length, bf16[512,2,2048]{2,1,0:T(2,128)(2,1)S(1)} %get-tuple-element.94.cached, ...), custom_call_target="tpu_custom_call", output_to_operand_aliasing={{4}: (3, {})} | custom-call | flops 2013265920 | bytes 12582912 | tf_op jit(solution)/shard_map/experts/pallas_call | solution.py:325
  56.3 1.3 %collective-permute-start.21 = (bf16[40,2048]{1,0:T(8,128)(2,1)S(1)}, bf16[40,2048]{1,0:T(8,128)(2,1)S(1)}, u32[]{:S(2)}, u32[]{:S(2)}) collective-permute-start(bf16[40,2048]{1,0:T(8,128)(2,1)S(1)} %get-tuple-element.142), channel_id=1, source_target_pairs={{0,2},{2,0},{4,6},{6,4},{1,3},{3,1},{5,7},{7,5},{8,10},{10,8},{12,... | collective-permute-start | bytes 491528 | tf_op jit(solution)/shard_map/ppermute | solution.py:248
  58.5 1.4 %collective-permute-start.23 = (bf16[40,2048]{1,0:T(8,128)(2,1)S(1)}, bf16[40,2048]{1,0:T(8,128)(2,1)S(1)}, u32[]{:S(2)}, u32[]{:S(2)}) collective-permute-start(bf16[40,2048]{1,0:T(8,128)(2,1)S(1)} %get-tuple-element.144), channel_id=1, source_target_pairs={{0,6},{2,4},{4,2},{6,0},{1,7},{3,5},{5,3},{7,1},{8,14},{10,12},{12... | collective-permute-start | bytes 491528 | tf_op jit(solution)/shard_map/ppermute | solution.py:248
  60.9 2.3 %experts.6 = (bf16[40,2048]{1,0:T(8,128)(2,1)S(1)}, bf16[40,2048]{1,0:T(8,128)(2,1)S(1)}, bf16[40,2048]{1,0:T(8,128)(2,1)S(1)}, bf16[40,2048]{1,0:T(8,128)(2,1)S(1)}, bf16[512,2,2048]{2,1,0:T(2,128)(2,1)}) custom-call(s32[1]{0:T(128)S(6)} %copy.20.length, bf16[512,2,2048]{2,1,0:T(2,128)(2,1)S(1)} %get-tuple-element.94.cached, ...), custom_call_target="tpu_custom_call", output_to_operand_aliasing={{4}: (3, {})} | custom-call | flops 2013265920 | bytes 12582912 | tf_op jit(solution)/shard_map/experts/pallas_call | solution.py:325
  63.3 2.5 %experts.7 = (bf16[40,2048]{1,0:T(8,128)(2,1)S(1)}, bf16[40,2048]{1,0:T(8,128)(2,1)S(1)}, bf16[40,2048]{1,0:T(8,128)(2,1)S(1)}, bf16[40,2048]{1,0:T(8,128)(2,1)S(1)}, bf16[512,2,2048]{2,1,0:T(2,128)(2,1)}) custom-call(s32[1]{0:T(128)S(6)} %copy.20.length, bf16[512,2,2048]{2,1,0:T(2,128)(2,1)S(1)} %get-tuple-element.94.cached, ...), custom_call_target="tpu_custom_call", output_to_operand_aliasing={{4}: (3, {})} | custom-call | flops 2013265920 | bytes 12582912 | tf_op jit(solution)/shard_map/experts/pallas_call | solution.py:325
  65.8 1.3 %collective-permute-start.29 = (bf16[40,2048]{1,0:T(8,128)(2,1)S(1)}, bf16[40,2048]{1,0:T(8,128)(2,1)S(1)}, u32[]{:S(2)}, u32[]{:S(2)}) collective-permute-start(bf16[40,2048]{1,0:T(8,128)(2,1)S(1)} %get-tuple-element.160), channel_id=1, source_target_pairs={{0,2},{2,0},{4,6},{6,4},{1,3},{3,1},{5,7},{7,5},{8,10},{10,8},{12,... | collective-permute-start | bytes 491528 | tf_op jit(solution)/shard_map/ppermute | solution.py:248
  68.6 1.6 %collective-permute-start.27 = (bf16[64,2048]{1,0:T(8,128)(2,1)S(1)}, bf16[64,2048]{1,0:T(8,128)(2,1)S(1)}, u32[]{:S(2)}, u32[]{:S(2)}) collective-permute-start(bf16[64,2048]{1,0:T(8,128)(2,1)S(1)} %combine.3), channel_id=1, source_target_pairs={{0,8},{8,0},{16,24},{24,16},{1,9},{9,1},{17,25},{25,17},{2,10},{10... | collective-permute-start | bytes 786440 | tf_op jit(solution)/shard_map/ppermute | solution.py:248
  70.2 1.4 %collective-permute-start.31 = (bf16[40,2048]{1,0:T(8,128)(2,1)S(1)}, bf16[40,2048]{1,0:T(8,128)(2,1)S(1)}, u32[]{:S(2)}, u32[]{:S(2)}) collective-permute-start(bf16[40,2048]{1,0:T(8,128)(2,1)S(1)} %get-tuple-element.162), channel_id=1, source_target_pairs={{0,6},{2,4},{4,2},{6,0},{1,7},{3,5},{5,3},{7,1},{8,14},{10,12},{12... | collective-permute-start | bytes 491528 | tf_op jit(solution)/shard_map/ppermute | solution.py:248
  71.6 1.2 %collective-permute-start.24 = (bf16[40,2048]{1,0:T(8,128)(2,1)S(1)}, bf16[40,2048]{1,0:T(8,128)(2,1)S(1)}, u32[]{:S(2)}, u32[]{:S(2)}) collective-permute-start(bf16[40,2048]{1,0:T(8,128)(2,1)S(1)} %get-tuple-element.146), channel_id=1, source_target_pairs={{0,2},{2,0},{4,6},{6,4},{1,3},{3,1},{5,7},{7,5},{8,10},{10,8},{12,... | collective-permute-start | bytes 491528 | tf_op jit(solution)/shard_map/ppermute | solution.py:248
  73.0 1.1 %collective-permute-start.25 = (bf16[40,2048]{1,0:T(8,128)(2,1)S(1)}, bf16[40,2048]{1,0:T(8,128)(2,1)S(1)}, u32[]{:S(2)}, u32[]{:S(2)}) collective-permute-start(bf16[40,2048]{1,0:T(8,128)(2,1)S(1)} %get-tuple-element.147), channel_id=1, source_target_pairs={{0,4},{2,6},{4,0},{6,2},{1,5},{3,7},{5,1},{7,3},{8,12},{10,14},{12... | collective-permute-start | bytes 491528 | tf_op jit(solution)/shard_map/ppermute | solution.py:248
  74.1 1.6 %collective-permute-start.26 = (bf16[40,2048]{1,0:T(8,128)(2,1)S(1)}, bf16[40,2048]{1,0:T(8,128)(2,1)S(1)}, u32[]{:S(2)}, u32[]{:S(2)}) collective-permute-start(bf16[40,2048]{1,0:T(8,128)(2,1)S(1)} %get-tuple-element.148), channel_id=1, source_target_pairs={{0,6},{2,4},{4,2},{6,0},{1,7},{3,5},{5,3},{7,1},{8,14},{10,12},{12... | collective-permute-start | bytes 491528 | tf_op jit(solution)/shard_map/ppermute | solution.py:248
  77.4 2.3 %collective-permute-start.32 = (bf16[64,2048]{1,0:T(8,128)(2,1)S(1)}, bf16[64,2048]{1,0:T(8,128)(2,1)S(1)}, u32[]{:S(2)}, u32[]{:S(2)}) collective-permute-start(bf16[64,2048]{1,0:T(8,128)(2,1)S(1)} %combine.5), channel_id=1, source_target_pairs={{0,8},{8,0},{16,24},{24,16},{1,9},{9,1},{17,25},{25,17},{2,10},{10... | collective-permute-start | bytes 786440 | tf_op jit(solution)/shard_map/ppermute | solution.py:248
  80.9 2.8 %collective-permute-start.28 = (bf16[64,2048]{1,0:T(8,128)(2,1)S(1)}, bf16[64,2048]{1,0:T(8,128)(2,1)S(1)}, u32[]{:S(2)}, u32[]{:S(2)}) collective-permute-start(bf16[64,2048]{1,0:T(8,128)(2,1)S(1)} %combine.4), channel_id=1, source_target_pairs={{0,16},{8,24},{16,0},{24,8},{1,17},{9,25},{17,1},{25,9},{2,18},{10... | collective-permute-start | bytes 786440 | tf_op jit(solution)/shard_map/ppermute | solution.py:248
  84.3 4.8 %collective-permute-done.32 = bf16[64,2048]{1,0:T(8,128)(2,1)S(1)} collective-permute-done((bf16[64,2048]{1,0:T(8,128)(2,1)S(1)}, bf16[64,2048]{1,0:T(8,128)(2,1)S(1)}, u32[]{:S(2)}, u32[]{:S(2)}) %collective-permute-start.32) | collective-permute-done | bytes 262176 | tf_op jit(solution)/shard_map/ppermute | solution.py:248
  (53 shorter events, 17.7 us)
Async XLA Ops:
  0.6 9.0 %collective-permute-start = (bf16[2048,512]{1,0:T(8,128)(2,1)}, bf16[2048,512]{1,0:T(8,128)(2,1)S(1)}, u32[]{:S(2)}, u32[]{:S(2)}) collective-permute-start(bf16[2048,512]{1,0:T(8,128)(2,1)} %bitcast.17), channel_id=1, source_target_pairs={{0,1},{1,0},{2,3},{3,2},{4,5},{5,4},{6,7},{7,6},{8,9},{9,8},{10,11... | collective-permute-start | bytes 6291464 | tf_op jit(solution)/shard_map/ppermute | solution.py:248
  1.2 8.4 %collective-permute-start.1 = (bf16[2048,512]{1,0:T(8,128)(2,1)}, bf16[2048,512]{1,0:T(8,128)(2,1)S(1)}, u32[]{:S(2)}, u32[]{:S(2)}) collective-permute-start(bf16[2048,512]{1,0:T(8,128)(2,1)} %bitcast.22), channel_id=1, source_target_pairs={{0,1},{1,0},{2,3},{3,2},{4,5},{5,4},{6,7},{7,6},{8,9},{9,8},{10,11... | collective-permute-start | bytes 6291464 | tf_op jit(solution)/shard_map/ppermute | solution.py:248
  1.2 9.9 %collective-permute-start.2 = (bf16[512,2048]{1,0:T(8,128)(2,1)}, bf16[512,2048]{1,0:T(8,128)(2,1)S(1)}, u32[]{:S(2)}, u32[]{:S(2)}) collective-permute-start(bf16[512,2048]{1,0:T(8,128)(2,1)} %bitcast.27), channel_id=1, source_target_pairs={{0,1},{1,0},{2,3},{3,2},{4,5},{5,4},{6,7},{7,6},{8,9},{9,8},{10,11... | collective-permute-start | bytes 6291464 | tf_op jit(solution)/shard_map/ppermute | solution.py:248
  11.1 8.5 %collective-permute-start.4 = (bf16[40,2048]{1,0:T(8,128)(2,1)S(1)}, bf16[40,2048]{1,0:T(8,128)(2,1)S(1)}, u32[]{:S(2)}, u32[]{:S(2)}) collective-permute-start(bf16[40,2048]{1,0:T(8,128)(2,1)S(1)} %get-tuple-element.97), channel_id=1, source_target_pairs={{0,2},{2,0},{4,6},{6,4},{1,3},{3,1},{5,7},{7,5},{8,10},{10,8},{12,... | collective-permute-start | bytes 491528 | tf_op jit(solution)/shard_map/ppermute | solution.py:248
  14.0 9.5 %collective-permute-start.5 = (bf16[40,2048]{1,0:T(8,128)(2,1)S(1)}, bf16[40,2048]{1,0:T(8,128)(2,1)S(1)}, u32[]{:S(2)}, u32[]{:S(2)}) collective-permute-start(bf16[40,2048]{1,0:T(8,128)(2,1)S(1)} %get-tuple-element.98), channel_id=1, source_target_pairs={{0,4},{2,6},{4,0},{6,2},{1,5},{3,7},{5,1},{7,3},{8,12},{10,14},{12... | collective-permute-start | bytes 491528 | tf_op jit(solution)/shard_map/ppermute | solution.py:248
  15.5 8.0 %collective-permute-start.6 = (bf16[40,2048]{1,0:T(8,128)(2,1)S(1)}, bf16[40,2048]{1,0:T(8,128)(2,1)S(1)}, u32[]{:S(2)}, u32[]{:S(2)}) collective-permute-start(bf16[40,2048]{1,0:T(8,128)(2,1)S(1)} %get-tuple-element.99), channel_id=1, source_target_pairs={{0,6},{2,4},{4,2},{6,0},{1,7},{3,5},{5,3},{7,1},{8,14},{10,12},{12... | collective-permute-start | bytes 491528 | tf_op jit(solution)/shard_map/ppermute | solution.py:248
  15.5 13.9 %collective-permute-start.10 = (bf16[64,2176]{1,0:T(8,128)(2,1)S(1)}, bf16[64,2176]{1,0:T(8,128)(2,1)S(1)}, u32[]{:S(2)}, u32[]{:S(2)}) collective-permute-start(bf16[64,2176]{1,0:T(8,128)(2,1)S(1)} %get-tuple-element.88.payload), channel_id=1, source_target_pairs={{0,24},{8,16},{16,8},{24,0},{1,25},{9,17},{17,9},{25,1},{2,26},{10... | collective-permute-start | bytes 835592 | tf_op jit(solution)/shard_map/ppermute | solution.py:248
  19.6 12.3 %collective-permute-start.3 = (bf16[64,2176]{1,0:T(8,128)(2,1)S(1)}, bf16[64,2176]{1,0:T(8,128)(2,1)S(1)}, u32[]{:S(2)}, u32[]{:S(2)}) collective-permute-start(bf16[64,2176]{1,0:T(8,128)(2,1)S(1)} %get-tuple-element.88.payload), channel_id=1, source_target_pairs={{0,8},{8,0},{16,24},{24,16},{1,9},{9,1},{17,25},{25,17},{2,10},{10... | collective-permute-start | bytes 835592 | tf_op jit(solution)/shard_map/ppermute | solution.py:248
  25.8 6.7 %collective-permute-start.7 = (bf16[40,2048]{1,0:T(8,128)(2,1)S(1)}, bf16[40,2048]{1,0:T(8,128)(2,1)S(1)}, u32[]{:S(2)}, u32[]{:S(2)}) collective-permute-start(bf16[40,2048]{1,0:T(8,128)(2,1)S(1)} %get-tuple-element.104), channel_id=1, source_target_pairs={{0,2},{2,0},{4,6},{6,4},{1,3},{3,1},{5,7},{7,5},{8,10},{10,8},{12,... | collective-permute-start | bytes 491528 | tf_op jit(solution)/shard_map/ppermute | solution.py:248
  27.1 8.6 %collective-permute-start.8 = (bf16[40,2048]{1,0:T(8,128)(2,1)S(1)}, bf16[40,2048]{1,0:T(8,128)(2,1)S(1)}, u32[]{:S(2)}, u32[]{:S(2)}) collective-permute-start(bf16[40,2048]{1,0:T(8,128)(2,1)S(1)} %get-tuple-element.105), channel_id=1, source_target_pairs={{0,4},{2,6},{4,0},{6,2},{1,5},{3,7},{5,1},{7,3},{8,12},{10,14},{12... | collective-permute-start | bytes 491528 | tf_op jit(solution)/shard_map/ppermute | solution.py:248
  28.0 7.8 %collective-permute-start.9 = (bf16[40,2048]{1,0:T(8,128)(2,1)S(1)}, bf16[40,2048]{1,0:T(8,128)(2,1)S(1)}, u32[]{:S(2)}, u32[]{:S(2)}) collective-permute-start(bf16[40,2048]{1,0:T(8,128)(2,1)S(1)} %get-tuple-element.106), channel_id=1, source_target_pairs={{0,6},{2,4},{4,2},{6,0},{1,7},{3,5},{5,3},{7,1},{8,14},{10,12},{12... | collective-permute-start | bytes 491528 | tf_op jit(solution)/shard_map/ppermute | solution.py:248
  29.4 14.3 %collective-permute-start.11 = (bf16[64,2176]{1,0:T(8,128)(2,1)S(1)}, bf16[64,2176]{1,0:T(8,128)(2,1)S(1)}, u32[]{:S(2)}, u32[]{:S(2)}) collective-permute-start(bf16[64,2176]{1,0:T(8,128)(2,1)S(1)} %collective-permute-done.10.payload), channel_id=1, source_target_pairs={{0,8},{8,0},{16,24},{24,16},{1,9},{9,1},{17,25},{25,17},{2,10},{10... | collective-permute-start | bytes 835592 | tf_op jit(solution)/shard_map/ppermute | solution.py:248
  35.8 7.1 %collective-permute-start.15 = (bf16[40,2048]{1,0:T(8,128)(2,1)S(1)}, bf16[40,2048]{1,0:T(8,128)(2,1)S(1)}, u32[]{:S(2)}, u32[]{:S(2)}) collective-permute-start(bf16[40,2048]{1,0:T(8,128)(2,1)S(1)} %get-tuple-element.126), channel_id=1, source_target_pairs={{0,2},{2,0},{4,6},{6,4},{1,3},{3,1},{5,7},{7,5},{8,10},{10,8},{12,... | collective-permute-start | bytes 491528 | tf_op jit(solution)/shard_map/ppermute | solution.py:248
  36.7 9.3 %collective-permute-start.16 = (bf16[40,2048]{1,0:T(8,128)(2,1)S(1)}, bf16[40,2048]{1,0:T(8,128)(2,1)S(1)}, u32[]{:S(2)}, u32[]{:S(2)}) collective-permute-start(bf16[40,2048]{1,0:T(8,128)(2,1)S(1)} %get-tuple-element.127), channel_id=1, source_target_pairs={{0,4},{2,6},{4,0},{6,2},{1,5},{3,7},{5,1},{7,3},{8,12},{10,14},{12... | collective-permute-start | bytes 491528 | tf_op jit(solution)/shard_map/ppermute | solution.py:248
  37.9 8.9 %collective-permute-start.17 = (bf16[40,2048]{1,0:T(8,128)(2,1)S(1)}, bf16[40,2048]{1,0:T(8,128)(2,1)S(1)}, u32[]{:S(2)}, u32[]{:S(2)}) collective-permute-start(bf16[40,2048]{1,0:T(8,128)(2,1)S(1)} %get-tuple-element.128), channel_id=1, source_target_pairs={{0,6},{2,4},{4,2},{6,0},{1,7},{3,5},{5,3},{7,1},{8,14},{10,12},{12... | collective-permute-start | bytes 491528 | tf_op jit(solution)/shard_map/ppermute | solution.py:248
  39.9 10.0 %collective-permute-start.12 = (bf16[40,2048]{1,0:T(8,128)(2,1)S(1)}, bf16[40,2048]{1,0:T(8,128)(2,1)S(1)}, u32[]{:S(2)}, u32[]{:S(2)}) collective-permute-start(bf16[40,2048]{1,0:T(8,128)(2,1)S(1)} %get-tuple-element.117), channel_id=1, source_target_pairs={{0,2},{2,0},{4,6},{6,4},{1,3},{3,1},{5,7},{7,5},{8,10},{10,8},{12,... | collective-permute-start | bytes 491528 | tf_op jit(solution)/shard_map/ppermute | solution.py:248
  42.8 11.1 %collective-permute-start.13 = (bf16[40,2048]{1,0:T(8,128)(2,1)S(1)}, bf16[40,2048]{1,0:T(8,128)(2,1)S(1)}, u32[]{:S(2)}, u32[]{:S(2)}) collective-permute-start(bf16[40,2048]{1,0:T(8,128)(2,1)S(1)} %get-tuple-element.118), channel_id=1, source_target_pairs={{0,4},{2,6},{4,0},{6,2},{1,5},{3,7},{5,1},{7,3},{8,12},{10,14},{12... | collective-permute-start | bytes 491528 | tf_op jit(solution)/shard_map/ppermute | solution.py:248
  43.7 10.2 %collective-permute-start.14 = (bf16[40,2048]{1,0:T(8,128)(2,1)S(1)}, bf16[40,2048]{1,0:T(8,128)(2,1)S(1)}, u32[]{:S(2)}, u32[]{:S(2)}) collective-permute-start(bf16[40,2048]{1,0:T(8,128)(2,1)S(1)} %get-tuple-element.119), channel_id=1, source_target_pairs={{0,6},{2,4},{4,2},{6,0},{1,7},{3,5},{5,3},{7,1},{8,14},{10,12},{12... | collective-permute-start | bytes 491528 | tf_op jit(solution)/shard_map/ppermute | solution.py:248
  46.8 11.7 %collective-permute-start.18 = (bf16[40,2048]{1,0:T(8,128)(2,1)S(1)}, bf16[40,2048]{1,0:T(8,128)(2,1)S(1)}, u32[]{:S(2)}, u32[]{:S(2)}) collective-permute-start(bf16[40,2048]{1,0:T(8,128)(2,1)S(1)} %get-tuple-element.130), channel_id=1, source_target_pairs={{0,2},{2,0},{4,6},{6,4},{1,3},{3,1},{5,7},{7,5},{8,10},{10,8},{12,... | collective-permute-start | bytes 491528 | tf_op jit(solution)/shard_map/ppermute | solution.py:248
  48.0 11.8 %collective-permute-start.19 = (bf16[40,2048]{1,0:T(8,128)(2,1)S(1)}, bf16[40,2048]{1,0:T(8,128)(2,1)S(1)}, u32[]{:S(2)}, u32[]{:S(2)}) collective-permute-start(bf16[40,2048]{1,0:T(8,128)(2,1)S(1)} %get-tuple-element.131), channel_id=1, source_target_pairs={{0,4},{2,6},{4,0},{6,2},{1,5},{3,7},{5,1},{7,3},{8,12},{10,14},{12... | collective-permute-start | bytes 491528 | tf_op jit(solution)/shard_map/ppermute | solution.py:248
  49.9 11.0 %collective-permute-start.20 = (bf16[40,2048]{1,0:T(8,128)(2,1)S(1)}, bf16[40,2048]{1,0:T(8,128)(2,1)S(1)}, u32[]{:S(2)}, u32[]{:S(2)}) collective-permute-start(bf16[40,2048]{1,0:T(8,128)(2,1)S(1)} %get-tuple-element.132), channel_id=1, source_target_pairs={{0,6},{2,4},{4,2},{6,0},{1,7},{3,5},{5,3},{7,1},{8,14},{10,12},{12... | collective-permute-start | bytes 491528 | tf_op jit(solution)/shard_map/ppermute | solution.py:248
  56.3 11.7 %collective-permute-start.21 = (bf16[40,2048]{1,0:T(8,128)(2,1)S(1)}, bf16[40,2048]{1,0:T(8,128)(2,1)S(1)}, u32[]{:S(2)}, u32[]{:S(2)}) collective-permute-start(bf16[40,2048]{1,0:T(8,128)(2,1)S(1)} %get-tuple-element.142), channel_id=1, source_target_pairs={{0,2},{2,0},{4,6},{6,4},{1,3},{3,1},{5,7},{7,5},{8,10},{10,8},{12,... | collective-permute-start | bytes 491528 | tf_op jit(solution)/shard_map/ppermute | solution.py:248
  57.6 10.4 %collective-permute-start.22 = (bf16[40,2048]{1,0:T(8,128)(2,1)S(1)}, bf16[40,2048]{1,0:T(8,128)(2,1)S(1)}, u32[]{:S(2)}, u32[]{:S(2)}) collective-permute-start(bf16[40,2048]{1,0:T(8,128)(2,1)S(1)} %get-tuple-element.143), channel_id=1, source_target_pairs={{0,4},{2,6},{4,0},{6,2},{1,5},{3,7},{5,1},{7,3},{8,12},{10,14},{12... | collective-permute-start | bytes 491528 | tf_op jit(solution)/shard_map/ppermute | solution.py:248
  58.5 9.5 %collective-permute-start.23 = (bf16[40,2048]{1,0:T(8,128)(2,1)S(1)}, bf16[40,2048]{1,0:T(8,128)(2,1)S(1)}, u32[]{:S(2)}, u32[]{:S(2)}) collective-permute-start(bf16[40,2048]{1,0:T(8,128)(2,1)S(1)} %get-tuple-element.144), channel_id=1, source_target_pairs={{0,6},{2,4},{4,2},{6,0},{1,7},{3,5},{5,3},{7,1},{8,14},{10,12},{12... | collective-permute-start | bytes 491528 | tf_op jit(solution)/shard_map/ppermute | solution.py:248
  65.8 7.2 %collective-permute-start.29 = (bf16[40,2048]{1,0:T(8,128)(2,1)S(1)}, bf16[40,2048]{1,0:T(8,128)(2,1)S(1)}, u32[]{:S(2)}, u32[]{:S(2)}) collective-permute-start(bf16[40,2048]{1,0:T(8,128)(2,1)S(1)} %get-tuple-element.160), channel_id=1, source_target_pairs={{0,2},{2,0},{4,6},{6,4},{1,3},{3,1},{5,7},{7,5},{8,10},{10,8},{12,... | collective-permute-start | bytes 491528 | tf_op jit(solution)/shard_map/ppermute | solution.py:248
  67.1 7.0 %collective-permute-start.30 = (bf16[40,2048]{1,0:T(8,128)(2,1)S(1)}, bf16[40,2048]{1,0:T(8,128)(2,1)S(1)}, u32[]{:S(2)}, u32[]{:S(2)}) collective-permute-start(bf16[40,2048]{1,0:T(8,128)(2,1)S(1)} %get-tuple-element.161), channel_id=1, source_target_pairs={{0,4},{2,6},{4,0},{6,2},{1,5},{3,7},{5,1},{7,3},{8,12},{10,14},{12... | collective-permute-start | bytes 491528 | tf_op jit(solution)/shard_map/ppermute | solution.py:248
  68.6 11.7 %collective-permute-start.27 = (bf16[64,2048]{1,0:T(8,128)(2,1)S(1)}, bf16[64,2048]{1,0:T(8,128)(2,1)S(1)}, u32[]{:S(2)}, u32[]{:S(2)}) collective-permute-start(bf16[64,2048]{1,0:T(8,128)(2,1)S(1)} %combine.3), channel_id=1, source_target_pairs={{0,8},{8,0},{16,24},{24,16},{1,9},{9,1},{17,25},{25,17},{2,10},{10... | collective-permute-start | bytes 786440 | tf_op jit(solution)/shard_map/ppermute | solution.py:248
  70.2 6.6 %collective-permute-start.31 = (bf16[40,2048]{1,0:T(8,128)(2,1)S(1)}, bf16[40,2048]{1,0:T(8,128)(2,1)S(1)}, u32[]{:S(2)}, u32[]{:S(2)}) collective-permute-start(bf16[40,2048]{1,0:T(8,128)(2,1)S(1)} %get-tuple-element.162), channel_id=1, source_target_pairs={{0,6},{2,4},{4,2},{6,0},{1,7},{3,5},{5,3},{7,1},{8,14},{10,12},{12... | collective-permute-start | bytes 491528 | tf_op jit(solution)/shard_map/ppermute | solution.py:248
  71.6 8.1 %collective-permute-start.24 = (bf16[40,2048]{1,0:T(8,128)(2,1)S(1)}, bf16[40,2048]{1,0:T(8,128)(2,1)S(1)}, u32[]{:S(2)}, u32[]{:S(2)}) collective-permute-start(bf16[40,2048]{1,0:T(8,128)(2,1)S(1)} %get-tuple-element.146), channel_id=1, source_target_pairs={{0,2},{2,0},{4,6},{6,4},{1,3},{3,1},{5,7},{7,5},{8,10},{10,8},{12,... | collective-permute-start | bytes 491528 | tf_op jit(solution)/shard_map/ppermute | solution.py:248
  73.0 6.7 %collective-permute-start.25 = (bf16[40,2048]{1,0:T(8,128)(2,1)S(1)}, bf16[40,2048]{1,0:T(8,128)(2,1)S(1)}, u32[]{:S(2)}, u32[]{:S(2)}) collective-permute-start(bf16[40,2048]{1,0:T(8,128)(2,1)S(1)} %get-tuple-element.147), channel_id=1, source_target_pairs={{0,4},{2,6},{4,0},{6,2},{1,5},{3,7},{5,1},{7,3},{8,12},{10,14},{12... | collective-permute-start | bytes 491528 | tf_op jit(solution)/shard_map/ppermute | solution.py:248
  77.4 11.7 %collective-permute-start.32 = (bf16[64,2048]{1,0:T(8,128)(2,1)S(1)}, bf16[64,2048]{1,0:T(8,128)(2,1)S(1)}, u32[]{:S(2)}, u32[]{:S(2)}) collective-permute-start(bf16[64,2048]{1,0:T(8,128)(2,1)S(1)} %combine.5), channel_id=1, source_target_pairs={{0,8},{8,0},{16,24},{24,16},{1,9},{9,1},{17,25},{25,17},{2,10},{10... | collective-permute-start | bytes 786440 | tf_op jit(solution)/shard_map/ppermute | solution.py:248
  80.9 8.2 %collective-permute-start.28 = (bf16[64,2048]{1,0:T(8,128)(2,1)S(1)}, bf16[64,2048]{1,0:T(8,128)(2,1)S(1)}, u32[]{:S(2)}, u32[]{:S(2)}) collective-permute-start(bf16[64,2048]{1,0:T(8,128)(2,1)S(1)} %combine.4), channel_id=1, source_target_pairs={{0,16},{8,24},{16,0},{24,8},{1,17},{9,25},{17,1},{25,9},{2,18},{10... | collective-permute-start | bytes 786440 | tf_op jit(solution)/shard_map/ppermute | solution.py:248
  (4 other events, 69.7 us)

commit v6 on v5

--- a/solution.py
+++ b/solution.py
@@ -62,11 +62,14 @@
 
 def gather_rows(rows, weights, chips, capacity, outs):
     base, mine = position(chips)
-    _, hit = slot_weights(weights, base, mine, chips, capacity)
+    gate_at, hit = slot_weights(weights, base, mine, chips, capacity)
+    high = gate_at.astype(jnp.bfloat16)
+    low = (gate_at - high.astype(jnp.float32)).astype(jnp.bfloat16)
+    outs[0][...] = jnp.concatenate([high, low], axis=0)
     picked = lax.dot_general(
         hit.astype(jnp.bfloat16), rows, (((0,), (0,)), ((), ())), preferred_element_type=jnp.float32
     )
-    scatter_out(picked, capacity, outs)
+    scatter_out(picked, capacity, outs[1:])
 
 
 def scatter_out(rows, capacity, outs):
@@ -83,13 +86,9 @@
     return jnp.concatenate([ref[...].astype(jnp.float32) for ref in refs], axis=0).astype(jnp.bfloat16)
 
 
-def combined(refs, weights, chips, capacity):
-    base, mine = position(chips)
-    gate_at, _ = slot_weights(weights, base, mine, chips, capacity)
-    high = gate_at.astype(jnp.bfloat16)
-    low = (gate_at - high.astype(jnp.float32)).astype(jnp.bfloat16)
-    tokens = gate_at.shape[0]
-    both = dot(jnp.concatenate([high, low], axis=0), stacked(refs))
+def combined(refs, table):
+    both = dot(table[...], stacked(refs))
+    tokens = both.shape[0] // 2
     return both[:tokens] + both[tokens:]
 
 
@@ -201,17 +200,15 @@
     write.wait()
 
 
-def combine_kernel(chips, capacity, experts, features, counts, payload, *refs):
-    weights = unpacked(payload, features, experts)
-    total = combined(refs[:counts], weights, chips, capacity)
+def combine_kernel(counts, table, *refs):
+    total = combined(refs[:counts], table)
     for ref in refs[counts:-1]:
         total = total + ref[...].astype(jnp.float32)
     refs[-1][...] = total.astype(jnp.bfloat16)
 
 
-def own_kernel(chips, capacity, experts, features, payload, stream, *refs):
-    weights = unpacked(payload, features, experts)
-    refs[-1][...] = stream[...] + combined(refs[:-1], weights, chips, capacity)
+def own_kernel(table, stream, *refs):
+    refs[-1][...] = stream[...] + combined(refs[:-1], table)
 
 
 def in_vmem(count):
@@ -255,6 +252,7 @@
     else:
         block_shapes = [jax.ShapeDtypeStruct((chips * capacity, features), bf16)]
     blocks_n = len(block_shapes)
+    table_shape = jax.ShapeDtypeStruct((2 * group, chips * capacity), bf16)
 
     def cut(blocks):
         return blocks if tiled else [blocks[0][j * capacity : (j + 1) * capacity] for j in range(chips)]
@@ -265,17 +263,18 @@
     own_halves = [w_gate[0], w_up[0], w_down[0]]
     other_halves = [across(half, "core", 1) for half in own_halves]
 
-    stream, payload, cached, newest, *outgoing = pl.pallas_call(
+    stream, payload, cached, newest, table, *outgoing = pl.pallas_call(
         functools.partial(attention_kernel, chips, capacity, experts),
         out_shape=[
             jax.ShapeDtypeStruct((group, features), jnp.float32),
             jax.ShapeDtypeStruct((group, width), bf16),
             jax.ShapeDtypeStruct(cache.shape[1:], bf16),
             jax.ShapeDtypeStruct(new_kv.shape[1:], bf16),
+            table_shape,
         ]
         + block_shapes,
         in_specs=[SMEM_SPEC] + [HBM_SPEC] * 8,
-        out_specs=in_vmem(4 + blocks_n),
+        out_specs=in_vmem(5 + blocks_n),
         scratch_shapes=[
             VMEM((group, features), bf16),
             VMEM((group, features), bf16),
@@ -309,9 +308,9 @@
     def gather(packed):
         return pl.pallas_call(
             functools.partial(gather_kernel, chips, capacity, experts, features),
-            out_shape=block_shapes,
+            out_shape=[table_shape] + block_shapes,
             in_specs=in_vmem(1),
-            out_specs=in_vmem(blocks_n),
+            out_specs=in_vmem(1 + blocks_n),
             compiler_params=params(8),
             name="gather",
         )(packed)
@@ -341,7 +340,7 @@
 
     def combine(packed, returned, extra):
         return pl.pallas_call(
-            functools.partial(combine_kernel, chips, capacity, experts, features, blocks_n),
+            functools.partial(combine_kernel, blocks_n),
             out_shape=jax.ShapeDtypeStruct((group, features), bf16),
             in_specs=in_vmem(1 + blocks_n + len(extra)),
             out_specs=pl.BlockSpec(memory_space=VMEM),
@@ -351,19 +350,22 @@
 
     payload_of = {0: payload, 1: across(payload, "req", 1), 3: across(payload, "req", 3)}
     payload_of[2] = across(payload_of[3], "req", 1)
-    calls, appended = 0, None
+    calls, appended, table_of = 0, None, {}
     arrived_of, returned_of, partials, moved = {}, {}, {}, []
 
     def send_back(s, hold):
         extra = [partials.pop(3)] if s == 2 else []
-        partial = combine(payload_of[s], returned_of.pop(s), extra)
+        partial = combine(table_of[s], returned_of.pop(s), extra)
         hold, partial = lax.optimization_barrier((hold, partial))
         partials[s] = across(partial, "req", 2 if s == 2 else 1)
         return hold
 
     for k, (way, s) in enumerate(ORDER):
         if way == "in":
-            blocks = outgoing if s == 0 else gather(payload_of[s])
+            if s == 0:
+                blocks = outgoing
+            else:
+                table_of[s], *blocks = gather(payload_of[s])
         else:
             blocks, appended = run_experts(arrived_of[s], calls, appended)
             calls += 1
@@ -384,13 +386,13 @@
             send_back(s, ())
     own_returned = returned_of[0]
     total = pl.pallas_call(
-        functools.partial(own_kernel, chips, capacity, experts, features),
+        own_kernel,
         out_shape=jax.ShapeDtypeStruct((group, features), jnp.float32),
         in_specs=in_vmem(2 + blocks_n),
         out_specs=pl.BlockSpec(memory_space=VMEM),
         compiler_params=params(8),
         name="own",
-    )(payload, stream, *own_returned)
+    )(table, stream, *own_returned)
     for partial in partials.values():
         total = total + partial.astype(jnp.float32)
     layer_out = total.astype(bf16)

time: 90.6 us -> 90.1 us (level)
  Pallas kernels: 21.1 us -> 19.8 us
  waiting for transfers between devices: 23 us -> 24.1 us
  starting transfers between devices: 43.5 us -> 42.5 us
    pallas_call x4, Pallas kernels: 2.38 us -> 1.14 us  [the longest x3 0.85 us: combine(): pl.pallas_call(functools.partial(combine_kernel, blocks_n), out_shape=jax...]
    ppermute x33, waiting for transfers between devices: 23 us -> 24.1 us  [across(): return lax.ppermute(x, axis, [(i, i ^ j) for i in range(size)])]
    ppermute x33, starting transfers between devices: 43.5 us -> 42.5 us  [across(): return lax.ppermute(x, axis, [(i, i ^ j) for i in range(size)])]
  transfers between devices with their start and end apart: 33 -> 33, of which waited for: 13 -> 15; matrix products, arithmetic and copies ran while one was open for 0% -> 0% of each run, Pallas kernels for 23% -> 22%
where the time goes in v6:
time: 90.1 us; the launch traced here: 88.6 us
  starting transfers between devices  42.5 us (47%)
  waiting for transfers between devices  24.1 us (27%)
  Pallas kernels  19.8 us (22%)
  between operations  1.47 us (2%)
    ppermute x33, starting transfers between devices, across(): return lax.ppermute(x, axis, [(i, i ^ j) for i in range(size)])  42.5 us
    ppermute x33, waiting for transfers between devices, across(): return lax.ppermute(x, axis, [(i, i ^ j) for i in range(size)])  24.1 us
    pallas_call x4, Pallas kernels, run_experts(): pl.pallas_call(functools.partial(expert_kernel, capacity, blocks_n, spans...  9.32 us
    pallas_call x1, Pallas kernels, shards(): pl.pallas_call(functools.partial(attention_kernel, chips, capacity, exper...  7.25 us
    pallas_call x3, Pallas kernels, gather(): pl.pallas_call(functools.partial(gather_kernel, chips, capacity, experts,...  2.05 us
  transfers between devices with their start and end apart: 33, of which 15 were waited for; matrix products, arithmetic and copies ran while one was open for 0% of the time, Pallas kernels for 22%

profile of v6, /device:TPU:0, one launch (start us, length us, event | category | flops | bytes accessed | tf_op | source)
XLA Modules:
  0.0 88.6 jit_solution(16196570035268307653)
XLA Ops:
  2.3 7.3 %attention.1 = (f32[64,2048]{1,0:T(8,128)S(1)}, bf16[64,2176]{1,0:T(8,128)(2,1)S(1)}, bf16[512,2,2048]{2,1,0:T(2,128)(2,1)S(1)}, bf16[64,2,2048]{2,1,0:T(2,128)(...) custom-call(s32[1]{0:T(128)S(6)} %copy.20.length, ...), custom_call_target="tpu_custom_call" | custom-call | flops 12000000000 | bytes 25165824 | tf_op jit(solution)/shard_map/attention/pallas_call | solution.py:266
  9.6 1.5 %collective-permute-done.2.refs_9_.refs_10_ = bf16[512,2048]{1,0:T(8,128)(2,1)S(1)} collective-permute-done((bf16[512,2048]{1,0:T(8,128)(2,1)}, bf16[512,2048]{1,0:T(8,128)(2,1)S(1)}, u32[]{:S(2)}, u32[]{:S(2)}) %collective-permute-start.2) | collective-permute-done | bytes 2097184 | tf_op jit(solution)/shard_map/ppermute | solution.py:245
  11.1 2.9 %collective-permute-start.4 = (bf16[40,2048]{1,0:T(8,128)(2,1)S(1)}, bf16[40,2048]{1,0:T(8,128)(2,1)S(1)}, u32[]{:S(2)}, u32[]{:S(2)}) collective-permute-start(bf16[40,2048]{1,0:T(8,128)(2,1)S(1)} %get-tuple-element.102), channel_id=1, source_target_pairs={{0,2},{2,0},{4,6},{6,4},{1,3},{3,1},{5,7},{7,5},{8,10},{10,8},{12,... | collective-permute-start | bytes 491528 | tf_op jit(solution)/shard_map/ppermute | solution.py:245
  14.0 1.5 %collective-permute-start.5 = (bf16[40,2048]{1,0:T(8,128)(2,1)S(1)}, bf16[40,2048]{1,0:T(8,128)(2,1)S(1)}, u32[]{:S(2)}, u32[]{:S(2)}) collective-permute-start(bf16[40,2048]{1,0:T(8,128)(2,1)S(1)} %get-tuple-element.103), channel_id=1, source_target_pairs={{0,4},{2,6},{4,0},{6,2},{1,5},{3,7},{5,1},{7,3},{8,12},{10,14},{12... | collective-permute-start | bytes 491528 | tf_op jit(solution)/shard_map/ppermute | solution.py:245
  15.5 4.1 %collective-permute-start.10 = (bf16[64,2176]{1,0:T(8,128)(2,1)S(1)}, bf16[64,2176]{1,0:T(8,128)(2,1)S(1)}, u32[]{:S(2)}, u32[]{:S(2)}) collective-permute-start(bf16[64,2176]{1,0:T(8,128)(2,1)S(1)} %get-tuple-element.94), channel_id=1, source_target_pairs={{0,24},{8,16},{16,8},{24,0},{1,25},{9,17},{17,9},{25,1},{2,26},{10... | collective-permute-start | bytes 835592 | tf_op jit(solution)/shard_map/ppermute | solution.py:245
  19.6 3.9 %collective-permute-done.5.refs_2_ = bf16[40,2048]{1,0:T(8,128)(2,1)S(1)} collective-permute-done((bf16[40,2048]{1,0:T(8,128)(2,1)S(1)}, bf16[40,2048]{1,0:T(8,128)(2,1)S(1)}, u32[]{:S(2)}, u32[]{:S(2)}) %collective-permute-start.5) | collective-permute-done | bytes 163872 | tf_op jit(solution)/shard_map/ppermute | solution.py:245
  23.5 2.3 %experts.4 = (bf16[40,2048]{1,0:T(8,128)(2,1)S(1)}, bf16[40,2048]{1,0:T(8,128)(2,1)S(1)}, bf16[40,2048]{1,0:T(8,128)(2,1)S(1)}, bf16[40,2048]{1,0:T(8,128)(2,1)S(1)}, bf16[512,2,2048]{2,1,0:T(2,128)(2,1)}) custom-call(s32[1]{0:T(128)S(6)} %copy.20.length, bf16[512,2,2048]{2,1,0:T(2,128)(2,1)S(1)} %get-tuple-element.99.cached, ...), custom_call_target="tpu_custom_call" | custom-call | flops 2013265920 | bytes 12582912 | tf_op jit(solution)/shard_map/experts/pallas_call | solution.py:324
  25.8 1.3 %collective-permute-start.7 = (bf16[40,2048]{1,0:T(8,128)(2,1)S(1)}, bf16[40,2048]{1,0:T(8,128)(2,1)S(1)}, u32[]{:S(2)}, u32[]{:S(2)}) collective-permute-start(bf16[40,2048]{1,0:T(8,128)(2,1)S(1)} %get-tuple-element.109), channel_id=1, source_target_pairs={{0,2},{2,0},{4,6},{6,4},{1,3},{3,1},{5,7},{7,5},{8,10},{10,8},{12,... | collective-permute-start | bytes 491528 | tf_op jit(solution)/shard_map/ppermute | solution.py:245
  28.0 1.4 %collective-permute-start.9 = (bf16[40,2048]{1,0:T(8,128)(2,1)S(1)}, bf16[40,2048]{1,0:T(8,128)(2,1)S(1)}, u32[]{:S(2)}, u32[]{:S(2)}) collective-permute-start(bf16[40,2048]{1,0:T(8,128)(2,1)S(1)} %get-tuple-element.111), channel_id=1, source_target_pairs={{0,6},{2,4},{4,2},{6,0},{1,7},{3,5},{5,3},{7,1},{8,14},{10,12},{12... | collective-permute-start | bytes 491528 | tf_op jit(solution)/shard_map/ppermute | solution.py:245
  29.4 2.0 %collective-permute-start.11 = (bf16[64,2176]{1,0:T(8,128)(2,1)S(1)}, bf16[64,2176]{1,0:T(8,128)(2,1)S(1)}, u32[]{:S(2)}, u32[]{:S(2)}) collective-permute-start(bf16[64,2176]{1,0:T(8,128)(2,1)S(1)} %collective-permute-done.10.payload), channel_id=1, source_target_pairs={{0,8},{8,0},{16,24},{24,16},{1,9},{9,1},{17,25},{25,17},{2,10},{10... | collective-permute-start | bytes 835592 | tf_op jit(solution)/shard_map/ppermute | solution.py:245
  32.6 3.2 %collective-permute-done.8.refs_2_ = bf16[40,2048]{1,0:T(8,128)(2,1)S(1)} collective-permute-done((bf16[40,2048]{1,0:T(8,128)(2,1)S(1)}, bf16[40,2048]{1,0:T(8,128)(2,1)S(1)}, u32[]{:S(2)}, u32[]{:S(2)}) %collective-permute-start.8) | collective-permute-done | bytes 163872 | tf_op jit(solution)/shard_map/ppermute | solution.py:245
  36.7 1.3 %collective-permute-start.16 = (bf16[40,2048]{1,0:T(8,128)(2,1)S(1)}, bf16[40,2048]{1,0:T(8,128)(2,1)S(1)}, u32[]{:S(2)}, u32[]{:S(2)}) collective-permute-start(bf16[40,2048]{1,0:T(8,128)(2,1)S(1)} %get-tuple-element.133), channel_id=1, source_target_pairs={{0,4},{2,6},{4,0},{6,2},{1,5},{3,7},{5,1},{7,3},{8,12},{10,14},{12... | collective-permute-start | bytes 491528 | tf_op jit(solution)/shard_map/ppermute | solution.py:245
  37.9 1.4 %collective-permute-start.17 = (bf16[40,2048]{1,0:T(8,128)(2,1)S(1)}, bf16[40,2048]{1,0:T(8,128)(2,1)S(1)}, u32[]{:S(2)}, u32[]{:S(2)}) collective-permute-start(bf16[40,2048]{1,0:T(8,128)(2,1)S(1)} %get-tuple-element.134), channel_id=1, source_target_pairs={{0,6},{2,4},{4,2},{6,0},{1,7},{3,5},{5,3},{7,1},{8,14},{10,12},{12... | collective-permute-start | bytes 491528 | tf_op jit(solution)/shard_map/ppermute | solution.py:245
  40.9 1.9 %collective-permute-done.15.refs_2_ = bf16[40,2048]{1,0:T(8,128)(2,1)S(1)} collective-permute-done((bf16[40,2048]{1,0:T(8,128)(2,1)S(1)}, bf16[40,2048]{1,0:T(8,128)(2,1)S(1)}, u32[]{:S(2)}, u32[]{:S(2)}) %collective-permute-start.15) | collective-permute-done | bytes 163872 | tf_op jit(solution)/shard_map/ppermute | solution.py:245
  43.8 1.6 %collective-permute-start.14 = (bf16[40,2048]{1,0:T(8,128)(2,1)S(1)}, bf16[40,2048]{1,0:T(8,128)(2,1)S(1)}, u32[]{:S(2)}, u32[]{:S(2)}) collective-permute-start(bf16[40,2048]{1,0:T(8,128)(2,1)S(1)} %get-tuple-element.125), channel_id=1, source_target_pairs={{0,6},{2,4},{4,2},{6,0},{1,7},{3,5},{5,3},{7,1},{8,14},{10,12},{12... | collective-permute-start | bytes 491528 | tf_op jit(solution)/shard_map/ppermute | solution.py:245
  46.8 1.2 %collective-permute-start.18 = (bf16[40,2048]{1,0:T(8,128)(2,1)S(1)}, bf16[40,2048]{1,0:T(8,128)(2,1)S(1)}, u32[]{:S(2)}, u32[]{:S(2)}) collective-permute-start(bf16[40,2048]{1,0:T(8,128)(2,1)S(1)} %get-tuple-element.136), channel_id=1, source_target_pairs={{0,2},{2,0},{4,6},{6,4},{1,3},{3,1},{5,7},{7,5},{8,10},{10,8},{12,... | collective-permute-start | bytes 491528 | tf_op jit(solution)/shard_map/ppermute | solution.py:245
  49.9 1.6 %collective-permute-start.20 = (bf16[40,2048]{1,0:T(8,128)(2,1)S(1)}, bf16[40,2048]{1,0:T(8,128)(2,1)S(1)}, u32[]{:S(2)}, u32[]{:S(2)}) collective-permute-start(bf16[40,2048]{1,0:T(8,128)(2,1)S(1)} %get-tuple-element.138), channel_id=1, source_target_pairs={{0,6},{2,4},{4,2},{6,0},{1,7},{3,5},{5,3},{7,1},{8,14},{10,12},{12... | collective-permute-start | bytes 491528 | tf_op jit(solution)/shard_map/ppermute | solution.py:245
  51.5 2.5 %collective-permute-done.13.refs_3_ = bf16[40,2048]{1,0:T(8,128)(2,1)S(1)} collective-permute-done((bf16[40,2048]{1,0:T(8,128)(2,1)S(1)}, bf16[40,2048]{1,0:T(8,128)(2,1)S(1)}, u32[]{:S(2)}, u32[]{:S(2)}) %collective-permute-start.13) | collective-permute-done | bytes 163872 | tf_op jit(solution)/shard_map/ppermute | solution.py:245
  54.0 2.3 %experts.5 = (bf16[40,2048]{1,0:T(8,128)(2,1)S(1)}, bf16[40,2048]{1,0:T(8,128)(2,1)S(1)}, bf16[40,2048]{1,0:T(8,128)(2,1)S(1)}, bf16[40,2048]{1,0:T(8,128)(2,1)S(1)}, bf16[512,2,2048]{2,1,0:T(2,128)(2,1)}) custom-call(s32[1]{0:T(128)S(6)} %copy.20.length, bf16[512,2,2048]{2,1,0:T(2,128)(2,1)S(1)} %get-tuple-element.99.cached, ...), custom_call_target="tpu_custom_call", output_to_operand_aliasing={{4}: (3, {})} | custom-call | flops 2013265920 | bytes 12582912 | tf_op jit(solution)/shard_map/experts/pallas_call | solution.py:324
  56.3 1.3 %collective-permute-start.21 = (bf16[40,2048]{1,0:T(8,128)(2,1)S(1)}, bf16[40,2048]{1,0:T(8,128)(2,1)S(1)}, u32[]{:S(2)}, u32[]{:S(2)}) collective-permute-start(bf16[40,2048]{1,0:T(8,128)(2,1)S(1)} %get-tuple-element.149), channel_id=1, source_target_pairs={{0,2},{2,0},{4,6},{6,4},{1,3},{3,1},{5,7},{7,5},{8,10},{10,8},{12,... | collective-permute-start | bytes 491528 | tf_op jit(solution)/shard_map/ppermute | solution.py:245
  58.5 1.4 %collective-permute-start.23 = (bf16[40,2048]{1,0:T(8,128)(2,1)S(1)}, bf16[40,2048]{1,0:T(8,128)(2,1)S(1)}, u32[]{:S(2)}, u32[]{:S(2)}) collective-permute-start(bf16[40,2048]{1,0:T(8,128)(2,1)S(1)} %get-tuple-element.151), channel_id=1, source_target_pairs={{0,6},{2,4},{4,2},{6,0},{1,7},{3,5},{5,3},{7,1},{8,14},{10,12},{12... | collective-permute-start | bytes 491528 | tf_op jit(solution)/shard_map/ppermute | solution.py:245
  60.9 2.3 %experts.6 = (bf16[40,2048]{1,0:T(8,128)(2,1)S(1)}, bf16[40,2048]{1,0:T(8,128)(2,1)S(1)}, bf16[40,2048]{1,0:T(8,128)(2,1)S(1)}, bf16[40,2048]{1,0:T(8,128)(2,1)S(1)}, bf16[512,2,2048]{2,1,0:T(2,128)(2,1)}) custom-call(s32[1]{0:T(128)S(6)} %copy.20.length, bf16[512,2,2048]{2,1,0:T(2,128)(2,1)S(1)} %get-tuple-element.99.cached, ...), custom_call_target="tpu_custom_call", output_to_operand_aliasing={{4}: (3, {})} | custom-call | flops 2013265920 | bytes 12582912 | tf_op jit(solution)/shard_map/experts/pallas_call | solution.py:324
  63.3 2.3 %experts.7 = (bf16[40,2048]{1,0:T(8,128)(2,1)S(1)}, bf16[40,2048]{1,0:T(8,128)(2,1)S(1)}, bf16[40,2048]{1,0:T(8,128)(2,1)S(1)}, bf16[40,2048]{1,0:T(8,128)(2,1)S(1)}, bf16[512,2,2048]{2,1,0:T(2,128)(2,1)}) custom-call(s32[1]{0:T(128)S(6)} %copy.20.length, bf16[512,2,2048]{2,1,0:T(2,128)(2,1)S(1)} %get-tuple-element.99.cached, ...), custom_call_target="tpu_custom_call", output_to_operand_aliasing={{4}: (3, {})} | custom-call | flops 2013265920 | bytes 12582912 | tf_op jit(solution)/shard_map/experts/pallas_call | solution.py:324
  65.6 1.3 %collective-permute-start.29 = (bf16[40,2048]{1,0:T(8,128)(2,1)S(1)}, bf16[40,2048]{1,0:T(8,128)(2,1)S(1)}, u32[]{:S(2)}, u32[]{:S(2)}) collective-permute-start(bf16[40,2048]{1,0:T(8,128)(2,1)S(1)} %get-tuple-element.168), channel_id=1, source_target_pairs={{0,2},{2,0},{4,6},{6,4},{1,3},{3,1},{5,7},{7,5},{8,10},{10,8},{12,... | collective-permute-start | bytes 491528 | tf_op jit(solution)/shard_map/ppermute | solution.py:245
  68.1 1.6 %collective-permute-start.27 = (bf16[64,2048]{1,0:T(8,128)(2,1)S(1)}, bf16[64,2048]{1,0:T(8,128)(2,1)S(1)}, u32[]{:S(2)}, u32[]{:S(2)}) collective-permute-start(bf16[64,2048]{1,0:T(8,128)(2,1)S(1)} %combine.3), channel_id=1, source_target_pairs={{0,8},{8,0},{16,24},{24,16},{1,9},{9,1},{17,25},{25,17},{2,10},{10... | collective-permute-start | bytes 786440 | tf_op jit(solution)/shard_map/ppermute | solution.py:245
  69.7 1.4 %collective-permute-start.31 = (bf16[40,2048]{1,0:T(8,128)(2,1)S(1)}, bf16[40,2048]{1,0:T(8,128)(2,1)S(1)}, u32[]{:S(2)}, u32[]{:S(2)}) collective-permute-start(bf16[40,2048]{1,0:T(8,128)(2,1)S(1)} %get-tuple-element.170), channel_id=1, source_target_pairs={{0,6},{2,4},{4,2},{6,0},{1,7},{3,5},{5,3},{7,1},{8,14},{10,12},{12... | collective-permute-start | bytes 491528 | tf_op jit(solution)/shard_map/ppermute | solution.py:245
  71.1 1.2 %collective-permute-start.24 = (bf16[40,2048]{1,0:T(8,128)(2,1)S(1)}, bf16[40,2048]{1,0:T(8,128)(2,1)S(1)}, u32[]{:S(2)}, u32[]{:S(2)}) collective-permute-start(bf16[40,2048]{1,0:T(8,128)(2,1)S(1)} %get-tuple-element.153), channel_id=1, source_target_pairs={{0,2},{2,0},{4,6},{6,4},{1,3},{3,1},{5,7},{7,5},{8,10},{10,8},{12,... | collective-permute-start | bytes 491528 | tf_op jit(solution)/shard_map/ppermute | solution.py:245
  73.9 1.6 %collective-permute-start.26 = (bf16[40,2048]{1,0:T(8,128)(2,1)S(1)}, bf16[40,2048]{1,0:T(8,128)(2,1)S(1)}, u32[]{:S(2)}, u32[]{:S(2)}) collective-permute-start(bf16[40,2048]{1,0:T(8,128)(2,1)S(1)} %get-tuple-element.155), channel_id=1, source_target_pairs={{0,6},{2,4},{4,2},{6,0},{1,7},{3,5},{5,3},{7,1},{8,14},{10,12},{12... | collective-permute-start | bytes 491528 | tf_op jit(solution)/shard_map/ppermute | solution.py:245
  76.7 1.3 %collective-permute-start.32 = (bf16[64,2048]{1,0:T(8,128)(2,1)S(1)}, bf16[64,2048]{1,0:T(8,128)(2,1)S(1)}, u32[]{:S(2)}, u32[]{:S(2)}) collective-permute-start(bf16[64,2048]{1,0:T(8,128)(2,1)S(1)} %combine.5), channel_id=1, source_target_pairs={{0,8},{8,0},{16,24},{24,16},{1,9},{9,1},{17,25},{25,17},{2,10},{10... | collective-permute-start | bytes 786440 | tf_op jit(solution)/shard_map/ppermute | solution.py:245
  78.2 1.9 %collective-permute-done.26.refs_3_ = bf16[40,2048]{1,0:T(8,128)(2,1)S(1)} collective-permute-done((bf16[40,2048]{1,0:T(8,128)(2,1)S(1)}, bf16[40,2048]{1,0:T(8,128)(2,1)S(1)}, u32[]{:S(2)}, u32[]{:S(2)}) %collective-permute-start.26) | collective-permute-done | bytes 163872 | tf_op jit(solution)/shard_map/ppermute | solution.py:245
  80.4 2.8 %collective-permute-start.28 = (bf16[64,2048]{1,0:T(8,128)(2,1)S(1)}, bf16[64,2048]{1,0:T(8,128)(2,1)S(1)}, u32[]{:S(2)}, u32[]{:S(2)}) collective-permute-start(bf16[64,2048]{1,0:T(8,128)(2,1)S(1)} %combine.4), channel_id=1, source_target_pairs={{0,16},{8,24},{16,0},{24,8},{1,17},{9,25},{17,1},{25,9},{2,18},{10... | collective-permute-start | bytes 786440 | tf_op jit(solution)/shard_map/ppermute | solution.py:245
  83.9 3.8 %collective-permute-done.28 = bf16[64,2048]{1,0:T(8,128)(2,1)S(1)} collective-permute-done((bf16[64,2048]{1,0:T(8,128)(2,1)S(1)}, bf16[64,2048]{1,0:T(8,128)(2,1)S(1)}, u32[]{:S(2)}, u32[]{:S(2)}) %collective-permute-start.28) | collective-permute-done | bytes 262176 | tf_op jit(solution)/shard_map/ppermute | solution.py:245
  (53 shorter events, 17.7 us)
Async XLA Ops:
  0.6 9.0 %collective-permute-start = (bf16[2048,512]{1,0:T(8,128)(2,1)}, bf16[2048,512]{1,0:T(8,128)(2,1)S(1)}, u32[]{:S(2)}, u32[]{:S(2)}) collective-permute-start(bf16[2048,512]{1,0:T(8,128)(2,1)} %bitcast.17), channel_id=1, source_target_pairs={{0,1},{1,0},{2,3},{3,2},{4,5},{5,4},{6,7},{7,6},{8,9},{9,8},{10,11... | collective-permute-start | bytes 6291464 | tf_op jit(solution)/shard_map/ppermute | solution.py:245
  1.2 8.5 %collective-permute-start.1 = (bf16[2048,512]{1,0:T(8,128)(2,1)}, bf16[2048,512]{1,0:T(8,128)(2,1)S(1)}, u32[]{:S(2)}, u32[]{:S(2)}) collective-permute-start(bf16[2048,512]{1,0:T(8,128)(2,1)} %bitcast.22), channel_id=1, source_target_pairs={{0,1},{1,0},{2,3},{3,2},{4,5},{5,4},{6,7},{7,6},{8,9},{9,8},{10,11... | collective-permute-start | bytes 6291464 | tf_op jit(solution)/shard_map/ppermute | solution.py:245
  1.2 9.9 %collective-permute-start.2 = (bf16[512,2048]{1,0:T(8,128)(2,1)}, bf16[512,2048]{1,0:T(8,128)(2,1)S(1)}, u32[]{:S(2)}, u32[]{:S(2)}) collective-permute-start(bf16[512,2048]{1,0:T(8,128)(2,1)} %bitcast.27), channel_id=1, source_target_pairs={{0,1},{1,0},{2,3},{3,2},{4,5},{5,4},{6,7},{7,6},{8,9},{9,8},{10,11... | collective-permute-start | bytes 6291464 | tf_op jit(solution)/shard_map/ppermute | solution.py:245
  11.1 8.5 %collective-permute-start.4 = (bf16[40,2048]{1,0:T(8,128)(2,1)S(1)}, bf16[40,2048]{1,0:T(8,128)(2,1)S(1)}, u32[]{:S(2)}, u32[]{:S(2)}) collective-permute-start(bf16[40,2048]{1,0:T(8,128)(2,1)S(1)} %get-tuple-element.102), channel_id=1, source_target_pairs={{0,2},{2,0},{4,6},{6,4},{1,3},{3,1},{5,7},{7,5},{8,10},{10,8},{12,... | collective-permute-start | bytes 491528 | tf_op jit(solution)/shard_map/ppermute | solution.py:245
  14.0 9.5 %collective-permute-start.5 = (bf16[40,2048]{1,0:T(8,128)(2,1)S(1)}, bf16[40,2048]{1,0:T(8,128)(2,1)S(1)}, u32[]{:S(2)}, u32[]{:S(2)}) collective-permute-start(bf16[40,2048]{1,0:T(8,128)(2,1)S(1)} %get-tuple-element.103), channel_id=1, source_target_pairs={{0,4},{2,6},{4,0},{6,2},{1,5},{3,7},{5,1},{7,3},{8,12},{10,14},{12... | collective-permute-start | bytes 491528 | tf_op jit(solution)/shard_map/ppermute | solution.py:245
  15.5 8.0 %collective-permute-start.6 = (bf16[40,2048]{1,0:T(8,128)(2,1)S(1)}, bf16[40,2048]{1,0:T(8,128)(2,1)S(1)}, u32[]{:S(2)}, u32[]{:S(2)}) collective-permute-start(bf16[40,2048]{1,0:T(8,128)(2,1)S(1)} %get-tuple-element.104), channel_id=1, source_target_pairs={{0,6},{2,4},{4,2},{6,0},{1,7},{3,5},{5,3},{7,1},{8,14},{10,12},{12... | collective-permute-start | bytes 491528 | tf_op jit(solution)/shard_map/ppermute | solution.py:245
  15.5 13.9 %collective-permute-start.10 = (bf16[64,2176]{1,0:T(8,128)(2,1)S(1)}, bf16[64,2176]{1,0:T(8,128)(2,1)S(1)}, u32[]{:S(2)}, u32[]{:S(2)}) collective-permute-start(bf16[64,2176]{1,0:T(8,128)(2,1)S(1)} %get-tuple-element.94), channel_id=1, source_target_pairs={{0,24},{8,16},{16,8},{24,0},{1,25},{9,17},{17,9},{25,1},{2,26},{10... | collective-permute-start | bytes 835592 | tf_op jit(solution)/shard_map/ppermute | solution.py:245
  19.6 12.3 %collective-permute-start.3 = (bf16[64,2176]{1,0:T(8,128)(2,1)S(1)}, bf16[64,2176]{1,0:T(8,128)(2,1)S(1)}, u32[]{:S(2)}, u32[]{:S(2)}) collective-permute-start(bf16[64,2176]{1,0:T(8,128)(2,1)S(1)} %get-tuple-element.94), channel_id=1, source_target_pairs={{0,8},{8,0},{16,24},{24,16},{1,9},{9,1},{17,25},{25,17},{2,10},{10... | collective-permute-start | bytes 835592 | tf_op jit(solution)/shard_map/ppermute | solution.py:245
  25.8 6.7 %collective-permute-start.7 = (bf16[40,2048]{1,0:T(8,128)(2,1)S(1)}, bf16[40,2048]{1,0:T(8,128)(2,1)S(1)}, u32[]{:S(2)}, u32[]{:S(2)}) collective-permute-start(bf16[40,2048]{1,0:T(8,128)(2,1)S(1)} %get-tuple-element.109), channel_id=1, source_target_pairs={{0,2},{2,0},{4,6},{6,4},{1,3},{3,1},{5,7},{7,5},{8,10},{10,8},{12,... | collective-permute-start | bytes 491528 | tf_op jit(solution)/shard_map/ppermute | solution.py:245
  27.1 8.6 %collective-permute-start.8 = (bf16[40,2048]{1,0:T(8,128)(2,1)S(1)}, bf16[40,2048]{1,0:T(8,128)(2,1)S(1)}, u32[]{:S(2)}, u32[]{:S(2)}) collective-permute-start(bf16[40,2048]{1,0:T(8,128)(2,1)S(1)} %get-tuple-element.110), channel_id=1, source_target_pairs={{0,4},{2,6},{4,0},{6,2},{1,5},{3,7},{5,1},{7,3},{8,12},{10,14},{12... | collective-permute-start | bytes 491528 | tf_op jit(solution)/shard_map/ppermute | solution.py:245
  28.0 7.8 %collective-permute-start.9 = (bf16[40,2048]{1,0:T(8,128)(2,1)S(1)}, bf16[40,2048]{1,0:T(8,128)(2,1)S(1)}, u32[]{:S(2)}, u32[]{:S(2)}) collective-permute-start(bf16[40,2048]{1,0:T(8,128)(2,1)S(1)} %get-tuple-element.111), channel_id=1, source_target_pairs={{0,6},{2,4},{4,2},{6,0},{1,7},{3,5},{5,3},{7,1},{8,14},{10,12},{12... | collective-permute-start | bytes 491528 | tf_op jit(solution)/shard_map/ppermute | solution.py:245
  29.4 14.4 %collective-permute-start.11 = (bf16[64,2176]{1,0:T(8,128)(2,1)S(1)}, bf16[64,2176]{1,0:T(8,128)(2,1)S(1)}, u32[]{:S(2)}, u32[]{:S(2)}) collective-permute-start(bf16[64,2176]{1,0:T(8,128)(2,1)S(1)} %collective-permute-done.10.payload), channel_id=1, source_target_pairs={{0,8},{8,0},{16,24},{24,16},{1,9},{9,1},{17,25},{25,17},{2,10},{10... | collective-permute-start | bytes 835592 | tf_op jit(solution)/shard_map/ppermute | solution.py:245
  35.8 7.1 %collective-permute-start.15 = (bf16[40,2048]{1,0:T(8,128)(2,1)S(1)}, bf16[40,2048]{1,0:T(8,128)(2,1)S(1)}, u32[]{:S(2)}, u32[]{:S(2)}) collective-permute-start(bf16[40,2048]{1,0:T(8,128)(2,1)S(1)} %get-tuple-element.132), channel_id=1, source_target_pairs={{0,2},{2,0},{4,6},{6,4},{1,3},{3,1},{5,7},{7,5},{8,10},{10,8},{12,... | collective-permute-start | bytes 491528 | tf_op jit(solution)/shard_map/ppermute | solution.py:245
  36.7 9.3 %collective-permute-start.16 = (bf16[40,2048]{1,0:T(8,128)(2,1)S(1)}, bf16[40,2048]{1,0:T(8,128)(2,1)S(1)}, u32[]{:S(2)}, u32[]{:S(2)}) collective-permute-start(bf16[40,2048]{1,0:T(8,128)(2,1)S(1)} %get-tuple-element.133), channel_id=1, source_target_pairs={{0,4},{2,6},{4,0},{6,2},{1,5},{3,7},{5,1},{7,3},{8,12},{10,14},{12... | collective-permute-start | bytes 491528 | tf_op jit(solution)/shard_map/ppermute | solution.py:245
  37.9 8.9 %collective-permute-start.17 = (bf16[40,2048]{1,0:T(8,128)(2,1)S(1)}, bf16[40,2048]{1,0:T(8,128)(2,1)S(1)}, u32[]{:S(2)}, u32[]{:S(2)}) collective-permute-start(bf16[40,2048]{1,0:T(8,128)(2,1)S(1)} %get-tuple-element.134), channel_id=1, source_target_pairs={{0,6},{2,4},{4,2},{6,0},{1,7},{3,5},{5,3},{7,1},{8,14},{10,12},{12... | collective-permute-start | bytes 491528 | tf_op jit(solution)/shard_map/ppermute | solution.py:245
  40.0 10.0 %collective-permute-start.12 = (bf16[40,2048]{1,0:T(8,128)(2,1)S(1)}, bf16[40,2048]{1,0:T(8,128)(2,1)S(1)}, u32[]{:S(2)}, u32[]{:S(2)}) collective-permute-start(bf16[40,2048]{1,0:T(8,128)(2,1)S(1)} %get-tuple-element.123), channel_id=1, source_target_pairs={{0,2},{2,0},{4,6},{6,4},{1,3},{3,1},{5,7},{7,5},{8,10},{10,8},{12,... | collective-permute-start | bytes 491528 | tf_op jit(solution)/shard_map/ppermute | solution.py:245
  42.8 11.1 %collective-permute-start.13 = (bf16[40,2048]{1,0:T(8,128)(2,1)S(1)}, bf16[40,2048]{1,0:T(8,128)(2,1)S(1)}, u32[]{:S(2)}, u32[]{:S(2)}) collective-permute-start(bf16[40,2048]{1,0:T(8,128)(2,1)S(1)} %get-tuple-element.124), channel_id=1, source_target_pairs={{0,4},{2,6},{4,0},{6,2},{1,5},{3,7},{5,1},{7,3},{8,12},{10,14},{12... | collective-permute-start | bytes 491528 | tf_op jit(solution)/shard_map/ppermute | solution.py:245
  43.8 10.2 %collective-permute-start.14 = (bf16[40,2048]{1,0:T(8,128)(2,1)S(1)}, bf16[40,2048]{1,0:T(8,128)(2,1)S(1)}, u32[]{:S(2)}, u32[]{:S(2)}) collective-permute-start(bf16[40,2048]{1,0:T(8,128)(2,1)S(1)} %get-tuple-element.125), channel_id=1, source_target_pairs={{0,6},{2,4},{4,2},{6,0},{1,7},{3,5},{5,3},{7,1},{8,14},{10,12},{12... | collective-permute-start | bytes 491528 | tf_op jit(solution)/shard_map/ppermute | solution.py:245
  46.8 11.7 %collective-permute-start.18 = (bf16[40,2048]{1,0:T(8,128)(2,1)S(1)}, bf16[40,2048]{1,0:T(8,128)(2,1)S(1)}, u32[]{:S(2)}, u32[]{:S(2)}) collective-permute-start(bf16[40,2048]{1,0:T(8,128)(2,1)S(1)} %get-tuple-element.136), channel_id=1, source_target_pairs={{0,2},{2,0},{4,6},{6,4},{1,3},{3,1},{5,7},{7,5},{8,10},{10,8},{12,... | collective-permute-start | bytes 491528 | tf_op jit(solution)/shard_map/ppermute | solution.py:245
  48.0 11.8 %collective-permute-start.19 = (bf16[40,2048]{1,0:T(8,128)(2,1)S(1)}, bf16[40,2048]{1,0:T(8,128)(2,1)S(1)}, u32[]{:S(2)}, u32[]{:S(2)}) collective-permute-start(bf16[40,2048]{1,0:T(8,128)(2,1)S(1)} %get-tuple-element.137), channel_id=1, source_target_pairs={{0,4},{2,6},{4,0},{6,2},{1,5},{3,7},{5,1},{7,3},{8,12},{10,14},{12... | collective-permute-start | bytes 491528 | tf_op jit(solution)/shard_map/ppermute | solution.py:245
  49.9 11.0 %collective-permute-start.20 = (bf16[40,2048]{1,0:T(8,128)(2,1)S(1)}, bf16[40,2048]{1,0:T(8,128)(2,1)S(1)}, u32[]{:S(2)}, u32[]{:S(2)}) collective-permute-start(bf16[40,2048]{1,0:T(8,128)(2,1)S(1)} %get-tuple-element.138), channel_id=1, source_target_pairs={{0,6},{2,4},{4,2},{6,0},{1,7},{3,5},{5,3},{7,1},{8,14},{10,12},{12... | collective-permute-start | bytes 491528 | tf_op jit(solution)/shard_map/ppermute | solution.py:245
  56.3 11.5 %collective-permute-start.21 = (bf16[40,2048]{1,0:T(8,128)(2,1)S(1)}, bf16[40,2048]{1,0:T(8,128)(2,1)S(1)}, u32[]{:S(2)}, u32[]{:S(2)}) collective-permute-start(bf16[40,2048]{1,0:T(8,128)(2,1)S(1)} %get-tuple-element.149), channel_id=1, source_target_pairs={{0,2},{2,0},{4,6},{6,4},{1,3},{3,1},{5,7},{7,5},{8,10},{10,8},{12,... | collective-permute-start | bytes 491528 | tf_op jit(solution)/shard_map/ppermute | solution.py:245
  57.6 10.2 %collective-permute-start.22 = (bf16[40,2048]{1,0:T(8,128)(2,1)S(1)}, bf16[40,2048]{1,0:T(8,128)(2,1)S(1)}, u32[]{:S(2)}, u32[]{:S(2)}) collective-permute-start(bf16[40,2048]{1,0:T(8,128)(2,1)S(1)} %get-tuple-element.150), channel_id=1, source_target_pairs={{0,4},{2,6},{4,0},{6,2},{1,5},{3,7},{5,1},{7,3},{8,12},{10,14},{12... | collective-permute-start | bytes 491528 | tf_op jit(solution)/shard_map/ppermute | solution.py:245
  58.5 9.3 %collective-permute-start.23 = (bf16[40,2048]{1,0:T(8,128)(2,1)S(1)}, bf16[40,2048]{1,0:T(8,128)(2,1)S(1)}, u32[]{:S(2)}, u32[]{:S(2)}) collective-permute-start(bf16[40,2048]{1,0:T(8,128)(2,1)S(1)} %get-tuple-element.151), channel_id=1, source_target_pairs={{0,6},{2,4},{4,2},{6,0},{1,7},{3,5},{5,3},{7,1},{8,14},{10,12},{12... | collective-permute-start | bytes 491528 | tf_op jit(solution)/shard_map/ppermute | solution.py:245
  65.6 7.2 %collective-permute-start.29 = (bf16[40,2048]{1,0:T(8,128)(2,1)S(1)}, bf16[40,2048]{1,0:T(8,128)(2,1)S(1)}, u32[]{:S(2)}, u32[]{:S(2)}) collective-permute-start(bf16[40,2048]{1,0:T(8,128)(2,1)S(1)} %get-tuple-element.168), channel_id=1, source_target_pairs={{0,2},{2,0},{4,6},{6,4},{1,3},{3,1},{5,7},{7,5},{8,10},{10,8},{12,... | collective-permute-start | bytes 491528 | tf_op jit(solution)/shard_map/ppermute | solution.py:245
  66.9 7.0 %collective-permute-start.30 = (bf16[40,2048]{1,0:T(8,128)(2,1)S(1)}, bf16[40,2048]{1,0:T(8,128)(2,1)S(1)}, u32[]{:S(2)}, u32[]{:S(2)}) collective-permute-start(bf16[40,2048]{1,0:T(8,128)(2,1)S(1)} %get-tuple-element.169), channel_id=1, source_target_pairs={{0,4},{2,6},{4,0},{6,2},{1,5},{3,7},{5,1},{7,3},{8,12},{10,14},{12... | collective-permute-start | bytes 491528 | tf_op jit(solution)/shard_map/ppermute | solution.py:245
  68.1 12.1 %collective-permute-start.27 = (bf16[64,2048]{1,0:T(8,128)(2,1)S(1)}, bf16[64,2048]{1,0:T(8,128)(2,1)S(1)}, u32[]{:S(2)}, u32[]{:S(2)}) collective-permute-start(bf16[64,2048]{1,0:T(8,128)(2,1)S(1)} %combine.3), channel_id=1, source_target_pairs={{0,8},{8,0},{16,24},{24,16},{1,9},{9,1},{17,25},{25,17},{2,10},{10... | collective-permute-start | bytes 786440 | tf_op jit(solution)/shard_map/ppermute | solution.py:245
  69.7 6.7 %collective-permute-start.31 = (bf16[40,2048]{1,0:T(8,128)(2,1)S(1)}, bf16[40,2048]{1,0:T(8,128)(2,1)S(1)}, u32[]{:S(2)}, u32[]{:S(2)}) collective-permute-start(bf16[40,2048]{1,0:T(8,128)(2,1)S(1)} %get-tuple-element.170), channel_id=1, source_target_pairs={{0,6},{2,4},{4,2},{6,0},{1,7},{3,5},{5,3},{7,1},{8,14},{10,12},{12... | collective-permute-start | bytes 491528 | tf_op jit(solution)/shard_map/ppermute | solution.py:245
  71.1 6.9 %collective-permute-start.24 = (bf16[40,2048]{1,0:T(8,128)(2,1)S(1)}, bf16[40,2048]{1,0:T(8,128)(2,1)S(1)}, u32[]{:S(2)}, u32[]{:S(2)}) collective-permute-start(bf16[40,2048]{1,0:T(8,128)(2,1)S(1)} %get-tuple-element.153), channel_id=1, source_target_pairs={{0,2},{2,0},{4,6},{6,4},{1,3},{3,1},{5,7},{7,5},{8,10},{10,8},{12,... | collective-permute-start | bytes 491528 | tf_op jit(solution)/shard_map/ppermute | solution.py:245
  73.9 6.2 %collective-permute-start.26 = (bf16[40,2048]{1,0:T(8,128)(2,1)S(1)}, bf16[40,2048]{1,0:T(8,128)(2,1)S(1)}, u32[]{:S(2)}, u32[]{:S(2)}) collective-permute-start(bf16[40,2048]{1,0:T(8,128)(2,1)S(1)} %get-tuple-element.155), channel_id=1, source_target_pairs={{0,6},{2,4},{4,2},{6,0},{1,7},{3,5},{5,3},{7,1},{8,14},{10,12},{12... | collective-permute-start | bytes 491528 | tf_op jit(solution)/shard_map/ppermute | solution.py:245
  76.7 7.2 %collective-permute-start.32 = (bf16[64,2048]{1,0:T(8,128)(2,1)S(1)}, bf16[64,2048]{1,0:T(8,128)(2,1)S(1)}, u32[]{:S(2)}, u32[]{:S(2)}) collective-permute-start(bf16[64,2048]{1,0:T(8,128)(2,1)S(1)} %combine.5), channel_id=1, source_target_pairs={{0,8},{8,0},{16,24},{24,16},{1,9},{9,1},{17,25},{25,17},{2,10},{10... | collective-permute-start | bytes 786440 | tf_op jit(solution)/shard_map/ppermute | solution.py:245
  80.4 7.3 %collective-permute-start.28 = (bf16[64,2048]{1,0:T(8,128)(2,1)S(1)}, bf16[64,2048]{1,0:T(8,128)(2,1)S(1)}, u32[]{:S(2)}, u32[]{:S(2)}) collective-permute-start(bf16[64,2048]{1,0:T(8,128)(2,1)S(1)} %combine.4), channel_id=1, source_target_pairs={{0,16},{8,24},{16,0},{24,8},{1,17},{9,25},{17,1},{25,9},{2,18},{10... | collective-permute-start | bytes 786440 | tf_op jit(solution)/shard_map/ppermute | solution.py:245
  (4 other events, 68.9 us)
